TPU v7x, 512 devices: a whole 4x8x8 slice. The times are simulated.
512 devices in a mesh: panel: 2 (over core), lon: 16 (over y_lo, x), lat: 16 (over y_hi, z).
Axes of the slice: x: 4, y: 8 (y_hi: 2, y_lo: 4; y = y_hi * 4 + y_lo), z: 8, core: 2. Of those that a mesh axis runs over, the one named last changes fastest.
Arguments:
- motion_and_stress: float32 [4, 2, 32, 256, 2048], P(None, 'panel', None, 'lat', 'lon'), may hold values from -6 to 6
- warmth: float32 [2, 32, 256, 2048], P('panel', None, 'lat', 'lon'), may hold values from 0 to 1
- substance_label: int32 [2, 32, 256, 2048], P('panel', None, 'lat', 'lon'), may hold values from 0 to 7
- substance_stiffness_exponent: float32 [8], replicated, may hold values from -2.3 to 2.3
- receiver_indices: int32 [2, 16, 16, 512], P('panel', 'lat', 'lon'), may hold values from 0 to 2047, as said below
- donor_indices: int32 [2, 16, 16, 4, 512], P('panel', 'lat', 'lon'), may hold values from 0 to 2047
- blend_factors: float32 [2, 16, 16, 4, 512], P('panel', 'lat', 'lon'), may hold values from 0.1 to 0.4
Outputs:
- flow_out: float32 [4, 2, 32, 256, 2048], P(None, 'panel', None, 'lat', 'lon')
- temperature_out: float32 [2, 32, 256, 2048], P('panel', None, 'lat', 'lon')
Inputs may be any that keep to these rules, and one draw needn't show every extreme that they name: `receiver_indices`: the 512 targets of one tile are distinct cells of that tile.
All inputs are finite; a program needn't handle non-finite values.
Results may differ from a plain program's by a relative error of at most 0.00011.
Values sent between devices are 32-bit elements; how exact they have to be, the bound alone decides.
No kernel may reach another device: no remote copies, remote signals or barrier semaphores. Data moves between devices by JAX's collectives and lax.ppermute only.
A program may use at most 128 MiB of HBM per device.

v0:
```python
import jax
import jax.numpy as jnp
from jax import lax
from jax.sharding import PartitionSpec as P

SWEEPS = 2


OMEGA = 0.6
BETA = 0.5
KAPPA = 1.0
TIME_STEP = 0.05
LIFT_FACTOR = 2.0
DIFFUSIVITY = 2.3


def padded_2(array, sides, width):
    for axis, dim in sides:
        count, length = (lax.axis_size(axis), array.shape[dim])
        up = [(i, (i + 1) % count) for i in range(count - 1)]
        down = [(j, i) for i, j in up]
        last = lax.slice_in_dim(array, length - width, length, axis=dim)
        first = lax.slice_in_dim(array, 0, width, axis=dim)
        before = lax.ppermute(last, axis, up)
        after = lax.ppermute(first, axis, down)
        array = jnp.concatenate([before, array, after], axis=dim)
    return array


def partner(array, axis, stride):
    return lax.ppermute(array, axis, [(i, i ^ 1 << stride) for i in range(lax.axis_size(axis))])


def neighbour(padded, direction, offset):
    window = [slice(1, -1), slice(1, -1), slice(1, -1)]
    extent = padded.shape[padded.ndim - 3 + direction]
    window[direction] = slice(1 + offset, extent - 1 + offset)
    leading = tuple((slice(None) for _ in range(padded.ndim - 3)))
    return padded[leading + tuple(window)]


def stiffness_array(substance_label, warmth, reference_chart):
    logarithm_value = jnp.zeros(substance_label.shape, jnp.float32)
    for entry in range(reference_chart.shape[0]):
        logarithm_value = logarithm_value + jnp.where(
            substance_label == entry, reference_chart[entry], 0.0
        )
    return jnp.exp(logarithm_value + DIFFUSIVITY * (0.5 - warmth))


def relax_flow(padded_flow, padded_eta, lifting_push):
    centre_eta = neighbour(padded_eta, 0, 0)
    centre = neighbour(padded_flow, 0, 0)
    diagonal = jnp.zeros_like(centre_eta)
    face_flux = jnp.zeros_like(centre[:3])
    for direction in range(3):
        for offset in (-1, 1):
            face_eta = 0.5 * (centre_eta + neighbour(padded_eta, direction, offset))
            diagonal = diagonal + face_eta
            face_flux = face_flux + face_eta * (
                neighbour(padded_flow[:3], direction, offset) - centre[:3]
            )
    pressure_grad = jnp.stack(
        [
            0.5
            * (neighbour(padded_flow[3], component, 1) - neighbour(padded_flow[3], component, -1))
            for component in range(3)
        ]
    )
    divergence = jnp.zeros_like(centre_eta)
    for component in range(3):
        divergence = divergence + 0.5 * (
            neighbour(padded_flow[component], component, 1)
            - neighbour(padded_flow[component], component, -1)
        )
    zero_part = jnp.zeros_like(lifting_push)
    push = jnp.stack([lifting_push, zero_part, zero_part])
    velocity = centre[:3] + OMEGA * (push + face_flux - pressure_grad) / diagonal
    pressure = centre[3] - BETA * centre_eta * divergence
    return jnp.concatenate([velocity, pressure[None]], 0)


def carry_warmth(padded_temp, velocity):
    centre = neighbour(padded_temp, 0, 0)
    change = jnp.zeros_like(centre)
    for direction in range(3):
        upper = neighbour(padded_temp, direction, 1)
        lower = neighbour(padded_temp, direction, -1)
        speed = velocity[direction]
        change = (
            change
            - jnp.maximum(speed, 0.0) * (centre - lower)
            - jnp.minimum(speed, 0.0) * (upper - centre)
            + KAPPA * (upper + lower - 2.0 * centre)
        )
    return centre + TIME_STEP * change


def blend_between(tile_flat, donor_sequence, blend_factor_sequence):
    total = blend_factor_sequence[0] * jnp.take(tile_flat, donor_sequence[0], axis=2)
    for entry in range(1, 4):
        total = total + blend_factor_sequence[entry] * jnp.take(
            tile_flat, donor_sequence[entry], axis=2
        )
    return total


def place_numbers(fields, receiver_sequence, incoming):
    lat_extent = fields.shape[-2]
    lon_extent = fields.shape[-1]
    grid_points = lat_extent * lon_extent
    intersection = receiver_sequence.shape[0]
    table = (
        receiver_sequence[:, None] == jnp.arange(grid_points, dtype=jnp.int32)[None, :]
    ).astype(jnp.float32)
    value_rows = incoming.reshape(-1, intersection)
    placed = jnp.dot(
        value_rows, table, precision=lax.Precision.HIGHEST, preferred_element_type=jnp.float32
    )
    placed = placed.reshape(fields.shape)
    struck = jnp.sum(table, axis=0).reshape(lat_extent, lon_extent) > 0.5
    return jnp.where(struck, placed, fields)


def pad_shell(field):
    return jnp.pad(field, [(0, 0)] * (field.ndim - 3) + [(1, 1), (0, 0), (0, 0)])


def shards(
    motion_and_stress,
    warmth,
    substance_label,
    substance_stiffness_exponent,
    receiver_indices,
    donor_indices,
    blend_factors,
):
    local_stiffness = stiffness_array(substance_label, warmth, substance_stiffness_exponent)
    margin_breadth = 1
    rim_eta, rim_temp = (
        padded_2(local_stiffness, (("lon", 3), ("lat", 2)), margin_breadth),
        padded_2(warmth, (("lon", 3), ("lat", 2)), margin_breadth),
    )
    padded_eta = pad_shell(rim_eta)
    lifting_push = LIFT_FACTOR * (warmth - 0.5)
    relaxed_motion = motion_and_stress
    for sweep_index in range(SWEEPS):
        rimmed = padded_2(relaxed_motion, (("lon", 4), ("lat", 3)), 1)
        relaxed_motion = relax_flow(pad_shell(rimmed), padded_eta, lifting_push)
    padded_temp = pad_shell(rim_temp)
    warmed_result = carry_warmth(padded_temp, relaxed_motion[:3])
    layer_count = relaxed_motion.shape[2]
    grid_points = relaxed_motion.shape[3] * relaxed_motion.shape[4]
    intersection = receiver_indices.shape[-1]
    fields = jnp.concatenate([relaxed_motion[:, 0], warmed_result], 0)
    fields_flat = fields.reshape(5, layer_count, grid_points)
    donor_sequence = donor_indices.reshape(4, intersection)
    blend_factor_sequence = blend_factors.reshape(4, intersection)
    numbers = blend_between(fields_flat, donor_sequence, blend_factor_sequence)
    bit_count = lax.axis_size("lon").bit_length() - 1
    for bit_index in range(bit_count):
        numbers = partner(numbers, "lon", bit_index)
    numbers = partner(numbers, "panel", 0)
    receiver_sequence = receiver_indices.reshape(intersection)
    finished = place_numbers(fields, receiver_sequence, numbers)
    return (finished[:4][:, None], finished[4:])


def solution(mesh):
    in_specs = (
        P(None, "panel", None, "lat", "lon"),
        P("panel", None, "lat", "lon"),
        P("panel", None, "lat", "lon"),
        P(),
        P("panel", "lat", "lon", None),
        P("panel", "lat", "lon", None, None),
        P("panel", "lat", "lon", None, None),
    )
    out_specs = (P(None, "panel", None, "lat", "lon"), P("panel", None, "lat", "lon"))
    return jax.shard_map(shards, mesh=mesh, in_specs=in_specs, out_specs=out_specs, check_vma=False)
```

profile of v0, /device:TPU:57, one launch (start us, length us, event | category | flops | bytes accessed | tf_op | source)
XLA Modules:
  0.0 224.2 jit_solution(6875789123503183761)
XLA Ops:
  3.1 3.1 %collective-permute-start.4 = (f32[4,1,32,16,1]{2,3,4,1,0:T(8,128)S(1)}, f32[4,1,32,16,1]{2,3,4,1,0:T(8,128)S(1)}, u32[]{:S(2)}, u32[]{:S(2)}) collective-permute-start(f32[4,1,32,16,1]{2,3,4,1,0:T(8,128)S(1)} %copy.193), channel_id=1, source_target_pairs={{0,16},{16,32},{32,48},{48,64},{64,80},{80,96},{96,112},{112,128},... | collective-permute-start | bytes 24584 | tf_op jit(solution)/shard_map/ppermute | solution.py:24
  6.8 4.3 %collective-permute-start.5 = (f32[4,1,32,16,1]{2,3,4,1,0:T(8,128)S(1)}, f32[4,1,32,16,1]{2,3,4,1,0:T(8,128)S(1)}, u32[]{:S(2)}, u32[]{:S(2)}) collective-permute-start(f32[4,1,32,16,1]{2,3,4,1,0:T(8,128)S(1)} %copy.194), channel_id=1, source_target_pairs={{16,0},{32,16},{48,32},{64,48},{80,64},{96,80},{112,96},{128,112},... | collective-permute-start | bytes 24584 | tf_op jit(solution)/shard_map/ppermute | solution.py:25
  16.9 4.0 %collective-permute-start.6 = (f32[4,1,32,1,130]{4,2,3,1,0:T(8,128)S(1)}, f32[4,1,32,1,130]{4,2,3,1,0:T(8,128)S(1)}, u32[]{:S(2)}, u32[]{:S(2)}) collective-permute-start(f32[4,1,32,1,130]{4,2,3,1,0:T(8,128)S(1)} %get-tuple-element.15), channel_id=1, source_target_pairs={{0,1},{1,2},{2,3},{3,4},{4,5},{5,6},{6,7},{7,8},{8,9},{9,10},{10,1... | collective-permute-start | bytes 199688 | tf_op jit(solution)/shard_map/ppermute | solution.py:24
  20.9 10.8 %collective-permute-start.7 = (f32[4,1,32,1,130]{4,2,3,1,0:T(8,128)S(1)}, f32[4,1,32,1,130]{4,2,3,1,0:T(8,128)S(1)}, u32[]{:S(2)}, u32[]{:S(2)}) collective-permute-start(f32[4,1,32,1,130]{4,2,3,1,0:T(8,128)S(1)} %get-tuple-element.16), channel_id=1, source_target_pairs={{1,0},{2,1},{3,2},{4,3},{5,4},{6,5},{7,6},{8,7},{9,8},{10,9},{11,1... | collective-permute-start | bytes 199688 | tf_op jit(solution)/shard_map/ppermute | solution.py:25
  35.9 5.5 %fusion.66 = (f32[1,32,16,128]{3,1,2,0:T(8,128)S(1)}, f32[1,32,16,128]{3,1,2,0:T(8,128)S(1)}, f32[1,1,32,16,128]{4,2,3,1,0:T(8,128)S(1)}, f32[1,32,16,128]{3,1,2,0:T(8,128)S(1)}) fusion(f32[1,34,18,130]{3,1,2,0:T(8,128)S(1)} %get-tuple-element.24, f32[1,34,18,130]{3,1,2,0:T(8,128)S(1)} %get-tuple-element.23, f32[1,34,18,130]{3,1,2,0:T(8,128)S(1)} %get-tuple-element.21, ...), kind=kLoop, calls=%fused_computation.149 | loop fusion | flops 2424832 | bytes 3407904 | tf_op jit(solution)/shard_map/sub | solution.py:79
  43.5 5.5 %collective-permute-start.1 = (f32[1,32,16,1]{3,1,2,0:T(8,128)S(1)}, f32[1,32,16,1]{3,1,2,0:T(8,128)S(1)}, u32[]{:S(2)}, u32[]{:S(2)}) collective-permute-start(f32[1,32,16,1]{3,1,2,0:T(8,128)S(1)} %get-tuple-element.47), channel_id=1, source_target_pairs={{16,0},{32,16},{48,32},{64,48},{80,64},{96,80},{112,96},{128,112},... | collective-permute-start | bytes 6152 | tf_op jit(solution)/shard_map/ppermute | solution.py:25
  54.3 11.2 %collective-permute-start.3 = (f32[1,32,1,130]{3,1,2,0:T(8,128)S(1)}, f32[1,32,1,130]{3,1,2,0:T(8,128)S(1)}, u32[]{:S(2)}, u32[]{:S(2)}) collective-permute-start(f32[1,32,1,130]{3,1,2,0:T(8,128)S(1)} %get-tuple-element.37), channel_id=1, source_target_pairs={{1,0},{2,1},{3,2},{4,3},{5,4},{6,5},{7,6},{8,7},{9,8},{10,9},{11,1... | collective-permute-start | bytes 49928 | tf_op jit(solution)/shard_map/ppermute | solution.py:25
  68.2 6.2 %collective-permute-start.13 = (f32[1,32,16,1]{3,1,2,0:T(8,128)}, f32[1,32,16,1]{3,1,2,0:T(8,128)}, u32[]{:S(2)}, u32[]{:S(2)}) collective-permute-start(f32[1,32,16,1]{3,1,2,0:T(8,128)} %get-tuple-element.51), channel_id=1, source_target_pairs={{16,0},{32,16},{48,32},{64,48},{80,64},{96,80},{112,96},{128,112},... | collective-permute-start | bytes 6152 | tf_op jit(solution)/shard_map/ppermute | solution.py:25
  81.0 5.5 %collective-permute-start.9 = (f32[4,1,32,16,1]{2,3,4,1,0:T(8,128)S(1)}, f32[4,1,32,16,1]{2,3,4,1,0:T(8,128)S(1)}, u32[]{:S(2)}, u32[]{:S(2)}) collective-permute-start(f32[4,1,32,16,1]{2,3,4,1,0:T(8,128)S(1)} %copy.160), channel_id=1, source_target_pairs={{16,0},{32,16},{48,32},{64,48},{80,64},{96,80},{112,96},{128,112},... | collective-permute-start | bytes 24584 | tf_op jit(solution)/shard_map/ppermute | solution.py:25
  89.9 9.4 %collective-permute-start.15 = (f32[1,32,1,130]{3,1,2,0:T(8,128)}, f32[1,32,1,130]{3,1,2,0:T(8,128)S(1)}, u32[]{:S(2)}, u32[]{:S(2)}) collective-permute-start(f32[1,32,1,130]{3,1,2,0:T(8,128)} %get-tuple-element.33), channel_id=1, source_target_pairs={{1,0},{2,1},{3,2},{4,3},{5,4},{6,5},{7,6},{8,7},{9,8},{10,9},{11,1... | collective-permute-start | bytes 49928 | tf_op jit(solution)/shard_map/ppermute | solution.py:25
  103.1 9.6 %collective-permute-start.11 = (f32[4,1,32,1,130]{4,2,3,1,0:T(8,128)S(1)}, f32[4,1,32,1,130]{4,2,3,1,0:T(8,128)S(1)}, u32[]{:S(2)}, u32[]{:S(2)}) collective-permute-start(f32[4,1,32,1,130]{4,2,3,1,0:T(8,128)S(1)} %get-tuple-element.14), channel_id=1, source_target_pairs={{1,0},{2,1},{3,2},{4,3},{5,4},{6,5},{7,6},{8,7},{9,8},{10,9},{11,1... | collective-permute-start | bytes 199688 | tf_op jit(solution)/shard_map/ppermute | solution.py:25
  119.6 2.9 %fusion.16 = f32[3,1,32,16,128]{4,2,3,1,0:T(8,128)} fusion(f32[3,1,32,16,128]{4,2,3,1,0:T(8,128)S(1)} %fusion.12, f32[1,1,32,16,128]{4,2,3,1,0:T(8,128)S(1)} %copy-done.21, f32[4,1,32,16,1]{4,2,3,1,0:T(8,128)S(1)} %copy.162, f32[1,1,32,16,128]{4,2,3,1,0:T(8,128)S(1)} %bitcast.154, f32[4,1,32,16,1]{4,2,3,1,0:T(8,128)S(1)} %copy.161, ...), kind=kLoop, calls=%fused_computation.40 | loop fusion | flops 7077888 | bytes 6440960 | tf_op jit(solution)/shard_map/add | solution.py:78
  122.5 4.6 %copy.191 = f32[3,1,32,16,128]{2,0,4,3,1:T(4,128)} copy(f32[3,1,32,16,128]{4,2,3,1,0:T(8,128)} %fusion.16) | data formatting | bytes 1572864 | tf_op jit(solution)/shard_map/concatenate | solution.py:80
  134.0 6.9 %pad_maximum_fusion = f32[5,32,2048]{1,0,2:T(8,128)} fusion(f32[1,32,2048]{1,0,2:T(1,128)S(1)} %copy.183, f32[1,32,2048]{1,0,2:T(1,128)S(1)} %copy.182, f32[3,32,2048]{1,0,2:T(4,128)} %bitcast.150), kind=kLoop, calls=%fused_computation.4 | loop fusion | flops 655360 | bytes 2621440 | tf_op jit(solution)/shard_map/concatenate | solution.py:155
  140.9 4.4 %gather_fusion = f32[512,5,32]{2,1,0:T(8,128)S(1)} fusion(f32[5,32,2048]{1,0,2:T(8,128)} %pad_maximum_fusion, s32[1024]{0:T(1024)S(1)} %pad_clamp_fusion.3), kind=kCustom, calls=%fused_computation.clone | custom fusion | bytes 657408 | tf_op jit(solution)/shard_map/jit(_take)/gather | solution.py:100
  145.7 4.4 %gather_fusion.1 = f32[512,5,32]{2,1,0:T(8,128)S(1)} fusion(f32[5,32,2048]{1,0,2:T(8,128)} %pad_maximum_fusion, s32[1024]{0:T(1024)S(1)} %pad_clamp_fusion.2), kind=kCustom, calls=%fused_computation.1.clone | custom fusion | bytes 657408 | tf_op jit(solution)/shard_map/jit(_take)/gather | solution.py:102
  151.4 4.4 %gather_fusion.2 = f32[512,5,32]{2,1,0:T(8,128)S(1)} fusion(f32[5,32,2048]{1,0,2:T(8,128)} %pad_maximum_fusion, s32[1024]{0:T(1024)S(1)} %pad_clamp_fusion.1), kind=kCustom, calls=%fused_computation.2.clone | custom fusion | bytes 657408 | tf_op jit(solution)/shard_map/jit(_take)/gather | solution.py:102
  156.9 4.4 %gather_fusion.3 = f32[512,5,32]{2,1,0:T(8,128)S(1)} fusion(f32[5,32,2048]{1,0,2:T(8,128)} %pad_maximum_fusion, s32[1024]{0:T(1024)S(1)} %pad_clamp_fusion), kind=kCustom, calls=%fused_computation.3.clone | custom fusion | bytes 657408 | tf_op jit(solution)/shard_map/jit(_take)/gather | solution.py:102
  165.9 5.9 %collective-permute-done.16 = f32[5,32,512]{2,1,0:T(8,128)S(1)} collective-permute-done((f32[5,32,512]{2,1,0:T(8,128)S(1)}, f32[5,32,512]{2,1,0:T(8,128)S(1)}, u32[]{:S(2)}, u32[]{:S(2)}) %collective-permute-start.16) | collective-permute-done | bytes 327712 | tf_op jit(solution)/shard_map/ppermute | solution.py:31
  173.7 7.4 %collective-permute-done.17 = f32[5,32,512]{2,1,0:T(8,128)S(1)} collective-permute-done((f32[5,32,512]{2,1,0:T(8,128)S(1)}, f32[5,32,512]{2,1,0:T(8,128)S(1)}, u32[]{:S(2)}, u32[]{:S(2)}) %collective-permute-start.17) | collective-permute-done | bytes 327712 | tf_op jit(solution)/shard_map/ppermute | solution.py:31
  181.1 2.9 %collective-permute-start.18 = (f32[5,32,512]{2,1,0:T(8,128)S(1)}, f32[5,32,512]{2,1,0:T(8,128)S(1)}, u32[]{:S(2)}, u32[]{:S(2)}) collective-permute-start(f32[5,32,512]{2,1,0:T(8,128)S(1)} %collective-permute-done.17), channel_id=1, source_target_pairs={{0,64},{16,80},{32,96},{48,112},{64,0},{80,16},{96,32},{112,48},{1... | collective-permute-start | bytes 983048 | tf_op jit(solution)/shard_map/ppermute | solution.py:31
  184.0 5.2 %collective-permute-done.18 = f32[5,32,512]{2,1,0:T(8,128)S(1)} collective-permute-done((f32[5,32,512]{2,1,0:T(8,128)S(1)}, f32[5,32,512]{2,1,0:T(8,128)S(1)}, u32[]{:S(2)}, u32[]{:S(2)}) %collective-permute-start.18) | collective-permute-done | bytes 327712 | tf_op jit(solution)/shard_map/ppermute | solution.py:31
  192.4 9.2 %collective-permute-done.19 = f32[5,32,512]{2,1,0:T(8,128)S(1)} collective-permute-done((f32[5,32,512]{2,1,0:T(8,128)S(1)}, f32[5,32,512]{2,1,0:T(8,128)S(1)}, u32[]{:S(2)}, u32[]{:S(2)}) %collective-permute-start.19) | collective-permute-done | bytes 327712 | tf_op jit(solution)/shard_map/ppermute | solution.py:31
  201.5 16.6 %collective-permute-start.20 = (f32[5,32,512]{2,1,0:T(8,128)S(1)}, f32[5,32,512]{2,1,0:T(8,128)S(1)}, u32[]{:S(2)}, u32[]{:S(2)}) collective-permute-start(f32[5,32,512]{2,1,0:T(8,128)S(1)} %collective-permute-done.19), channel_id=1, source_target_pairs={{0,256},{256,0},{1,257},{257,1},{2,258},{258,2},{3,259},{259,3},{4... | collective-permute-start | bytes 983048 | tf_op jit(solution)/shard_map/ppermute | solution.py:31
  (169 shorter events, 68.5 us)
Async XLA Ops:
  3.1 10.7 %collective-permute-start.4 = (f32[4,1,32,16,1]{2,3,4,1,0:T(8,128)S(1)}, f32[4,1,32,16,1]{2,3,4,1,0:T(8,128)S(1)}, u32[]{:S(2)}, u32[]{:S(2)}) collective-permute-start(f32[4,1,32,16,1]{2,3,4,1,0:T(8,128)S(1)} %copy.193), channel_id=1, source_target_pairs={{0,16},{16,32},{32,48},{48,64},{64,80},{80,96},{96,112},{112,128},... | collective-permute-start | bytes 24584 | tf_op jit(solution)/shard_map/ppermute | solution.py:24
  6.8 7.6 %collective-permute-start.5 = (f32[4,1,32,16,1]{2,3,4,1,0:T(8,128)S(1)}, f32[4,1,32,16,1]{2,3,4,1,0:T(8,128)S(1)}, u32[]{:S(2)}, u32[]{:S(2)}) collective-permute-start(f32[4,1,32,16,1]{2,3,4,1,0:T(8,128)S(1)} %copy.194), channel_id=1, source_target_pairs={{16,0},{32,16},{48,32},{64,48},{80,64},{96,80},{112,96},{128,112},... | collective-permute-start | bytes 24584 | tf_op jit(solution)/shard_map/ppermute | solution.py:25
  16.9 15.4 %collective-permute-start.6 = (f32[4,1,32,1,130]{4,2,3,1,0:T(8,128)S(1)}, f32[4,1,32,1,130]{4,2,3,1,0:T(8,128)S(1)}, u32[]{:S(2)}, u32[]{:S(2)}) collective-permute-start(f32[4,1,32,1,130]{4,2,3,1,0:T(8,128)S(1)} %get-tuple-element.15), channel_id=1, source_target_pairs={{0,1},{1,2},{2,3},{3,4},{4,5},{5,6},{6,7},{7,8},{8,9},{9,10},{10,1... | collective-permute-start | bytes 199688 | tf_op jit(solution)/shard_map/ppermute | solution.py:24
  20.9 12.8 %collective-permute-start.7 = (f32[4,1,32,1,130]{4,2,3,1,0:T(8,128)S(1)}, f32[4,1,32,1,130]{4,2,3,1,0:T(8,128)S(1)}, u32[]{:S(2)}, u32[]{:S(2)}) collective-permute-start(f32[4,1,32,1,130]{4,2,3,1,0:T(8,128)S(1)} %get-tuple-element.16), channel_id=1, source_target_pairs={{1,0},{2,1},{3,2},{4,3},{5,4},{6,5},{7,6},{8,7},{9,8},{10,9},{11,1... | collective-permute-start | bytes 199688 | tf_op jit(solution)/shard_map/ppermute | solution.py:25
  41.4 36.4 %copy-start.3 = (f32[1,32,16,128]{3,1,2,0:T(8,128)}, f32[1,32,16,128]{3,1,2,0:T(8,128)S(1)}, u32[]{:S(2)}) copy-start(f32[1,32,16,128]{3,1,2,0:T(8,128)S(1)} %get-tuple-element.11) | copy-start | bytes 786436
  41.5 9.7 %collective-permute-start = (f32[1,32,16,1]{3,1,2,0:T(8,128)S(1)}, f32[1,32,16,1]{3,1,2,0:T(8,128)S(1)}, u32[]{:S(2)}, u32[]{:S(2)}) collective-permute-start(f32[1,32,16,1]{3,1,2,0:T(8,128)S(1)} %get-tuple-element.46), channel_id=1, source_target_pairs={{0,16},{16,32},{32,48},{48,64},{64,80},{80,96},{96,112},{112,128},... | collective-permute-start | bytes 6152 | tf_op jit(solution)/shard_map/ppermute | solution.py:24
  43.5 8.8 %collective-permute-start.1 = (f32[1,32,16,1]{3,1,2,0:T(8,128)S(1)}, f32[1,32,16,1]{3,1,2,0:T(8,128)S(1)}, u32[]{:S(2)}, u32[]{:S(2)}) collective-permute-start(f32[1,32,16,1]{3,1,2,0:T(8,128)S(1)} %get-tuple-element.47), channel_id=1, source_target_pairs={{16,0},{32,16},{48,32},{64,48},{80,64},{96,80},{112,96},{128,112},... | collective-permute-start | bytes 6152 | tf_op jit(solution)/shard_map/ppermute | solution.py:25
  52.3 22.1 %collective-permute-start.2 = (f32[1,32,1,130]{3,1,2,0:T(8,128)S(1)}, f32[1,32,1,130]{3,1,2,0:T(8,128)S(1)}, u32[]{:S(2)}, u32[]{:S(2)}) collective-permute-start(f32[1,32,1,130]{3,1,2,0:T(8,128)S(1)} %get-tuple-element.36), channel_id=1, source_target_pairs={{0,1},{1,2},{2,3},{3,4},{4,5},{5,6},{6,7},{7,8},{8,9},{9,10},{10,1... | collective-permute-start | bytes 49928 | tf_op jit(solution)/shard_map/ppermute | solution.py:24
  54.3 20.2 %collective-permute-start.3 = (f32[1,32,1,130]{3,1,2,0:T(8,128)S(1)}, f32[1,32,1,130]{3,1,2,0:T(8,128)S(1)}, u32[]{:S(2)}, u32[]{:S(2)}) collective-permute-start(f32[1,32,1,130]{3,1,2,0:T(8,128)S(1)} %get-tuple-element.37), channel_id=1, source_target_pairs={{1,0},{2,1},{3,2},{4,3},{5,4},{6,5},{7,6},{8,7},{9,8},{10,9},{11,1... | collective-permute-start | bytes 49928 | tf_op jit(solution)/shard_map/ppermute | solution.py:25
  66.3 20.2 %collective-permute-start.12 = (f32[1,32,16,1]{3,1,2,0:T(8,128)}, f32[1,32,16,1]{3,1,2,0:T(8,128)}, u32[]{:S(2)}, u32[]{:S(2)}) collective-permute-start(f32[1,32,16,1]{3,1,2,0:T(8,128)} %get-tuple-element.50), channel_id=1, source_target_pairs={{0,16},{16,32},{32,48},{48,64},{64,80},{80,96},{96,112},{112,128},... | collective-permute-start | bytes 6152 | tf_op jit(solution)/shard_map/ppermute | solution.py:24
  68.2 18.3 %collective-permute-start.13 = (f32[1,32,16,1]{3,1,2,0:T(8,128)}, f32[1,32,16,1]{3,1,2,0:T(8,128)}, u32[]{:S(2)}, u32[]{:S(2)}) collective-permute-start(f32[1,32,16,1]{3,1,2,0:T(8,128)} %get-tuple-element.51), channel_id=1, source_target_pairs={{16,0},{32,16},{48,32},{64,48},{80,64},{96,80},{112,96},{128,112},... | collective-permute-start | bytes 6152 | tf_op jit(solution)/shard_map/ppermute | solution.py:25
  78.7 20.7 %collective-permute-start.8 = (f32[4,1,32,16,1]{2,3,4,1,0:T(8,128)S(1)}, f32[4,1,32,16,1]{2,3,4,1,0:T(8,128)S(1)}, u32[]{:S(2)}, u32[]{:S(2)}) collective-permute-start(f32[4,1,32,16,1]{2,3,4,1,0:T(8,128)S(1)} %copy.159), channel_id=1, source_target_pairs={{0,16},{16,32},{32,48},{48,64},{64,80},{80,96},{96,112},{112,128},... | collective-permute-start | bytes 24584 | tf_op jit(solution)/shard_map/ppermute | solution.py:24
  81.0 18.8 %collective-permute-start.9 = (f32[4,1,32,16,1]{2,3,4,1,0:T(8,128)S(1)}, f32[4,1,32,16,1]{2,3,4,1,0:T(8,128)S(1)}, u32[]{:S(2)}, u32[]{:S(2)}) collective-permute-start(f32[4,1,32,16,1]{2,3,4,1,0:T(8,128)S(1)} %copy.160), channel_id=1, source_target_pairs={{16,0},{32,16},{48,32},{64,48},{80,64},{96,80},{112,96},{128,112},... | collective-permute-start | bytes 24584 | tf_op jit(solution)/shard_map/ppermute | solution.py:25
  88.0 24.7 %collective-permute-start.14 = (f32[1,32,1,130]{3,1,2,0:T(8,128)}, f32[1,32,1,130]{3,1,2,0:T(8,128)S(1)}, u32[]{:S(2)}, u32[]{:S(2)}) collective-permute-start(f32[1,32,1,130]{3,1,2,0:T(8,128)} %get-tuple-element.32), channel_id=1, source_target_pairs={{0,1},{1,2},{2,3},{3,4},{4,5},{5,6},{6,7},{7,8},{8,9},{9,10},{10,1... | collective-permute-start | bytes 49928 | tf_op jit(solution)/shard_map/ppermute | solution.py:24
  89.9 22.8 %collective-permute-start.15 = (f32[1,32,1,130]{3,1,2,0:T(8,128)}, f32[1,32,1,130]{3,1,2,0:T(8,128)S(1)}, u32[]{:S(2)}, u32[]{:S(2)}) collective-permute-start(f32[1,32,1,130]{3,1,2,0:T(8,128)} %get-tuple-element.33), channel_id=1, source_target_pairs={{1,0},{2,1},{3,2},{4,3},{5,4},{6,5},{7,6},{8,7},{9,8},{10,9},{11,1... | collective-permute-start | bytes 49928 | tf_op jit(solution)/shard_map/ppermute | solution.py:25
  101.2 13.8 %collective-permute-start.10 = (f32[4,1,32,1,130]{4,2,3,1,0:T(8,128)S(1)}, f32[4,1,32,1,130]{4,2,3,1,0:T(8,128)S(1)}, u32[]{:S(2)}, u32[]{:S(2)}) collective-permute-start(f32[4,1,32,1,130]{4,2,3,1,0:T(8,128)S(1)} %get-tuple-element.13), channel_id=1, source_target_pairs={{0,1},{1,2},{2,3},{3,4},{4,5},{5,6},{6,7},{7,8},{8,9},{9,10},{10,1... | collective-permute-start | bytes 199688 | tf_op jit(solution)/shard_map/ppermute | solution.py:24
  103.1 11.9 %collective-permute-start.11 = (f32[4,1,32,1,130]{4,2,3,1,0:T(8,128)S(1)}, f32[4,1,32,1,130]{4,2,3,1,0:T(8,128)S(1)}, u32[]{:S(2)}, u32[]{:S(2)}) collective-permute-start(f32[4,1,32,1,130]{4,2,3,1,0:T(8,128)S(1)} %get-tuple-element.14), channel_id=1, source_target_pairs={{1,0},{2,1},{3,2},{4,3},{5,4},{6,5},{7,6},{8,7},{9,8},{10,9},{11,1... | collective-permute-start | bytes 199688 | tf_op jit(solution)/shard_map/ppermute | solution.py:25
  156.9 61.2 %copy-start.23 = (f32[1,32,16,128]{3,1,2,0:T(8,128)S(1)}, f32[1,32,16,128]{3,1,2,0:T(8,128)}, u32[]{:S(2)}) copy-start(f32[1,32,16,128]{3,1,2,0:T(8,128)} %copy-done.22) | copy-start | bytes 786436
  162.6 56.6 %copy-start.26 = (f32[1,32,16,128]{3,1,2,0:T(8,128)S(1)}, f32[1,32,16,128]{3,1,2,0:T(8,128)}, u32[]{:S(2)}) copy-start(f32[1,32,16,128]{3,1,2,0:T(8,128)} %copy-done.25) | copy-start | bytes 786436
  164.0 7.8 %collective-permute-start.16 = (f32[5,32,512]{2,1,0:T(8,128)S(1)}, f32[5,32,512]{2,1,0:T(8,128)S(1)}, u32[]{:S(2)}, u32[]{:S(2)}) collective-permute-start(f32[5,32,512]{2,1,0:T(8,128)S(1)} %fusion.49), channel_id=1, source_target_pairs={{0,16},{16,0},{32,48},{48,32},{64,80},{80,64},{96,112},{112,96},{1... | collective-permute-start | bytes 983048 | tf_op jit(solution)/shard_map/ppermute | solution.py:31
  171.8 9.3 %collective-permute-start.17 = (f32[5,32,512]{2,1,0:T(8,128)S(1)}, f32[5,32,512]{2,1,0:T(8,128)S(1)}, u32[]{:S(2)}, u32[]{:S(2)}) collective-permute-start(f32[5,32,512]{2,1,0:T(8,128)S(1)} %collective-permute-done.16), channel_id=1, source_target_pairs={{0,32},{16,48},{32,0},{48,16},{64,96},{80,112},{96,64},{112,80},{1... | collective-permute-start | bytes 983048 | tf_op jit(solution)/shard_map/ppermute | solution.py:31
  181.1 8.1 %collective-permute-start.18 = (f32[5,32,512]{2,1,0:T(8,128)S(1)}, f32[5,32,512]{2,1,0:T(8,128)S(1)}, u32[]{:S(2)}, u32[]{:S(2)}) collective-permute-start(f32[5,32,512]{2,1,0:T(8,128)S(1)} %collective-permute-done.17), channel_id=1, source_target_pairs={{0,64},{16,80},{32,96},{48,112},{64,0},{80,16},{96,32},{112,48},{1... | collective-permute-start | bytes 983048 | tf_op jit(solution)/shard_map/ppermute | solution.py:31
  189.2 12.3 %collective-permute-start.19 = (f32[5,32,512]{2,1,0:T(8,128)S(1)}, f32[5,32,512]{2,1,0:T(8,128)S(1)}, u32[]{:S(2)}, u32[]{:S(2)}) collective-permute-start(f32[5,32,512]{2,1,0:T(8,128)S(1)} %collective-permute-done.18), channel_id=1, source_target_pairs={{0,128},{16,144},{32,160},{48,176},{64,192},{80,208},{96,224},{112... | collective-permute-start | bytes 983048 | tf_op jit(solution)/shard_map/ppermute | solution.py:31
  201.5 17.6 %collective-permute-start.20 = (f32[5,32,512]{2,1,0:T(8,128)S(1)}, f32[5,32,512]{2,1,0:T(8,128)S(1)}, u32[]{:S(2)}, u32[]{:S(2)}) collective-permute-start(f32[5,32,512]{2,1,0:T(8,128)S(1)} %collective-permute-done.19), channel_id=1, source_target_pairs={{0,256},{256,0},{1,257},{257,1},{2,258},{258,2},{3,259},{259,3},{4... | collective-permute-start | bytes 983048 | tf_op jit(solution)/shard_map/ppermute | solution.py:31
  (38 other events, 288.0 us)
where the time goes:
time: 225 us; the launch traced here: 224 us
  starting transfers between devices  107 us (48%)
  local copies, waits for them, and re-layouts  43.5 us (19%)
  other arithmetic  36.4 us (16%)
  waiting for transfers between devices  33.4 us (15%)
  matrix products  2.42 us (1%)
    ppermute x8, starting transfers between devices, padded_2(): after = lax.ppermute(first, axis, down)  62.4 us
    ppermute x5, waiting for transfers between devices, partner(): lax.ppermute(array, axis, [(i, i ^ 1 << stride) for i in range(lax.axis_s...  28.6 us
    ppermute x5, starting transfers between devices, partner(): lax.ppermute(array, axis, [(i, i ^ 1 << stride) for i in range(lax.axis_s...  25.9 us
    ppermute x8, starting transfers between devices, padded_2(): before = lax.ppermute(last, axis, up)  18.6 us
    gather x6, local copies, waits for them, and re-layouts, blend_between(): jnp.take(tile_flat, donor_sequence[entry], axis=2)  16.7 us
    sub x2, other arithmetic, relax_flow(): pressure = centre[3] - BETA * centre_eta * divergence  8 us
    concatenate x1, other arithmetic, shards(): fields = jnp.concatenate([relaxed_motion[:, 0], warmed_result], 0)  6.88 us
    unnamed x87, local copies, waits for them, and re-layouts  6.12 us
  transfers between devices with their start and end apart: 21, of which 9 were waited for; matrix products, arithmetic and copies ran while one was open for 7% of the time, Pallas kernels for 0%

commit v1 on v0

v1 whole, which is shorter than its diff:
```python
import jax
import jax.numpy as jnp
from jax import lax
from jax.experimental import pallas as pl
from jax.experimental.pallas import tpu as pltpu
from jax.sharding import PartitionSpec as P

OMEGA = 0.6
BETA = 0.5
TIME_STEP = 0.05
DIFFUSIVITY = 2.3

F32 = jnp.float32
BF16 = jnp.bfloat16
ANY = pl.BlockSpec(memory_space=pl.ANY)
VMEM = pl.BlockSpec(memory_space=pltpu.VMEM)
SMEM = pl.BlockSpec(memory_space=pltpu.SMEM)

LAT, DEP, LON = 16, 32, 128


def iota(dim, shape=(DEP, LON)):
    return lax.broadcasted_iota(jnp.int32, shape, dim)


def roll(x, shift, axis):
    return pltpu.roll(x, shift, axis)


def depth_pair(x):
    row = iota(0, x.shape)
    lower = jnp.where(row == 0, 0.0, roll(x, 1, 0))
    upper = jnp.where(row == x.shape[0] - 1, 0.0, roll(x, x.shape[0] - 1, 0))
    return lower, upper


def lon_pair(x, edge, r):
    lane = iota(1, x.shape)
    halo = roll(edge, 122 - 4 * r, 1)
    lower = jnp.where(lane == 0, halo, roll(x, 1, 1))
    upper = jnp.where(lane == LON - 1, halo, roll(x, LON - 1, 1))
    return lower, upper


def swap_middle(c):
    pos = iota(1, c.shape) & 3
    return jnp.where(pos == 1, roll(c, LON - 1, 1), roll(c, 1, 1))


def relax(centre, pairs, faces, scale, eta, warmth):
    out = []
    for c in range(3):
        total = 0.0
        for e in range(3):
            for s in range(2):
                total = total + faces[e][s] * pairs[c][e][s]
        total = total - (pairs[3][c][1] - pairs[3][c][0])
        if c == 0:
            total = total + 4.0 * (warmth - 0.5)
        out.append((1.0 - OMEGA) * centre[c] + total * scale)
    div = 0.0
    for c in range(3):
        div = div + (pairs[c][c][1] - pairs[c][c][0])
    out.append(centre[3] - (0.5 * BETA) * eta * div)
    return out


def edges_kernel(motion, warmth, label, chart, eta_out, cols_out, up_out, down_out, m, t, lab, sems):
    copies = []
    for r in range(LAT):
        copies.append(pltpu.make_async_copy(warmth.at[0, :, r, :], t.at[r], sems.at[0, r]))
        copies.append(pltpu.make_async_copy(label.at[0, :, r, :], lab.at[r], sems.at[1, r]))
    for r in range(LAT):
        copies.append(pltpu.make_async_copy(motion.at[:, 0, :, r, :], m.at[:, r], sems.at[2, r]))
    for c in copies:
        c.start()
    for c in copies:
        c.wait()

    def stiffness(r, _):
        kind = lab[r]
        exponent = jnp.full(kind.shape, chart[0], F32)
        for entry in range(1, 8):
            exponent = jnp.where(kind == entry, chart[entry], exponent)
        eta_out[r] = jnp.exp(exponent + DIFFUSIVITY * (0.5 - t[r]))
        return 0

    lax.fori_loop(0, LAT, stiffness, 0)

    group = iota(1) >> 2

    def pack(r, acc):
        fields = (m[0, r], m[1, r], m[2, r], m[3, r], eta_out[r], t[r])
        new = []
        for q in range(3):
            first = roll(fields[2 * q], 4 * r + 2, 1)
            second = roll(fields[2 * q + 1], 4 * r + 66, 1)
            new.append(jnp.where(group == r, first, jnp.where(group == r + 16, second, acc[q])))
        return tuple(new)

    zero = jnp.zeros((DEP, LON), F32)
    packed = lax.fori_loop(0, LAT, pack, (zero, zero, zero))
    for q in range(3):
        cols_out[q] = packed[q]
    for out, outer, inner in ((up_out, 14, 15), (down_out, 1, 0)):
        for f in range(4):
            out[f] = m[f, outer]
            out[5 + f] = m[f, inner]
        out[4] = eta_out[outer]
        out[9] = eta_out[inner]
        out[10] = t[inner]
        out[11] = zero


def corners_kernel(left, right, up, down, up_out, down_out, cu, cd, sems):
    lane = iota(1)
    pos = lane & 3
    group = (lane >> 2) & 15
    pairs = [jnp.where(pos < 2, left[q], right[q]) for q in range(3)]
    cu[...] = jnp.where(group == 15, pairs[0], jnp.where(group == 14, roll(pairs[1], 124, 1), roll(pairs[2], 120, 1)))
    cd[...] = jnp.where(group == 0, pairs[0], jnp.where(group == 1, roll(pairs[1], 4, 1), roll(pairs[2], 8, 1)))
    a = pltpu.make_async_copy(cu, up_out.at[11], sems.at[0])
    b = pltpu.make_async_copy(cd, down_out.at[11], sems.at[1])
    a.start()
    b.start()
    a.wait()
    b.wait()


def weights_kernel(donors, factors, hi, lo):
    def body(i, _):
        cell = iota(0, (32, 512)) + i * 32
        w = jnp.zeros((32, 512), F32)
        for j in range(4):
            w = w + jnp.where(cell == donors[j : j + 1, :], factors[j : j + 1, :], 0.0)
        top = w.astype(BF16)
        at = pl.ds(pl.multiple_of(i * 32, 32), 32)
        hi[at, :] = top
        lo[at, :] = (w - top.astype(F32)).astype(BF16)
        return 0

    lax.fori_loop(0, LAT * LON // 32, body, 0)


def table_kernel(receivers, table):
    def body(i, _):
        cell = iota(0, (32, 512)) + i * 32
        table[pl.ds(pl.multiple_of(i * 32, 32), 32), :] = jnp.where(cell == receivers[...], 1.0, 0.0).astype(BF16)
        return 0

    lax.fori_loop(0, LAT * LON // 32, body, 0)


def flow_kernel(motion, warmth, eta, cols, left, right, south, north, whi, wlo, fields_out, values_out, f, s1, faces, edge, lhs, sems):
    copies = []
    for r in range(LAT):
        copies.append(pltpu.make_async_copy(motion.at[:, 0, :, r, :], f.at[0:4, r + 2], sems.at[0, r]))
        copies.append(pltpu.make_async_copy(warmth.at[0, :, r, :], f.at[5, r + 2], sems.at[1, r]))
    copies.append(pltpu.make_async_copy(eta, f.at[4, 2:18], sems.at[2, 0]))
    copies.append(pltpu.make_async_copy(south.at[0:5], f.at[0:5, 0], sems.at[2, 1]))
    copies.append(pltpu.make_async_copy(south.at[5:11], f.at[:, 1], sems.at[2, 2]))
    copies.append(pltpu.make_async_copy(north.at[0:5], f.at[0:5, 19], sems.at[2, 3]))
    copies.append(pltpu.make_async_copy(north.at[5:11], f.at[:, 18], sems.at[2, 4]))
    corner_s, corner_n = edge.at[10], edge.at[11]
    copies.append(pltpu.make_async_copy(south.at[11], corner_s, sems.at[2, 5]))
    copies.append(pltpu.make_async_copy(north.at[11], corner_n, sems.at[2, 6]))
    for c in copies:
        c.start()
    for c in copies:
        c.wait()

    lane = iota(1)
    pos = lane & 3
    group = lane >> 2
    middle = pos == 1

    halo, own = [], []
    for k in range(6):
        q, h = k // 2, k % 2
        both = jnp.where(pos < 2, left[q], right[q])
        c = roll(both, 4 + 64 * h, 1)
        low = roll(corner_s[...], (128 - (64 * h + 60 - 4 * q)) % 128, 1)
        high = roll(corner_n[...], (68 - 64 * h - 4 * q) % 128, 1)
        c = jnp.where(group == 0, low, jnp.where(group == 17, high, c))
        halo.append(c)
        own.append(roll(cols[q], 4 + 64 * h, 1))
        edge[k] = swap_middle(c)

    def column_pairs(k):
        c, o = halo[k], own[k]
        lower = jnp.where(middle, roll(c, 1, 1), roll(o, 1, 1))
        upper = jnp.where(middle, roll(o, LON - 1, 1), roll(c, LON - 1, 1))
        return depth_pair(c), (roll(c, 4, 1), roll(c, LON - 4, 1)), (lower, upper)

    eta_pairs = column_pairs(4)
    col_faces = [[halo[4] + n for n in pair] for pair in eta_pairs]
    diagonal = 0.0
    for pair in col_faces:
        diagonal = diagonal + pair[0] + pair[1]
    inside = halo[4] > 0.0
    scale = OMEGA / jnp.where(inside, diagonal, 1.0)
    new = relax(halo[:4], [column_pairs(k) for k in range(4)], col_faces, scale, halo[4], halo[5])
    for k in range(4):
        edge[6 + k] = swap_middle(jnp.where(inside, new[k], 0.0))

    def first(i, _):
        r = i - 1
        eta_c = f[4, i + 1]
        eta_pairs = (depth_pair(eta_c), (f[4, i], f[4, i + 2]), lon_pair(eta_c, edge[4], r))
        both = [[eta_c + n for n in pair] for pair in eta_pairs]
        diagonal = both[0][0] + both[0][1] + both[1][0] + both[1][1] + both[2][0] + both[2][1]
        scale = OMEGA / diagonal
        faces[0, i] = both[0][0]
        faces[1, i] = both[0][1]
        faces[2, i] = both[2][0]
        faces[3, i] = both[2][1]
        faces[4, i] = scale
        centre = [f[k, i + 1] for k in range(4)]
        pairs = [(depth_pair(centre[k]), (f[k, i], f[k, i + 2]), lon_pair(centre[k], edge[k], r)) for k in range(4)]
        new = relax(centre, pairs, both, scale, eta_c, f[5, i + 1])
        for k in range(4):
            s1[k, i] = new[k]
        return 0

    lax.fori_loop(0, LAT + 2, first, 0)
    for i in (0, LAT + 1):
        here = f[4, i + 1] > 0.0
        for k in range(4):
            s1[k, i] = jnp.where(here, s1[k, i], 0.0)

    def second(r, _):
        i = r + 1
        eta_c = f[4, r + 2]
        both = [
            (faces[0, i], faces[1, i]),
            (eta_c + f[4, r + 1], eta_c + f[4, r + 3]),
            (faces[2, i], faces[3, i]),
        ]
        centre = [s1[k, i] for k in range(4)]
        pairs = [(depth_pair(centre[k]), (s1[k, i - 1], s1[k, i + 1]), lon_pair(centre[k], edge[6 + k], r)) for k in range(4)]
        t = f[5, r + 2]
        new = relax(centre, pairs, both, faces[4, i], eta_c, t)
        change = 0.0
        for e, (lower, upper) in enumerate((depth_pair(t), (f[5, r + 1], f[5, r + 3]), lon_pair(t, edge[5], r))):
            change = (
                change
                - jnp.maximum(new[e], 0.0) * (t - lower)
                - jnp.minimum(new[e], 0.0) * (upper - t)
                + (upper + lower - 2.0 * t)
            )
        new.append(t + TIME_STEP * change)
        at = pl.ds(pl.multiple_of(r * LON, LON), LON)
        for k in range(5):
            fields_out[k, r] = new[k]
            top = new[k].astype(BF16)
            lhs[k * DEP : (k + 1) * DEP, at] = top
            lhs[(5 + k) * DEP : (6 + k) * DEP, at] = (new[k] - top.astype(F32)).astype(BF16)
        return 0

    lax.fori_loop(0, LAT, second, 0)
    n = 5 * DEP
    wide = jnp.dot(lhs[...], whi[...], preferred_element_type=F32)
    values_out[...] = wide[:n] + wide[n:] + jnp.dot(lhs[:n], wlo[...], preferred_element_type=F32)


def place_kernel(fields, values, table, flow_out, warmth_out, lhs, out, sems):
    n = 5 * DEP
    v = values[...]
    top = v.astype(BF16)
    lhs[0:n] = top
    lhs[n : 2 * n] = (v - top.astype(F32)).astype(BF16)
    lhs[2 * n : 2 * n + 16] = jnp.ones((16, 512), BF16)
    copies = []
    for g in range(LAT // 2):
        rows = table[g * 256 : (g + 1) * 256, :]
        placed = lax.dot_general(lhs[...], rows, (((1,), (1,)), ((), ())), preferred_element_type=F32)
        struck = placed[2 * n : 2 * n + 1] > 0.5
        merged = placed[:n] + placed[n : 2 * n]
        for h in range(2):
            r = 2 * g + h
            at = slice(h * LON, (h + 1) * LON)
            for k in range(5):
                out[k, r] = jnp.where(struck[:, at], merged[k * DEP : (k + 1) * DEP, at], fields[k, r])
            copies.append(pltpu.make_async_copy(out.at[0:4, r], flow_out.at[:, 0, :, r, :], sems.at[0, r]))
            copies.append(pltpu.make_async_copy(out.at[4, r], warmth_out.at[0, :, r, :], sems.at[1, r]))
            copies[-2].start()
            copies[-1].start()
    for c in copies:
        c.wait()


def shape(*dims, dtype=F32):
    return jax.ShapeDtypeStruct(dims, dtype)


def call(kernel, outs, ins, scratch=(), out_specs=None, flops=0, size=0, aliases=None, limit=None):
    return pl.pallas_call(
        kernel,
        out_shape=outs,
        in_specs=ins,
        out_specs=out_specs or [VMEM] * len(outs),
        scratch_shapes=list(scratch),
        input_output_aliases=aliases or {},
        cost_estimate=pl.CostEstimate(flops=flops, bytes_accessed=size, transcendentals=0),
        compiler_params=pltpu.CompilerParams(vmem_limit_bytes=limit or (32 << 20)),
    )


def shards(motion, warmth, label, chart, receivers, donors, factors):
    lon, lat = lax.axis_size("lon"), lax.axis_size("lat")
    receivers = receivers.reshape(1, 512)
    donors = donors.reshape(4, 512)
    factors = factors.reshape(4, 512)

    slab = (LAT, DEP, LON)
    eta, cols, up, down = call(
        edges_kernel,
        [shape(*slab), shape(3, DEP, LON), shape(12, DEP, LON), shape(12, DEP, LON)],
        [ANY, ANY, ANY, SMEM],
        [pltpu.VMEM((4,) + slab, F32), pltpu.VMEM(slab, F32), pltpu.VMEM(slab, jnp.int32), pltpu.SemaphoreType.DMA((3, LAT))],
        size=2 << 20,
    )(motion, warmth, label, chart)

    ahead = lambda n: [(i, i + 1) for i in range(n - 1)]
    back = lambda n: [(i + 1, i) for i in range(n - 1)]
    left = lax.ppermute(cols, "lon", ahead(lon))
    right = lax.ppermute(cols, "lon", back(lon))
    up, down = call(
        corners_kernel,
        [shape(12, DEP, LON), shape(12, DEP, LON)],
        [VMEM, VMEM, ANY, ANY],
        [pltpu.VMEM((DEP, LON), F32), pltpu.VMEM((DEP, LON), F32), pltpu.SemaphoreType.DMA((2,))],
        out_specs=[ANY, ANY],
        aliases={2: 0, 3: 1},
        size=1 << 16,
    )(left, right, up, down)
    south = lax.ppermute(up, "lat", ahead(lat))
    north = lax.ppermute(down, "lat", back(lat))

    whi, wlo = call(
        weights_kernel,
        [shape(LAT * LON, 512, dtype=BF16), shape(LAT * LON, 512, dtype=BF16)],
        [VMEM, VMEM],
        size=4 << 20,
        flops=20 << 20,
    )(donors, factors)

    fields, values = call(
        flow_kernel,
        [shape(5, *slab), shape(5 * DEP, 512)],
        [ANY, ANY, ANY, VMEM, VMEM, VMEM, ANY, ANY, VMEM, VMEM],
        [
            pltpu.VMEM((6, LAT + 4, DEP, LON), F32),
            pltpu.VMEM((4, LAT + 2, DEP, LON), F32),
            pltpu.VMEM((5, LAT + 2, DEP, LON), F32),
            pltpu.VMEM((12, DEP, LON), F32),
            pltpu.VMEM((10 * DEP, LAT * LON), BF16),
            pltpu.SemaphoreType.DMA((3, LAT)),
        ],
        size=8 << 20,
        flops=1 << 30,
    )(motion, warmth, eta, cols, left, right, south, north, whi, wlo)

    mirror = [(p * lon + b, (1 - p) * lon + lon - 1 - b) for p in range(2) for b in range(lon)]
    incoming = lax.ppermute(values, ("panel", "lon"), mirror)

    (table,) = call(table_kernel, [shape(LAT * LON, 512, dtype=BF16)], [VMEM], size=2 << 20, flops=4 << 20)(receivers)

    flow, warm = call(
        place_kernel,
        [shape(4, 1, DEP, LAT, LON), shape(1, DEP, LAT, LON)],
        [VMEM, VMEM, VMEM],
        [pltpu.VMEM((10 * DEP + 16, 512), BF16), pltpu.VMEM((5,) + slab, F32), pltpu.SemaphoreType.DMA((2, LAT))],
        out_specs=[ANY, ANY],
        size=8 << 20,
        flops=1 << 30,
    )(fields, incoming, table)
    return flow, warm


def solution(mesh):
    field = P("panel", None, "lat", "lon")
    tile = ("panel", "lat", "lon")
    in_specs = (
        P(None, "panel", None, "lat", "lon"),
        field,
        field,
        P(),
        P(*tile, None),
        P(*tile, None, None),
        P(*tile, None, None),
    )
    out_specs = (P(None, "panel", None, "lat", "lon"), field)
    return jax.shard_map(shards, mesh=mesh, in_specs=in_specs, out_specs=out_specs, check_vma=False)
```

time: 225 us -> 70.8 us (0.31)
  the two profiles are of different devices: /device:TPU:57 before, /device:TPU:48 now
where the time goes in v1:
time: 70.8 us; the launch traced here: 70.1 us
  starting transfers between devices  27 us (38%)
  Pallas kernels  19.2 us (27%)
  waiting for transfers between devices  18 us (25%)
  local copies, waits for them, and re-layouts  5.17 us (7%)
  between operations  0.73 us (1%)
    ppermute x1, waiting for transfers between devices, shards(): incoming = lax.ppermute(values, ('panel', 'lon'), mirror)  13.6 us
    ppermute x1, starting transfers between devices, shards(): north = lax.ppermute(down, 'lat', back(lat))  9.93 us
    pallas_call x1, Pallas kernels, shards(): call(flow_kernel, [shape(5, *slab), shape(5 * DEP, 512)], [ANY, ANY, ANY,...  8.08 us
    unnamed x16, local copies, waits for them, and re-layouts  5.17 us
    ppermute x1, starting transfers between devices, shards(): incoming = lax.ppermute(values, ('panel', 'lon'), mirror)  4.86 us
    ppermute x1, starting transfers between devices, shards(): right = lax.ppermute(cols, 'lon', back(lon))  4.55 us
    ppermute x1, starting transfers between devices, shards(): south = lax.ppermute(up, 'lat', ahead(lat))  4.28 us
    pallas_call x1, Pallas kernels, shards(): call(edges_kernel, [shape(*slab), shape(3, DEP, LON), shape(12, DEP, LON)...  3.97 us
  transfers between devices with their start and end apart: 5, of which 5 were waited for; matrix products, arithmetic and copies ran while one was open for 0% of the time, Pallas kernels for 4%

profile of v1, /device:TPU:48, one launch (start us, length us, event | category | flops | bytes accessed | tf_op | source)
XLA Modules:
  0.0 70.1 jit_solution(7421770869218382771)
XLA Ops:
  0.6 0.0 copy-start
  0.6 1.2 %copy-done = f32[4,1,32,16,128]{4,3,2,1,0:T(8,128)S(1)} copy-done((f32[4,1,32,16,128]{4,3,2,1,0:T(8,128)S(1)}, f32[4,1,32,16,128]{4,3,2,1,0:T(8,128)}, u32[]{:S(2)}) %copy-start) | copy-done | bytes 1048600
  1.9 0.9 %copy-done.2 = f32[1,32,16,128]{3,2,1,0:T(8,128)S(1)} copy-done((f32[1,32,16,128]{3,2,1,0:T(8,128)S(1)}, f32[1,32,16,128]{3,2,1,0:T(8,128)}, u32[]{:S(2)}) %copy-start.2) | copy-done | bytes 262168
  2.8 0.9 %copy-done.3 = s32[1,32,16,128]{3,2,1,0:T(8,128)S(1)} copy-done((s32[1,32,16,128]{3,2,1,0:T(8,128)S(1)}, s32[1,32,16,128]{3,2,1,0:T(8,128)}, u32[]{:S(2)}) %copy-start.3) | copy-done | bytes 262168
  3.8 0.7 copy-done.5
  4.4 4.0 %shard_map.86 = (f32[16,32,128]{2,1,0:T(8,128)S(1)}, f32[3,32,128]{2,1,0:T(8,128)S(1)}, f32[12,32,128]{2,1,0:T(8,128)S(1)}, f32[12,32,128]{2,1,0:T(8,128)S(1)}) custom-call(f32[4,1,32,16,128]{4,3,2,1,0:T(8,128)S(1)} %copy-done, f32[1,32,16,128]{3,2,1,0:T(8,128)S(1)} %copy-done.2, s32[1,32,16,128]{3,2,1,0:T(8,128)S(1)} %copy-done.3, f32[8]{0:T(128)S(1)} %copy-done.5), custom_call_target="tpu_custom_call" | custom-call | bytes 2097152 | tf_op jit(solution)/shard_map/pallas_call | solution.py:316
  8.4 3.4 %collective-permute-start = (f32[3,32,128]{2,1,0:T(8,128)S(1)}, f32[3,32,128]{2,1,0:T(8,128)S(1)}, u32[]{:S(2)}, u32[]{:S(2)}) collective-permute-start(f32[3,32,128]{2,1,0:T(8,128)S(1)} %get-tuple-element.13.cols), channel_id=1, source_target_pairs={{0,16},{16,32},{32,48},{48,64},{64,80},{80,96},{96,112},{112,128},... | collective-permute-start | bytes 147464 | tf_op jit(solution)/shard_map/ppermute | solution.py:326
  11.8 4.6 %collective-permute-start.1 = (f32[3,32,128]{2,1,0:T(8,128)S(1)}, f32[3,32,128]{2,1,0:T(8,128)S(1)}, u32[]{:S(2)}, u32[]{:S(2)}) collective-permute-start(f32[3,32,128]{2,1,0:T(8,128)S(1)} %get-tuple-element.13.cols), channel_id=1, source_target_pairs={{16,0},{32,16},{48,32},{64,48},{80,64},{96,80},{112,96},{128,112},... | collective-permute-start | bytes 147464 | tf_op jit(solution)/shard_map/ppermute | solution.py:327
  16.4 0.1 collective-permute-done.left
  16.5 1.6 %collective-permute-done.1.right = f32[3,32,128]{2,1,0:T(8,128)S(1)} collective-permute-done((f32[3,32,128]{2,1,0:T(8,128)S(1)}, f32[3,32,128]{2,1,0:T(8,128)S(1)}, u32[]{:S(2)}, u32[]{:S(2)}) %collective-permute-start.1) | collective-permute-done | bytes 49184 | tf_op jit(solution)/shard_map/ppermute | solution.py:327
  18.1 0.1 shard_map.87
  18.2 4.3 %collective-permute-start.2 = (f32[12,32,128]{2,1,0:T(8,128)S(1)}, f32[12,32,128]{2,1,0:T(8,128)S(1)}, u32[]{:S(2)}, u32[]{:S(2)}) collective-permute-start(f32[12,32,128]{2,1,0:T(8,128)S(1)} %get-tuple-element.16), channel_id=1, source_target_pairs={{0,1},{1,2},{2,3},{3,4},{4,5},{5,6},{6,7},{7,8},{8,9},{9,10},{10,1... | collective-permute-start | bytes 589832 | tf_op jit(solution)/shard_map/ppermute | solution.py:337
  22.5 9.9 %collective-permute-start.3 = (f32[12,32,128]{2,1,0:T(8,128)S(1)}, f32[12,32,128]{2,1,0:T(8,128)S(1)}, u32[]{:S(2)}, u32[]{:S(2)}) collective-permute-start(f32[12,32,128]{2,1,0:T(8,128)S(1)} %get-tuple-element.17), channel_id=1, source_target_pairs={{1,0},{2,1},{3,2},{4,3},{5,4},{6,5},{7,6},{8,7},{9,8},{10,9},{11,1... | collective-permute-start | bytes 589832 | tf_op jit(solution)/shard_map/ppermute | solution.py:338
  32.5 0.0 copy-start.6
  32.5 0.7 copy-done.6
  33.2 0.7 copy-done.7
  33.9 2.3 %shard_map.88 = (bf16[2048,512]{1,0:T(8,128)(2,1)S(1)}, bf16[2048,512]{1,0:T(8,128)(2,1)S(1)}) custom-call(s32[4,512]{1,0:T(4,128)S(1)} %bitcast.4, f32[4,512]{1,0:T(4,128)S(1)} %bitcast.5), custom_call_target="tpu_custom_call" | custom-call | flops 20971520 | bytes 4194304 | tf_op jit(solution)/shard_map/pallas_call | solution.py:340
  36.2 1.5 %collective-permute-done.2.south = f32[12,32,128]{2,1,0:T(8,128)S(1)} collective-permute-done((f32[12,32,128]{2,1,0:T(8,128)S(1)}, f32[12,32,128]{2,1,0:T(8,128)S(1)}, u32[]{:S(2)}, u32[]{:S(2)}) %collective-permute-start.2) | collective-permute-done | bytes 196640 | tf_op jit(solution)/shard_map/ppermute | solution.py:337
  37.7 1.2 %collective-permute-done.3.north = f32[12,32,128]{2,1,0:T(8,128)S(1)} collective-permute-done((f32[12,32,128]{2,1,0:T(8,128)S(1)}, f32[12,32,128]{2,1,0:T(8,128)S(1)}, u32[]{:S(2)}, u32[]{:S(2)}) %collective-permute-start.3) | collective-permute-done | bytes 196640 | tf_op jit(solution)/shard_map/ppermute | solution.py:338
  38.9 8.1 %shard_map.89 = (f32[5,16,32,128]{3,2,1,0:T(8,128)S(1)}, f32[160,512]{1,0:T(8,128)S(1)}) custom-call(f32[4,1,32,16,128]{4,3,2,1,0:T(8,128)S(1)} %copy-done.1, f32[1,32,16,128]{3,2,1,0:T(8,128)S(1)} %copy-done.2, f32[16,32,128]{2,1,0:T(8,128)S(1)} %get-tuple-element.12.eta, f32[3,32,128]{2,1,0:T(8,128)S(1)} %get-tuple-element.13.cols, ...), custom_call_target="tpu_custom_call" | custom-call | flops 1073741824 | bytes 8388608 | tf_op jit(solution)/shard_map/pallas_call | solution.py:348
  47.0 4.9 %collective-permute-start.4 = (f32[160,512]{1,0:T(8,128)S(1)}, f32[160,512]{1,0:T(8,128)S(1)}, u32[]{:S(2)}, u32[]{:S(2)}) collective-permute-start(f32[160,512]{1,0:T(8,128)S(1)} %get-tuple-element.21), channel_id=1, source_target_pairs={{0,496},{16,480},{32,464},{48,448},{64,432},{80,416},{96,400},{112... | collective-permute-start | bytes 983048 | tf_op jit(solution)/shard_map/ppermute | solution.py:365
  51.8 0.7 %shard_map.90.table = bf16[2048,512]{1,0:T(8,128)(2,1)S(1)} custom-call(s32[1,512]{1,0:T(1,128)S(1)} %bitcast.3), custom_call_target="tpu_custom_call" | custom-call | flops 4194304 | bytes 2097152 | tf_op jit(solution)/shard_map/pallas_call | solution.py:367
  52.5 13.6 %collective-permute-done.4.values = f32[160,512]{1,0:T(8,128)S(1)} collective-permute-done((f32[160,512]{1,0:T(8,128)S(1)}, f32[160,512]{1,0:T(8,128)S(1)}, u32[]{:S(2)}, u32[]{:S(2)}) %collective-permute-start.4) | collective-permute-done | bytes 327712 | tf_op jit(solution)/shard_map/ppermute | solution.py:365
  66.2 3.9 %shard_map.91 = (f32[4,1,32,16,128]{4,3,2,1,0:T(8,128)}, f32[1,32,16,128]{3,2,1,0:T(8,128)}) custom-call(f32[5,16,32,128]{3,2,1,0:T(8,128)S(1)} %get-tuple-element.20.fields, f32[160,512]{1,0:T(8,128)S(1)} %collective-permute-done.4.values, bf16[2048,512]{1,0:T(8,128)(2,1)S(1)} %shard_map.90.table), custom_call_target="tpu_custom_call" | custom-call | flops 1073741824 | bytes 8388608 | tf_op jit(solution)/shard_map/pallas_call | solution.py:369
  (8 shorter events, 0.0 us)
Async XLA Ops:
  0.6 1.2 %copy-start = (f32[4,1,32,16,128]{4,3,2,1,0:T(8,128)S(1)}, f32[4,1,32,16,128]{4,3,2,1,0:T(8,128)}, u32[]{:S(2)}) copy-start(f32[4,1,32,16,128]{4,3,2,1,0:T(8,128)} %motion.3) | copy-start | bytes 3145732
  1.9 0.9 %copy-start.2 = (f32[1,32,16,128]{3,2,1,0:T(8,128)S(1)}, f32[1,32,16,128]{3,2,1,0:T(8,128)}, u32[]{:S(2)}) copy-start(f32[1,32,16,128]{3,2,1,0:T(8,128)} %warmth.3) | copy-start | bytes 786436
  2.8 0.9 %copy-start.3 = (s32[1,32,16,128]{3,2,1,0:T(8,128)S(1)}, s32[1,32,16,128]{3,2,1,0:T(8,128)}, u32[]{:S(2)}) copy-start(s32[1,32,16,128]{3,2,1,0:T(8,128)} %label.1) | copy-start | bytes 786436
  3.8 0.7 copy-start.5
  4.4 34.5 %copy-start.1 = (f32[4,1,32,16,128]{4,3,2,1,0:T(8,128)S(1)}, f32[4,1,32,16,128]{4,3,2,1,0:T(8,128)}, u32[]{:S(2)}) copy-start(f32[4,1,32,16,128]{4,3,2,1,0:T(8,128)} %motion.3) | copy-start | bytes 3145732
  8.4 8.1 %collective-permute-start = (f32[3,32,128]{2,1,0:T(8,128)S(1)}, f32[3,32,128]{2,1,0:T(8,128)S(1)}, u32[]{:S(2)}, u32[]{:S(2)}) collective-permute-start(f32[3,32,128]{2,1,0:T(8,128)S(1)} %get-tuple-element.13.cols), channel_id=1, source_target_pairs={{0,16},{16,32},{32,48},{48,64},{64,80},{80,96},{96,112},{112,128},... | collective-permute-start | bytes 147464 | tf_op jit(solution)/shard_map/ppermute | solution.py:326
  11.8 6.3 %collective-permute-start.1 = (f32[3,32,128]{2,1,0:T(8,128)S(1)}, f32[3,32,128]{2,1,0:T(8,128)S(1)}, u32[]{:S(2)}, u32[]{:S(2)}) collective-permute-start(f32[3,32,128]{2,1,0:T(8,128)S(1)} %get-tuple-element.13.cols), channel_id=1, source_target_pairs={{16,0},{32,16},{48,32},{64,48},{80,64},{96,80},{112,96},{128,112},... | collective-permute-start | bytes 147464 | tf_op jit(solution)/shard_map/ppermute | solution.py:327
  18.2 19.4 %collective-permute-start.2 = (f32[12,32,128]{2,1,0:T(8,128)S(1)}, f32[12,32,128]{2,1,0:T(8,128)S(1)}, u32[]{:S(2)}, u32[]{:S(2)}) collective-permute-start(f32[12,32,128]{2,1,0:T(8,128)S(1)} %get-tuple-element.16), channel_id=1, source_target_pairs={{0,1},{1,2},{2,3},{3,4},{4,5},{5,6},{6,7},{7,8},{8,9},{9,10},{10,1... | collective-permute-start | bytes 589832 | tf_op jit(solution)/shard_map/ppermute | solution.py:337
  22.5 16.3 %collective-permute-start.3 = (f32[12,32,128]{2,1,0:T(8,128)S(1)}, f32[12,32,128]{2,1,0:T(8,128)S(1)}, u32[]{:S(2)}, u32[]{:S(2)}) collective-permute-start(f32[12,32,128]{2,1,0:T(8,128)S(1)} %get-tuple-element.17), channel_id=1, source_target_pairs={{1,0},{2,1},{3,2},{4,3},{5,4},{6,5},{7,6},{8,7},{9,8},{10,9},{11,1... | collective-permute-start | bytes 589832 | tf_op jit(solution)/shard_map/ppermute | solution.py:338
  32.5 0.7 copy-start.6
  33.2 0.7 copy-start.7
  38.9 13.0 %copy-start.4 = (s32[1,1,1,512]{3,2,1,0:T(1,128)S(1)}, s32[1,1,1,512]{3,2,1,0:T(1,128)}, u32[]{:S(2)}) copy-start(s32[1,1,1,512]{3,2,1,0:T(1,128)} %param.11) | copy-start | bytes 6148
  47.0 19.2 %collective-permute-start.4 = (f32[160,512]{1,0:T(8,128)S(1)}, f32[160,512]{1,0:T(8,128)S(1)}, u32[]{:S(2)}, u32[]{:S(2)}) collective-permute-start(f32[160,512]{1,0:T(8,128)S(1)} %get-tuple-element.21), channel_id=1, source_target_pairs={{0,496},{16,480},{32,464},{48,448},{64,432},{80,416},{96,400},{112... | collective-permute-start | bytes 983048 | tf_op jit(solution)/shard_map/ppermute | solution.py:365

commit v2 on v1

v2 whole, which is shorter than its diff:
```python
import jax
import jax.numpy as jnp
from jax import lax
from jax.experimental import pallas as pl
from jax.experimental.pallas import tpu as pltpu
from jax.sharding import PartitionSpec as P

OMEGA = 0.6
BETA = 0.5
TIME_STEP = 0.05
DIFFUSIVITY = 2.3

F32 = jnp.float32
BF16 = jnp.bfloat16
ANY = pl.BlockSpec(memory_space=pl.ANY)
VMEM = pl.BlockSpec(memory_space=pltpu.VMEM)
HBM = pl.BlockSpec(memory_space=pltpu.HBM)

LAT, DEP, LON = 16, 32, 128


def iota(dim, shape=(DEP, LON)):
    return lax.broadcasted_iota(jnp.int32, shape, dim)


def roll(x, shift, axis):
    return pltpu.roll(x, shift, axis)


def depth_pair(x):
    row = iota(0, x.shape)
    lower = jnp.where(row == 0, 0.0, roll(x, 1, 0))
    upper = jnp.where(row == x.shape[0] - 1, 0.0, roll(x, x.shape[0] - 1, 0))
    return lower, upper


def lon_pair(x, edge, r):
    lane = iota(1, x.shape)
    halo = roll(edge, 122 - 4 * r, 1)
    lower = jnp.where(lane == 0, halo, roll(x, 1, 1))
    upper = jnp.where(lane == LON - 1, halo, roll(x, LON - 1, 1))
    return lower, upper


def swap_middle(c):
    pos = iota(1, c.shape) & 3
    return jnp.where(pos == 1, roll(c, LON - 1, 1), roll(c, 1, 1))


def relax(centre, pairs, faces, scale, eta, warmth):
    out = []
    for c in range(3):
        total = 0.0
        for e in range(3):
            for s in range(2):
                total = total + faces[e][s] * pairs[c][e][s]
        total = total - (pairs[3][c][1] - pairs[3][c][0])
        if c == 0:
            total = total + 4.0 * (warmth - 0.5)
        out.append((1.0 - OMEGA) * centre[c] + total * scale)
    div = 0.0
    for c in range(3):
        div = div + (pairs[c][c][1] - pairs[c][c][0])
    out.append(centre[3] - (0.5 * BETA) * eta * div)
    return out


def stage_kernel(
    motion, warmth, label, chart, receivers, donors, factors,
    f, cols_out, up_out, down_out, receivers_out, donors_out, factors_out,
    lab, table, sems,
):
    small = [
        pltpu.make_async_copy(chart, table, sems.at[3, 0]),
        pltpu.make_async_copy(receivers, receivers_out, sems.at[3, 1]),
        pltpu.make_async_copy(donors, donors_out, sems.at[3, 2]),
        pltpu.make_async_copy(factors, factors_out, sems.at[3, 3]),
    ]
    scalars, flow = [], []
    for r in range(LAT):
        scalars.append(pltpu.make_async_copy(warmth.at[0, :, r, :], f.at[5, r], sems.at[0, r]))
        scalars.append(pltpu.make_async_copy(label.at[0, :, r, :], lab.at[r], sems.at[1, r]))
        flow.append(pltpu.make_async_copy(motion.at[:, 0, :, r, :], f.at[0:4, r], sems.at[2, r]))
    for c in small[:1] + scalars + flow + small[1:]:
        c.start()
    for c in small[:1] + scalars:
        c.wait()

    def stiffness(r, _):
        kind = lab[r]
        exponent = jnp.full(kind.shape, table[0], F32)
        for entry in range(1, 8):
            exponent = jnp.where(kind == entry, table[entry], exponent)
        f[4, r] = jnp.exp(exponent + DIFFUSIVITY * (0.5 - f[5, r]))
        return 0

    lax.fori_loop(0, LAT, stiffness, 0, unroll=4)
    for c in flow:
        c.wait()

    group = iota(1) >> 2

    def pack(r, acc):
        new = []
        for q in range(3):
            first = roll(f[2 * q, r], 4 * r + 2, 1)
            second = roll(f[2 * q + 1, r], 4 * r + 66, 1)
            new.append(jnp.where(group == r, first, jnp.where(group == r + 16, second, acc[q])))
        return tuple(new)

    zero = jnp.zeros((DEP, LON), F32)
    packed = lax.fori_loop(0, LAT, pack, (zero, zero, zero), unroll=4)
    for q in range(3):
        cols_out[q] = packed[q]
    for out, outer, inner in ((up_out, 14, 15), (down_out, 1, 0)):
        for k in range(5):
            out[k] = f[k, outer]
        for k in range(6):
            out[5 + k] = f[k, inner]
        out[11] = zero
    for c in small[1:]:
        c.wait()


def corners_kernel(left, right, up, down, _, up_out, down_out, cu, cd, sems):
    lane = iota(1)
    pos = lane & 3
    group = (lane >> 2) & 15
    pairs = [jnp.where(pos < 2, left[q], right[q]) for q in range(3)]
    cu[...] = jnp.where(group == 15, pairs[0], jnp.where(group == 14, roll(pairs[1], 124, 1), roll(pairs[2], 120, 1)))
    cd[...] = jnp.where(group == 0, pairs[0], jnp.where(group == 1, roll(pairs[1], 4, 1), roll(pairs[2], 8, 1)))
    a = pltpu.make_async_copy(cu, up_out.at[11], sems.at[0])
    b = pltpu.make_async_copy(cd, down_out.at[11], sems.at[1])
    a.start()
    b.start()
    a.wait()
    b.wait()


def weights_kernel(donors, factors, hi, lo):
    def body(i, _):
        cell = iota(0, (32, 512)) + i * 32
        w = jnp.zeros((32, 512), F32)
        for j in range(4):
            w = w + jnp.where(cell == donors[j : j + 1, :], factors[j : j + 1, :], 0.0)
        top = w.astype(BF16)
        at = pl.ds(pl.multiple_of(i * 32, 32), 32)
        hi[at, :] = top
        lo[at, :] = (w - top.astype(F32)).astype(BF16)
        return 0

    lax.fori_loop(0, LAT * LON // 32, body, 0)


def table_kernel(receivers, table, struck):
    columns = []
    for b in range(4):
        row = receivers[:, b * 128 : (b + 1) * 128].astype(F32)
        columns.append(jnp.broadcast_to(row, (128, 128)).T.astype(jnp.int32))

    def body(i, _):
        cell = iota(1, (128, LON)) + i * LON
        at = pl.ds(pl.multiple_of(i * LON, LON), LON)
        total = jnp.zeros((1, LON), F32)
        for b in range(4):
            hit = jnp.where(cell == columns[b], 1.0, 0.0)
            table[b * 128 : (b + 1) * 128, at] = hit.astype(BF16)
            total = total + jnp.sum(hit, axis=0, keepdims=True)
        struck[:, at] = jnp.broadcast_to(total, (8, LON))
        return 0

    lax.fori_loop(0, LAT, body, 0)


def edge_columns(cols, left, right, corners):
    lane = iota(1)
    pos, group = lane & 3, lane >> 2
    halo, own = [], []
    for k in range(6):
        q, h = k // 2, k % 2
        c = roll(jnp.where(pos < 2, left[q], right[q]), 4 + 64 * h, 1)
        low = high = 0.0
        if corners is not None:
            low = roll(corners[0], (68 + 64 * h + 4 * q) % 128, 1)
            high = roll(corners[1], (68 + 64 * h - 4 * q) % 128, 1)
        halo.append(jnp.where(group == 0, low, jnp.where(group == 17, high, c)))
        own.append(roll(cols[q], 4 + 64 * h, 1))
    return halo, own


def relax_columns(halo, own):
    middle = (iota(1) & 3) == 1

    def pairs_of(k):
        c, o = halo[k], own[k]
        lower = jnp.where(middle, roll(c, 1, 1), roll(o, 1, 1))
        upper = jnp.where(middle, roll(o, LON - 1, 1), roll(c, LON - 1, 1))
        return depth_pair(c), (roll(c, 4, 1), roll(c, LON - 4, 1)), (lower, upper)

    faces, scale = faces_of(halo[4], pairs_of(4))
    inside = halo[4] > 0.0
    new = relax(halo[:4], [pairs_of(k) for k in range(4)], faces, scale, halo[4], halo[5])
    return [jnp.where(inside, v, 0.0) for v in new]


def faces_of(eta, pairs):
    faces = [[eta + n for n in pair] for pair in pairs]
    diagonal = faces[0][0] + faces[0][1] + faces[1][0] + faces[1][1] + faces[2][0] + faces[2][1]
    return faces, OMEGA / jnp.where(diagonal > 0.0, diagonal, 1.0)


def advance(t, pairs, speed):
    change = 0.0
    for e, (lower, upper) in enumerate(pairs):
        change = (
            change
            - jnp.maximum(speed[e], 0.0) * (t - lower)
            - jnp.minimum(speed[e], 0.0) * (upper - t)
            + (upper + lower - 2.0 * t)
        )
    return t + TIME_STEP * change


def blend(lhs, hi, lo):
    n = 5 * DEP
    wide = jnp.dot(lhs, hi, preferred_element_type=F32)
    return wide[:n] + wide[n:] + jnp.dot(lhs[:n], lo, preferred_element_type=F32)


def put_split(lhs, k, at, value):
    top = value.astype(BF16)
    lhs[k * DEP : (k + 1) * DEP, at] = top
    lhs[(5 + k) * DEP : (6 + k) * DEP, at] = (value - top.astype(F32)).astype(BF16)


def inner_kernel(f, cols, left, right, whi, wlo, mid_out, values_out, s1_out, faces_out, s1, faces, edge, lhs):
    halo, own = edge_columns(cols, left, right, None)
    for k in range(6):
        edge[k] = swap_middle(halo[k])
    for k, v in enumerate(relax_columns(halo, own)):
        edge[6 + k] = swap_middle(v)

    def first(r, _):
        eta = f[4, r]
        both, scale = faces_of(eta, (depth_pair(eta), (f[4, r - 1], f[4, r + 1]), lon_pair(eta, edge[4], r)))
        for j, v in enumerate((both[0][0], both[0][1], both[2][0], both[2][1], scale)):
            faces[j, r] = v
        centre = [f[k, r] for k in range(4)]
        pairs = [(depth_pair(centre[k]), (f[k, r - 1], f[k, r + 1]), lon_pair(centre[k], edge[k], r)) for k in range(4)]
        for k, v in enumerate(relax(centre, pairs, both, scale, eta, f[5, r])):
            s1[k, r] = v
        return 0

    lax.fori_loop(1, LAT - 1, first, 0)

    def second(r, _):
        eta = f[4, r]
        both = ((faces[0, r], faces[1, r]), (eta + f[4, r - 1], eta + f[4, r + 1]), (faces[2, r], faces[3, r]))
        centre = [s1[k, r] for k in range(4)]
        pairs = [(depth_pair(centre[k]), (s1[k, r - 1], s1[k, r + 1]), lon_pair(centre[k], edge[6 + k], r)) for k in range(4)]
        t = f[5, r]
        new = relax(centre, pairs, both, faces[4, r], eta, t)
        new.append(advance(t, (depth_pair(t), (f[5, r - 1], f[5, r + 1]), lon_pair(t, edge[5], r)), new))
        at = pl.ds(pl.multiple_of((r - 2) * LON, LON), LON)
        for k in range(5):
            mid_out[k, r - 2] = new[k]
            put_split(lhs, k, at, new[k])
        return 0

    lax.fori_loop(2, LAT - 2, second, 0)
    values_out[...] = blend(lhs[...], whi[2 * LON : 14 * LON], wlo[2 * LON : 14 * LON])
    for k in range(4):
        for j, r in enumerate((1, 2, 13, 14)):
            s1_out[k, j] = s1[k, r]
    for k in range(5):
        for j, r in enumerate((1, 14)):
            faces_out[k, j] = faces[k, r]


def rim_kernel(f, cols, left, right, south, north, s1_in, faces_in, partial, whi, wlo, rim_out, values_out, lhs):
    halo, own = edge_columns(cols, left, right, (south[11], north[11]))
    edge = [swap_middle(h) for h in halo]
    edge1 = [swap_middle(v) for v in relax_columns(halo, own)]

    def field(k, r):
        if r < 0:
            return south[k] if r == -2 else south[5 + k]
        if r >= LAT:
            return north[k] if r == LAT + 1 else north[5 + k]
        return f[k, r]

    s1, faces = {}, {}
    for j, r in enumerate((1, 2, 13, 14)):
        s1[r] = [s1_in[k, j] for k in range(4)]
    for j, r in enumerate((1, 14)):
        low, high, left_face, right_face, scale = (faces_in[k, j] for k in range(5))
        eta = f[4, r]
        faces[r] = (((low, high), (eta + f[4, r - 1], eta + f[4, r + 1]), (left_face, right_face)), scale)
    for r in (-1, 0, LAT - 1, LAT):
        eta = field(4, r)
        faces[r] = faces_of(eta, (depth_pair(eta), (field(4, r - 1), field(4, r + 1)), lon_pair(eta, edge[4], r)))
        centre = [field(k, r) for k in range(4)]
        pairs = [(depth_pair(centre[k]), (field(k, r - 1), field(k, r + 1)), lon_pair(centre[k], edge[k], r)) for k in range(4)]
        s1[r] = relax(centre, pairs, *faces[r], eta, field(5, r))
        if r < 0 or r >= LAT:
            s1[r] = [jnp.where(eta > 0.0, v, 0.0) for v in s1[r]]
    for j, r in enumerate((0, 1, 14, 15)):
        centre = s1[r]
        pairs = [(depth_pair(centre[k]), (s1[r - 1][k], s1[r + 1][k]), lon_pair(centre[k], edge1[k], r)) for k in range(4)]
        t = f[5, r]
        new = relax(centre, pairs, *faces[r], f[4, r], t)
        new.append(advance(t, (depth_pair(t), (field(5, r - 1), field(5, r + 1)), lon_pair(t, edge[5], r)), new))
        for k in range(5):
            rim_out[k, j] = new[k]
            put_split(lhs, k, slice(j * LON, (j + 1) * LON), new[k])
    low, high = slice(0, 2 * LON), slice(14 * LON, 16 * LON)
    values_out[...] = (
        partial[...] + blend(lhs[:, : 2 * LON], whi[low], wlo[low]) + blend(lhs[:, 2 * LON :], whi[high], wlo[high])
    )


def place_kernel(mid, rim, values, table, struck, flow_out, warmth_out, lhs, out, sems):
    n = 5 * DEP
    v = values[...]
    top = v.astype(BF16)
    lhs[0:n] = top
    lhs[n : 2 * n] = (v - top.astype(F32)).astype(BF16)
    copies = []
    for g in range(LAT // 2):
        placed = jnp.dot(lhs[...], table[:, g * 256 : (g + 1) * 256], preferred_element_type=F32)
        merged = placed[:n] + placed[n : 2 * n]
        for h in range(2):
            r = 2 * g + h
            at = slice(h * LON, (h + 1) * LON)
            hit = struck[0:1, r * LON : (r + 1) * LON] > 0.5
            for k in range(5):
                kept = mid[k, r - 2] if 2 <= r < 14 else rim[k, r if r < 2 else r - 12]
                out[k, r] = jnp.where(hit, merged[k * DEP : (k + 1) * DEP, at], kept)
            copies.append(pltpu.make_async_copy(out.at[0:4, r], flow_out.at[:, 0, :, r, :], sems.at[0, r]))
            copies.append(pltpu.make_async_copy(out.at[4, r], warmth_out.at[0, :, r, :], sems.at[1, r]))
            copies[-2].start()
            copies[-1].start()
    for c in copies:
        c.wait()


def shape(*dims, dtype=F32):
    return jax.ShapeDtypeStruct(dims, dtype)


def call(kernel, outs, ins, scratch=(), out_specs=None, flops=0, size=0, aliases=None, limit=None):
    return pl.pallas_call(
        kernel,
        out_shape=outs,
        in_specs=ins,
        out_specs=out_specs or [VMEM] * len(outs),
        scratch_shapes=list(scratch),
        input_output_aliases=aliases or {},
        cost_estimate=pl.CostEstimate(flops=flops, bytes_accessed=size, transcendentals=0),
        compiler_params=pltpu.CompilerParams(vmem_limit_bytes=limit or (32 << 20)),
    )


def in_hbm(x):
    return pltpu.with_memory_space_constraint(x, pltpu.HBM)


def shards(motion, warmth, label, chart, receivers, donors, factors):
    lon, lat = lax.axis_size("lon"), lax.axis_size("lat")
    n, slab = 5 * DEP, (DEP, LON)

    f, cols, up, down, receivers, donors, factors = call(
        stage_kernel,
        [
            shape(6, LAT, *slab), shape(3, *slab), shape(12, *slab), shape(12, *slab),
            shape(1, 512, dtype=jnp.int32), shape(4, 512, dtype=jnp.int32), shape(4, 512),
        ],
        [HBM] * 7,
        [pltpu.VMEM((LAT,) + slab, jnp.int32), pltpu.SMEM((8,), F32), pltpu.SemaphoreType.DMA((4, LAT))],
        size=2 << 20,
    )(*map(in_hbm, (motion, warmth, label, chart, receivers.reshape(1, 512), donors.reshape(4, 512), factors.reshape(4, 512))))

    ahead = lambda n: [(i, i + 1) for i in range(n - 1)]
    back = lambda n: [(i + 1, i) for i in range(n - 1)]
    left = lax.ppermute(cols, "lon", ahead(lon))
    right = lax.ppermute(cols, "lon", back(lon))
    whi, wlo = call(
        weights_kernel,
        [shape(LAT * LON, 512, dtype=BF16), shape(LAT * LON, 512, dtype=BF16)],
        [VMEM, VMEM],
        size=4 << 20,
        flops=20 << 20,
    )(donors, factors)
    up, down = call(
        corners_kernel,
        [shape(12, *slab), shape(12, *slab)],
        [VMEM, VMEM, ANY, ANY, ANY],
        [pltpu.VMEM(slab, F32), pltpu.VMEM(slab, F32), pltpu.SemaphoreType.DMA((2,))],
        out_specs=[ANY, ANY],
        aliases={2: 0, 3: 1},
        size=1 << 16,
    )(left, right, up, down, whi)
    south = lax.ppermute(up, "lat", ahead(lat))
    north = lax.ppermute(down, "lat", back(lat))

    mid, partial, s1, faces = call(
        inner_kernel,
        [shape(5, 12, *slab), shape(n, 512), shape(4, 4, *slab), shape(5, 2, *slab)],
        [VMEM] * 6,
        [
            pltpu.VMEM((4, LAT) + slab, F32),
            pltpu.VMEM((5, LAT) + slab, F32),
            pltpu.VMEM((10,) + slab, F32),
            pltpu.VMEM((2 * n, 12 * LON), BF16),
        ],
        size=8 << 20,
        flops=1 << 30,
    )(f, cols, left, right, whi, wlo)
    rim, values = call(
        rim_kernel,
        [shape(5, 4, *slab), shape(n, 512)],
        [VMEM] * 11,
        [pltpu.VMEM((2 * n, 4 * LON), BF16)],
        size=2 << 20,
        flops=1 << 28,
    )(f, cols, left, right, south, north, s1, faces, partial, whi, wlo)

    mirror = [(p * lon + b, (1 - p) * lon + lon - 1 - b) for p in range(2) for b in range(lon)]
    incoming = lax.ppermute(values, ("panel", "lon"), mirror)

    table, struck = call(
        table_kernel,
        [shape(512, LAT * LON, dtype=BF16), shape(8, LAT * LON)],
        [VMEM],
        size=2 << 20,
        flops=4 << 20,
    )(receivers)

    flow, warm = call(
        place_kernel,
        [shape(4, 1, DEP, LAT, LON), shape(1, DEP, LAT, LON)],
        [VMEM] * 5,
        [pltpu.VMEM((2 * n, 512), BF16), pltpu.VMEM((5, LAT) + slab, F32), pltpu.SemaphoreType.DMA((2, LAT))],
        out_specs=[ANY, ANY],
        size=8 << 20,
        flops=1 << 30,
    )(mid, rim, incoming, table, struck)
    return flow, warm


def solution(mesh):
    field = P("panel", None, "lat", "lon")
    tile = ("panel", "lat", "lon")
    in_specs = (
        P(None, "panel", None, "lat", "lon"),
        field,
        field,
        P(),
        P(*tile, None),
        P(*tile, None, None),
        P(*tile, None, None),
    )
    out_specs = (P(None, "panel", None, "lat", "lon"), field)
    return jax.shard_map(shards, mesh=mesh, in_specs=in_specs, out_specs=out_specs, check_vma=False)
```

time: 70.8 us -> 60.7 us (0.86)
  local copies, waits for them, and re-layouts: 5.17 us -> 0 us
  waiting for transfers between devices: 18 us -> 14.9 us
  Pallas kernels: 19.2 us -> 16.2 us
  starting transfers between devices: 27 us -> 28.3 us
    unnamed x16 -> x0, local copies, waits for them, and re-layouts: 5.17 us -> none
    pallas_call x4 -> x5, Pallas kernels: 12.9 us -> 10.3 us  [the longest x1 4.9 us: shards(): call(inner_kernel, [shape(5, 12, *slab), shape(n, 512), shape(4, 4, *slab...]
    ppermute x1, waiting for transfers between devices: 1.6 us -> 0.01 us  [shards(): right = lax.ppermute(cols, 'lon', back(lon))]
    ppermute x1, waiting for transfers between devices: 1.48 us -> 0.01 us  [shards(): south = lax.ppermute(up, 'lat', ahead(lat))]
    ppermute x1, starting transfers between devices: 4.86 us -> 6.12 us  [shards(): incoming = lax.ppermute(values, ('panel', 'lon'), mirror)]
  transfers between devices with their start and end apart: 5 -> 5, of which waited for: 5 -> 2; matrix products, arithmetic and copies ran while one was open for 0% -> 0% of each run, Pallas kernels for 4% -> 14%
where the time goes in v2:
time: 60.7 us; the launch traced here: 60.1 us
  starting transfers between devices  28.3 us (47%)
  Pallas kernels  16.2 us (27%)
  waiting for transfers between devices  14.9 us (25%)
  between operations  0.74 us (1%)
    ppermute x1, waiting for transfers between devices, shards(): incoming = lax.ppermute(values, ('panel', 'lon'), mirror)  14 us
    ppermute x1, starting transfers between devices, shards(): north = lax.ppermute(down, 'lat', back(lat))  9.93 us
    ppermute x1, starting transfers between devices, shards(): incoming = lax.ppermute(values, ('panel', 'lon'), mirror)  6.12 us
    pallas_call x1, Pallas kernels, shards(): call(inner_kernel, [shape(5, 12, *slab), shape(n, 512), shape(4, 4, *slab...  4.9 us
    ppermute x1, starting transfers between devices, shards(): right = lax.ppermute(cols, 'lon', back(lon))  4.55 us
    ppermute x1, starting transfers between devices, shards(): south = lax.ppermute(up, 'lat', ahead(lat))  4.28 us
    pallas_call x1, Pallas kernels, shards(): call(place_kernel, [shape(4, 1, DEP, LAT, LON), shape(1, DEP, LAT, LON)],...  3.56 us
    ppermute x1, starting transfers between devices, shards(): left = lax.ppermute(cols, 'lon', ahead(lon))  3.4 us
  transfers between devices with their start and end apart: 5, of which 2 were waited for; matrix products, arithmetic and copies ran while one was open for 0% of the time, Pallas kernels for 14%

profile of v2, /device:TPU:48, one launch (start us, length us, event | category | flops | bytes accessed | tf_op | source)
XLA Modules:
  0.0 60.1 jit_solution(16907173379502820413)
XLA Ops:
  0.6 2.8 %shard_map.86 = (f32[6,16,32,128]{3,2,1,0:T(8,128)S(1)}, f32[3,32,128]{2,1,0:T(8,128)S(1)}, f32[12,32,128]{2,1,0:T(8,128)S(1)}, f32[12,32,128]{2,1,0:T(8,128)S(1...) custom-call(f32[4,1,32,16,128]{4,3,2,1,0:T(8,128)} %motion.1, f32[1,32,16,128]{3,2,1,0:T(8,128)} %warmth.1, ...), custom_call_target="tpu_custom_call" | custom-call | bytes 2097152 | tf_op jit(solution)/shard_map/pallas_call | solution.py:372
  3.5 3.4 %collective-permute-start = (f32[3,32,128]{2,1,0:T(8,128)S(1)}, f32[3,32,128]{2,1,0:T(8,128)S(1)}, u32[]{:S(2)}, u32[]{:S(2)}) collective-permute-start(f32[3,32,128]{2,1,0:T(8,128)S(1)} %get-tuple-element.22.cols), channel_id=1, source_target_pairs={{0,16},{16,32},{32,48},{48,64},{64,80},{80,96},{96,112},{112,128},... | collective-permute-start | bytes 147464 | tf_op jit(solution)/shard_map/ppermute | solution.py:385
  6.9 4.6 %collective-permute-start.1 = (f32[3,32,128]{2,1,0:T(8,128)S(1)}, f32[3,32,128]{2,1,0:T(8,128)S(1)}, u32[]{:S(2)}, u32[]{:S(2)}) collective-permute-start(f32[3,32,128]{2,1,0:T(8,128)S(1)} %get-tuple-element.22.cols), channel_id=1, source_target_pairs={{16,0},{32,16},{48,32},{64,48},{80,64},{96,80},{112,96},{128,112},... | collective-permute-start | bytes 147464 | tf_op jit(solution)/shard_map/ppermute | solution.py:386
  11.5 2.3 %shard_map.87 = (bf16[2048,512]{1,0:T(8,128)(2,1)S(1)}, bf16[2048,512]{1,0:T(8,128)(2,1)S(1)}) custom-call(s32[4,512]{1,0:T(4,128)S(1)} %get-tuple-element.23.donors, f32[4,512]{1,0:T(4,128)S(1)} %get-tuple-element.24.factors), custom_call_target="tpu_custom_call" | custom-call | flops 20971520 | bytes 4194304 | tf_op jit(solution)/shard_map/pallas_call | solution.py:387
  13.8 0.0 collective-permute-done.left
  13.8 0.0 collective-permute-done.1.right
  13.8 0.1 shard_map.89
  14.0 4.3 %collective-permute-start.2 = (f32[12,32,128]{2,1,0:T(8,128)S(1)}, f32[12,32,128]{2,1,0:T(8,128)S(1)}, u32[]{:S(2)}, u32[]{:S(2)}) collective-permute-start(f32[12,32,128]{2,1,0:T(8,128)S(1)} %get-tuple-element.30), channel_id=1, source_target_pairs={{0,1},{1,2},{2,3},{3,4},{4,5},{5,6},{6,7},{7,8},{8,9},{9,10},{10,1... | collective-permute-start | bytes 589832 | tf_op jit(solution)/shard_map/ppermute | solution.py:403
  18.3 9.9 %collective-permute-start.3 = (f32[12,32,128]{2,1,0:T(8,128)S(1)}, f32[12,32,128]{2,1,0:T(8,128)S(1)}, u32[]{:S(2)}, u32[]{:S(2)}) collective-permute-start(f32[12,32,128]{2,1,0:T(8,128)S(1)} %get-tuple-element.31), channel_id=1, source_target_pairs={{1,0},{2,1},{3,2},{4,3},{5,4},{6,5},{7,6},{8,7},{9,8},{10,9},{11,1... | collective-permute-start | bytes 589832 | tf_op jit(solution)/shard_map/ppermute | solution.py:404
  28.2 4.9 %shard_map.88 = (f32[5,12,32,128]{3,2,1,0:T(8,128)S(1)}, f32[160,512]{1,0:T(8,128)S(1)}, f32[4,4,32,128]{3,2,1,0:T(8,128)S(1)}, f32[5,2,32,128]{3,2,1,0:T(8,128)S(1)}) custom-call(f32[6,16,32,128]{3,2,1,0:T(8,128)S(1)} %get-tuple-element.21.f, f32[3,32,128]{2,1,0:T(8,128)S(1)} %get-tuple-element.22.cols, f32[3,32,128]{2,1,0:T(8,128)S(1)} %collective-permute-done.left, ...), custom_call_target="tpu_custom_call" | custom-call | flops 1073741824 | bytes 8388608 | tf_op jit(solution)/shard_map/pallas_call | solution.py:406
  33.1 0.0 collective-permute-done.2.south
  33.1 0.8 %collective-permute-done.3.north = f32[12,32,128]{2,1,0:T(8,128)S(1)} collective-permute-done((f32[12,32,128]{2,1,0:T(8,128)S(1)}, f32[12,32,128]{2,1,0:T(8,128)S(1)}, u32[]{:S(2)}, u32[]{:S(2)}) %collective-permute-start.3) | collective-permute-done | bytes 196640 | tf_op jit(solution)/shard_map/ppermute | solution.py:404
  34.0 1.3 %shard_map.90 = (f32[5,4,32,128]{3,2,1,0:T(8,128)S(1)}, f32[160,512]{1,0:T(8,128)S(1)}) custom-call(f32[6,16,32,128]{3,2,1,0:T(8,128)S(1)} %get-tuple-element.21.f, f32[3,32,128]{2,1,0:T(8,128)S(1)} %get-tuple-element.22.cols, f32[3,32,128]{2,1,0:T(8,128)S(1)} %collective-permute-done.left, f32[3,32,128]{2,1,0:T(8,128)S(1)} %collective-permute-done.1.right, ...), custom_call_target="tpu_custom_call" | custom-call | flops 268435456 | bytes 2097152 | tf_op jit(solution)/shard_map/pallas_call | solution.py:419
  35.3 6.1 %collective-permute-start.4 = (f32[160,512]{1,0:T(8,128)S(1)}, f32[160,512]{1,0:T(8,128)S(1)}, u32[]{:S(2)}, u32[]{:S(2)}) collective-permute-start(f32[160,512]{1,0:T(8,128)S(1)} %get-tuple-element.36), channel_id=1, source_target_pairs={{0,496},{16,480},{32,464},{48,448},{64,432},{80,416},{96,400},{112... | collective-permute-start | bytes 983048 | tf_op jit(solution)/shard_map/ppermute | solution.py:429
  41.4 1.1 %shard_map.91 = (bf16[512,2048]{1,0:T(8,128)(2,1)S(1)}, f32[8,2048]{1,0:T(8,128)S(1)}) custom-call(s32[1,512]{1,0:T(1,128)S(1)} %get-tuple-element.37.receivers), custom_call_target="tpu_custom_call" | custom-call | flops 4194304 | bytes 2097152 | tf_op jit(solution)/shard_map/pallas_call | solution.py:431
  42.5 14.0 %collective-permute-done.4.values = f32[160,512]{1,0:T(8,128)S(1)} collective-permute-done((f32[160,512]{1,0:T(8,128)S(1)}, f32[160,512]{1,0:T(8,128)S(1)}, u32[]{:S(2)}, u32[]{:S(2)}) %collective-permute-start.4) | collective-permute-done | bytes 327712 | tf_op jit(solution)/shard_map/ppermute | solution.py:429
  56.5 3.6 %shard_map.92 = (f32[4,1,32,16,128]{4,3,2,1,0:T(8,128)}, f32[1,32,16,128]{3,2,1,0:T(8,128)}) custom-call(f32[5,12,32,128]{3,2,1,0:T(8,128)S(1)} %get-tuple-element.27.mid, f32[5,4,32,128]{3,2,1,0:T(8,128)S(1)} %get-tuple-element.35.rim, f32[160,512]{1,0:T(8,128)S(1)} %collective-permute-done.4.values, bf16[512,2048]{1,0:T(8,128)(2,1)S(1)} %get-tuple-element.38.table, ...), custom_call_target="tpu_custom_call" | custom-call | flops 1073741824 | bytes 8388608 | tf_op jit(solution)/shard_map/pallas_call | solution.py:439
Async XLA Ops:
  3.5 10.3 %collective-permute-start = (f32[3,32,128]{2,1,0:T(8,128)S(1)}, f32[3,32,128]{2,1,0:T(8,128)S(1)}, u32[]{:S(2)}, u32[]{:S(2)}) collective-permute-start(f32[3,32,128]{2,1,0:T(8,128)S(1)} %get-tuple-element.22.cols), channel_id=1, source_target_pairs={{0,16},{16,32},{32,48},{48,64},{64,80},{80,96},{96,112},{112,128},... | collective-permute-start | bytes 147464 | tf_op jit(solution)/shard_map/ppermute | solution.py:385
  6.9 6.9 %collective-permute-start.1 = (f32[3,32,128]{2,1,0:T(8,128)S(1)}, f32[3,32,128]{2,1,0:T(8,128)S(1)}, u32[]{:S(2)}, u32[]{:S(2)}) collective-permute-start(f32[3,32,128]{2,1,0:T(8,128)S(1)} %get-tuple-element.22.cols), channel_id=1, source_target_pairs={{16,0},{32,16},{48,32},{64,48},{80,64},{96,80},{112,96},{128,112},... | collective-permute-start | bytes 147464 | tf_op jit(solution)/shard_map/ppermute | solution.py:386
  14.0 19.1 %collective-permute-start.2 = (f32[12,32,128]{2,1,0:T(8,128)S(1)}, f32[12,32,128]{2,1,0:T(8,128)S(1)}, u32[]{:S(2)}, u32[]{:S(2)}) collective-permute-start(f32[12,32,128]{2,1,0:T(8,128)S(1)} %get-tuple-element.30), channel_id=1, source_target_pairs={{0,1},{1,2},{2,3},{3,4},{4,5},{5,6},{6,7},{7,8},{8,9},{9,10},{10,1... | collective-permute-start | bytes 589832 | tf_op jit(solution)/shard_map/ppermute | solution.py:403
  18.3 15.7 %collective-permute-start.3 = (f32[12,32,128]{2,1,0:T(8,128)S(1)}, f32[12,32,128]{2,1,0:T(8,128)S(1)}, u32[]{:S(2)}, u32[]{:S(2)}) collective-permute-start(f32[12,32,128]{2,1,0:T(8,128)S(1)} %get-tuple-element.31), channel_id=1, source_target_pairs={{1,0},{2,1},{3,2},{4,3},{5,4},{6,5},{7,6},{8,7},{9,8},{10,9},{11,1... | collective-permute-start | bytes 589832 | tf_op jit(solution)/shard_map/ppermute | solution.py:404
  35.3 21.2 %collective-permute-start.4 = (f32[160,512]{1,0:T(8,128)S(1)}, f32[160,512]{1,0:T(8,128)S(1)}, u32[]{:S(2)}, u32[]{:S(2)}) collective-permute-start(f32[160,512]{1,0:T(8,128)S(1)} %get-tuple-element.36), channel_id=1, source_target_pairs={{0,496},{16,480},{32,464},{48,448},{64,432},{80,416},{96,400},{112... | collective-permute-start | bytes 983048 | tf_op jit(solution)/shard_map/ppermute | solution.py:429

commit v3 on v2

--- a/solution.py
+++ b/solution.py
@@ -65,9 +65,13 @@
     return out
 
 
+def odd(axis):
+    return lax.rem(lax.axis_index(axis), 2) == 1
+
+
 def stage_kernel(
     motion, warmth, label, chart, receivers, donors, factors,
-    f, cols_out, up_out, down_out, receivers_out, donors_out, factors_out,
+    f, cols_out, first_out, second_out, receivers_out, donors_out, factors_out,
     lab, table, sems,
 ):
     small = [
@@ -83,54 +87,63 @@
         flow.append(pltpu.make_async_copy(motion.at[:, 0, :, r, :], f.at[0:4, r], sems.at[2, r]))
     for c in small[:1] + scalars + flow + small[1:]:
         c.start()
-    for c in small[:1] + scalars:
-        c.wait()
-
-    def stiffness(r, _):
-        kind = lab[r]
-        exponent = jnp.full(kind.shape, table[0], F32)
-        for entry in range(1, 8):
-            exponent = jnp.where(kind == entry, table[entry], exponent)
-        f[4, r] = jnp.exp(exponent + DIFFUSIVITY * (0.5 - f[5, r]))
-        return 0
-
-    lax.fori_loop(0, LAT, stiffness, 0, unroll=4)
-    for c in flow:
-        c.wait()
+    small[0].wait()
+
+    step = 4
+    for start in range(0, LAT, step):
+        for c in scalars[2 * start : 2 * (start + step)]:
+            c.wait()
+        for r in range(start, start + step):
+            kind = lab[r]
+            exponent = jnp.full(kind.shape, table[0], F32)
+            for entry in range(1, 8):
+                exponent = jnp.where(kind == entry, table[entry], exponent)
+            f[4, r] = jnp.exp(exponent + DIFFUSIVITY * (0.5 - f[5, r]))
 
     group = iota(1) >> 2
 
-    def pack(r, acc):
-        new = []
-        for q in range(3):
-            first = roll(f[2 * q, r], 4 * r + 2, 1)
-            second = roll(f[2 * q + 1, r], 4 * r + 66, 1)
-            new.append(jnp.where(group == r, first, jnp.where(group == r + 16, second, acc[q])))
-        return tuple(new)
-
-    zero = jnp.zeros((DEP, LON), F32)
-    packed = lax.fori_loop(0, LAT, pack, (zero, zero, zero), unroll=4)
+    def pack(q, r, acc):
+        first = roll(f[2 * q, r], 4 * r + 2, 1)
+        second = roll(f[2 * q + 1, r], 4 * r + 66, 1)
+        return jnp.where(group == r, first, jnp.where(group == r + 16, second, acc))
+
+    packed = [jnp.zeros((DEP, LON), F32) for _ in range(3)]
+    for start in range(0, LAT, step):
+        rows = range(start, start + step)
+        for r in rows:
+            packed[2] = pack(2, r, packed[2])
+        for c in flow[start : start + step]:
+            c.wait()
+        for r in rows:
+            packed[0] = pack(0, r, packed[0])
+            packed[1] = pack(1, r, packed[1])
     for q in range(3):
         cols_out[q] = packed[q]
-    for out, outer, inner in ((up_out, 14, 15), (down_out, 1, 0)):
+    is_odd = odd("lat")
+    for out, above in ((first_out, is_odd), (second_out, jnp.logical_not(is_odd))):
+        outer, inner = jnp.where(above, 14, 1), jnp.where(above, 15, 0)
         for k in range(5):
             out[k] = f[k, outer]
         for k in range(6):
             out[5 + k] = f[k, inner]
-        out[11] = zero
     for c in small[1:]:
         c.wait()
 
 
-def corners_kernel(left, right, up, down, _, up_out, down_out, cu, cd, sems):
-    lane = iota(1)
-    pos = lane & 3
-    group = (lane >> 2) & 15
-    pairs = [jnp.where(pos < 2, left[q], right[q]) for q in range(3)]
-    cu[...] = jnp.where(group == 15, pairs[0], jnp.where(group == 14, roll(pairs[1], 124, 1), roll(pairs[2], 120, 1)))
-    cd[...] = jnp.where(group == 0, pairs[0], jnp.where(group == 1, roll(pairs[1], 4, 1), roll(pairs[2], 8, 1)))
-    a = pltpu.make_async_copy(cu, up_out.at[11], sems.at[0])
-    b = pltpu.make_async_copy(cd, down_out.at[11], sems.at[1])
+def from_sides(first, second):
+    left_lanes = (iota(1) & 3) < 2
+    return [jnp.where(left_lanes == odd("lon"), second[q], first[q]) for q in range(3)]
+
+
+def corners_kernel(cols_first, cols_second, rows_first, rows_second, _, first_out, second_out, c1, c2, sems):
+    group = (iota(1) >> 2) & 15
+    pairs = from_sides(cols_first, cols_second)
+    up = jnp.where(group == 15, pairs[0], jnp.where(group == 14, roll(pairs[1], 124, 1), roll(pairs[2], 120, 1)))
+    down = jnp.where(group == 0, pairs[0], jnp.where(group == 1, roll(pairs[1], 4, 1), roll(pairs[2], 8, 1)))
+    c1[...] = jnp.where(odd("lat"), up, down)
+    c2[...] = jnp.where(odd("lat"), down, up)
+    a = pltpu.make_async_copy(c1, first_out.at[11], sems.at[0])
+    b = pltpu.make_async_copy(c2, second_out.at[11], sems.at[1])
     a.start()
     b.start()
     a.wait()
@@ -172,13 +185,14 @@
     lax.fori_loop(0, LAT, body, 0)
 
 
-def edge_columns(cols, left, right, corners):
+def edge_columns(cols, first, second, corners):
     lane = iota(1)
-    pos, group = lane & 3, lane >> 2
+    group = lane >> 2
+    sides = from_sides(first, second)
     halo, own = [], []
     for k in range(6):
         q, h = k // 2, k % 2
-        c = roll(jnp.where(pos < 2, left[q], right[q]), 4 + 64 * h, 1)
+        c = roll(sides[q], 4 + 64 * h, 1)
         low = high = 0.0
         if corners is not None:
             low = roll(corners[0], (68 + 64 * h + 4 * q) % 128, 1)
@@ -233,8 +247,8 @@
     lhs[(5 + k) * DEP : (6 + k) * DEP, at] = (value - top.astype(F32)).astype(BF16)
 
 
-def inner_kernel(f, cols, left, right, whi, wlo, mid_out, values_out, s1_out, faces_out, s1, faces, edge, lhs):
-    halo, own = edge_columns(cols, left, right, None)
+def inner_kernel(f, cols, cols_first, cols_second, whi, wlo, mid_out, values_out, s1_out, faces_out, s1, faces, edge, lhs):
+    halo, own = edge_columns(cols, cols_first, cols_second, None)
     for k in range(6):
         edge[k] = swap_middle(halo[k])
     for k, v in enumerate(relax_columns(halo, own)):
@@ -277,16 +291,19 @@
             faces_out[k, j] = faces[k, r]
 
 
-def rim_kernel(f, cols, left, right, south, north, s1_in, faces_in, partial, whi, wlo, rim_out, values_out, lhs):
-    halo, own = edge_columns(cols, left, right, (south[11], north[11]))
+def rim_kernel(f, cols, cols_first, cols_second, rows_first, rows_second, s1_in, faces_in, partial, whi, wlo, rim_out, values_out, lhs):
+    is_odd = odd("lat")
+    south = lambda i: jnp.where(is_odd, rows_second[i], rows_first[i])
+    north = lambda i: jnp.where(is_odd, rows_first[i], rows_second[i])
+    halo, own = edge_columns(cols, cols_first, cols_second, (south(11), north(11)))
     edge = [swap_middle(h) for h in halo]
     edge1 = [swap_middle(v) for v in relax_columns(halo, own)]
 
     def field(k, r):
         if r < 0:
-            return south[k] if r == -2 else south[5 + k]
+            return south(k if r == -2 else 5 + k)
         if r >= LAT:
-            return north[k] if r == LAT + 1 else north[5 + k]
+            return north(k if r == LAT + 1 else 5 + k)
         return f[k, r]
 
     s1, faces = {}, {}
@@ -326,16 +343,17 @@
     lhs[0:n] = top
     lhs[n : 2 * n] = (v - top.astype(F32)).astype(BF16)
     copies = []
-    for g in range(LAT // 2):
-        placed = jnp.dot(lhs[...], table[:, g * 256 : (g + 1) * 256], preferred_element_type=F32)
+    half = LAT // 2
+    for g in range(2):
+        placed = jnp.dot(lhs[...], table[:, g * half * LON : (g + 1) * half * LON], preferred_element_type=F32)
         merged = placed[:n] + placed[n : 2 * n]
-        for h in range(2):
-            r = 2 * g + h
-            at = slice(h * LON, (h + 1) * LON)
+        for h in range(half):
+            r = g * half + h
             hit = struck[0:1, r * LON : (r + 1) * LON] > 0.5
             for k in range(5):
                 kept = mid[k, r - 2] if 2 <= r < 14 else rim[k, r if r < 2 else r - 12]
-                out[k, r] = jnp.where(hit, merged[k * DEP : (k + 1) * DEP, at], kept)
+                out[k, r] = jnp.where(hit, merged[k * DEP : (k + 1) * DEP, h * LON : (h + 1) * LON], kept)
+        for r in range(g * half, (g + 1) * half):
             copies.append(pltpu.make_async_copy(out.at[0:4, r], flow_out.at[:, 0, :, r, :], sems.at[0, r]))
             copies.append(pltpu.make_async_copy(out.at[4, r], warmth_out.at[0, :, r, :], sems.at[1, r]))
             copies[-2].start()
@@ -369,7 +387,7 @@
     lon, lat = lax.axis_size("lon"), lax.axis_size("lat")
     n, slab = 5 * DEP, (DEP, LON)
 
-    f, cols, up, down, receivers, donors, factors = call(
+    f, cols, rows_first, rows_second, receivers, donors, factors = call(
         stage_kernel,
         [
             shape(6, LAT, *slab), shape(3, *slab), shape(12, *slab), shape(12, *slab),
@@ -380,10 +398,9 @@
         size=2 << 20,
     )(*map(in_hbm, (motion, warmth, label, chart, receivers.reshape(1, 512), donors.reshape(4, 512), factors.reshape(4, 512))))
 
-    ahead = lambda n: [(i, i + 1) for i in range(n - 1)]
-    back = lambda n: [(i + 1, i) for i in range(n - 1)]
-    left = lax.ppermute(cols, "lon", ahead(lon))
-    right = lax.ppermute(cols, "lon", back(lon))
+    swap = lambda n, start: [(i + j, i + 1 - j) for i in range(start, n - 1, 2) for j in range(2)]
+    cols_first = lax.ppermute(cols, "lon", swap(lon, 1))
+    cols_second = lax.ppermute(cols, "lon", swap(lon, 0))
     whi, wlo = call(
         weights_kernel,
         [shape(LAT * LON, 512, dtype=BF16), shape(LAT * LON, 512, dtype=BF16)],
@@ -391,7 +408,7 @@
         size=4 << 20,
         flops=20 << 20,
     )(donors, factors)
-    up, down = call(
+    rows_first, rows_second = call(
         corners_kernel,
         [shape(12, *slab), shape(12, *slab)],
         [VMEM, VMEM, ANY, ANY, ANY],
@@ -399,9 +416,9 @@
         out_specs=[ANY, ANY],
         aliases={2: 0, 3: 1},
         size=1 << 16,
-    )(left, right, up, down, whi)
-    south = lax.ppermute(up, "lat", ahead(lat))
-    north = lax.ppermute(down, "lat", back(lat))
+    )(cols_first, cols_second, rows_first, rows_second, whi)
+    rows_first = lax.ppermute(rows_first, "lat", swap(lat, 1))
+    rows_second = lax.ppermute(rows_second, "lat", swap(lat, 0))
 
     mid, partial, s1, faces = call(
         inner_kernel,
@@ -415,7 +432,7 @@
         ],
         size=8 << 20,
         flops=1 << 30,
-    )(f, cols, left, right, whi, wlo)
+    )(f, cols, cols_first, cols_second, whi, wlo)
     rim, values = call(
         rim_kernel,
         [shape(5, 4, *slab), shape(n, 512)],
@@ -423,7 +440,7 @@
         [pltpu.VMEM((2 * n, 4 * LON), BF16)],
         size=2 << 20,
         flops=1 << 28,
-    )(f, cols, left, right, south, north, s1, faces, partial, whi, wlo)
+    )(f, cols, cols_first, cols_second, rows_first, rows_second, s1, faces, partial, whi, wlo)
 
     mirror = [(p * lon + b, (1 - p) * lon + lon - 1 - b) for p in range(2) for b in range(lon)]
     incoming = lax.ppermute(values, ("panel", "lon"), mirror)

time: 60.7 us -> 58.3 us (0.960)
  starting transfers between devices: 28.3 us -> 23.3 us
  waiting for transfers between devices: 14.9 us -> 19.3 us
  Pallas kernels: 16.2 us -> 14.4 us
    ppermute x1, starting transfers between devices: 6.12 us -> 2.59 us  [shards(): incoming = lax.ppermute(values, ('panel', 'lon'), mirror)]
    ppermute x1, waiting for transfers between devices: 14 us -> 16.9 us  [shards(): incoming = lax.ppermute(values, ('panel', 'lon'), mirror)]
    ppermute x4, waiting for transfers between devices: 0.85 us -> 2.43 us  [the longest x1 1.71 us: shards(): cols_second = lax.ppermute(cols, 'lon', swap(lon, 0))]
    ppermute x4, starting transfers between devices: 22.2 us -> 20.7 us  [the longest x1 11.4 us: shards(): rows_first = lax.ppermute(rows_first, 'lat', swap(lat, 1))]
    pallas_call x1, Pallas kernels: 3.56 us -> 2.14 us  [shards(): call(place_kernel, [shape(4, 1, DEP, LAT, LON), shape(1, DEP, LAT, LON)],...]
  transfers between devices with their start and end apart: 5 -> 5, of which waited for: 2 -> 4; matrix products, arithmetic and copies ran while one was open for 0% -> 0% of each run, Pallas kernels for 14% -> 14%
where the time goes in v3:
time: 58.3 us; the launch traced here: 57.8 us
  starting transfers between devices  23.3 us (40%)
  waiting for transfers between devices  19.3 us (33%)
  Pallas kernels  14.4 us (25%)
  between operations  0.73 us (1%)
    ppermute x1, waiting for transfers between devices, shards(): incoming = lax.ppermute(values, ('panel', 'lon'), mirror)  16.9 us
    ppermute x1, starting transfers between devices, shards(): rows_first = lax.ppermute(rows_first, 'lat', swap(lat, 1))  11.4 us
    ppermute x1, starting transfers between devices, shards(): cols_first = lax.ppermute(cols, 'lon', swap(lon, 1))  5.45 us
    pallas_call x1, Pallas kernels, shards(): call(inner_kernel, [shape(5, 12, *slab), shape(n, 512), shape(4, 4, *slab...  4.91 us
    ppermute x1, starting transfers between devices, shards(): incoming = lax.ppermute(values, ('panel', 'lon'), mirror)  2.59 us
    pallas_call x1, Pallas kernels, shards(): call(stage_kernel, [shape(6, LAT, *slab), shape(3, *slab), shape(12, *sla...  2.49 us
    pallas_call x1, Pallas kernels, shards(): call(weights_kernel, [shape(LAT * LON, 512, dtype=BF16), shape(LAT * LON,...  2.33 us
    pallas_call x1, Pallas kernels, shards(): call(place_kernel, [shape(4, 1, DEP, LAT, LON), shape(1, DEP, LAT, LON)],...  2.14 us
  transfers between devices with their start and end apart: 5, of which 4 were waited for; matrix products, arithmetic and copies ran while one was open for 0% of the time, Pallas kernels for 14%

profile of v3, /device:TPU:48, one launch (start us, length us, event | category | flops | bytes accessed | tf_op | source)
XLA Modules:
  0.0 57.8 jit_solution(3424382147698713325)
XLA Ops:
  0.6 2.5 %shard_map.86 = (f32[6,16,32,128]{3,2,1,0:T(8,128)S(1)}, f32[3,32,128]{2,1,0:T(8,128)S(1)}, f32[12,32,128]{2,1,0:T(8,128)S(1)}, f32[12,32,128]{2,1,0:T(8,128)S(1...) custom-call(f32[4,1,32,16,128]{4,3,2,1,0:T(8,128)} %motion.1, f32[1,32,16,128]{3,2,1,0:T(8,128)} %warmth.1, ...), custom_call_target="tpu_custom_call" | custom-call | bytes 2097152 | tf_op jit(solution)/shard_map/pallas_call | solution.py:390
  3.1 5.5 %collective-permute-start = (f32[3,32,128]{2,1,0:T(8,128)S(1)}, f32[3,32,128]{2,1,0:T(8,128)S(1)}, u32[]{:S(2)}, u32[]{:S(2)}) collective-permute-start(f32[3,32,128]{2,1,0:T(8,128)S(1)} %get-tuple-element.22.cols), channel_id=1, source_target_pairs={{16,32},{32,16},{48,64},{64,48},{80,96},{96,80},{112,128},{128,112... | collective-permute-start | bytes 147464 | tf_op jit(solution)/shard_map/ppermute | solution.py:402
  8.6 1.9 %collective-permute-start.1 = (f32[3,32,128]{2,1,0:T(8,128)S(1)}, f32[3,32,128]{2,1,0:T(8,128)S(1)}, u32[]{:S(2)}, u32[]{:S(2)}) collective-permute-start(f32[3,32,128]{2,1,0:T(8,128)S(1)} %get-tuple-element.22.cols), channel_id=1, source_target_pairs={{0,16},{16,0},{32,48},{48,32},{64,80},{80,64},{96,112},{112,96},{1... | collective-permute-start | bytes 147464 | tf_op jit(solution)/shard_map/ppermute | solution.py:403
  10.5 2.3 %shard_map.87 = (bf16[2048,512]{1,0:T(8,128)(2,1)S(1)}, bf16[2048,512]{1,0:T(8,128)(2,1)S(1)}) custom-call(s32[4,512]{1,0:T(4,128)S(1)} %get-tuple-element.23.donors, f32[4,512]{1,0:T(4,128)S(1)} %get-tuple-element.24.factors), custom_call_target="tpu_custom_call" | custom-call | flops 20971520 | bytes 4194304 | tf_op jit(solution)/shard_map/pallas_call | solution.py:404
  12.9 0.0 collective-permute-done.cols_first
  12.9 1.7 %collective-permute-done.1.cols_second = f32[3,32,128]{2,1,0:T(8,128)S(1)} collective-permute-done((f32[3,32,128]{2,1,0:T(8,128)S(1)}, f32[3,32,128]{2,1,0:T(8,128)S(1)}, u32[]{:S(2)}, u32[]{:S(2)}) %collective-permute-start.1) | collective-permute-done | bytes 49184 | tf_op jit(solution)/shard_map/ppermute | solution.py:403
  14.6 0.1 shard_map.89
  14.7 11.4 %collective-permute-start.2 = (f32[12,32,128]{2,1,0:T(8,128)S(1)}, f32[12,32,128]{2,1,0:T(8,128)S(1)}, u32[]{:S(2)}, u32[]{:S(2)}) collective-permute-start(f32[12,32,128]{2,1,0:T(8,128)S(1)} %get-tuple-element.30), channel_id=1, source_target_pairs={{1,2},{2,1},{3,4},{4,3},{5,6},{6,5},{7,8},{8,7},{9,10},{10,9},{11,... | collective-permute-start | bytes 589832 | tf_op jit(solution)/shard_map/ppermute | solution.py:420
  26.1 1.9 %collective-permute-start.3 = (f32[12,32,128]{2,1,0:T(8,128)S(1)}, f32[12,32,128]{2,1,0:T(8,128)S(1)}, u32[]{:S(2)}, u32[]{:S(2)}) collective-permute-start(f32[12,32,128]{2,1,0:T(8,128)S(1)} %get-tuple-element.31), channel_id=1, source_target_pairs={{0,1},{1,0},{2,3},{3,2},{4,5},{5,4},{6,7},{7,6},{8,9},{9,8},{10,11... | collective-permute-start | bytes 589832 | tf_op jit(solution)/shard_map/ppermute | solution.py:421
  28.1 4.9 %shard_map.88 = (f32[5,12,32,128]{3,2,1,0:T(8,128)S(1)}, f32[160,512]{1,0:T(8,128)S(1)}, f32[4,4,32,128]{3,2,1,0:T(8,128)S(1)}, f32[5,2,32,128]{3,2,1,0:T(8,128)S(1)}) custom-call(f32[6,16,32,128]{3,2,1,0:T(8,128)S(1)} %get-tuple-element.21.f, f32[3,32,128]{2,1,0:T(8,128)S(1)} %get-tuple-element.22.cols, f32[3,32,128]{2,1,0:T(8,128)S(1)} %collective-permute-done.cols_first, ...), custom_call_target="tpu_custom_call" | custom-call | flops 1073741824 | bytes 8388608 | tf_op jit(solution)/shard_map/pallas_call | solution.py:423
  33.0 0.1 collective-permute-done.2.rows_first
  33.1 0.6 %collective-permute-done.3.rows_second = f32[12,32,128]{2,1,0:T(8,128)S(1)} collective-permute-done((f32[12,32,128]{2,1,0:T(8,128)S(1)}, f32[12,32,128]{2,1,0:T(8,128)S(1)}, u32[]{:S(2)}, u32[]{:S(2)}) %collective-permute-start.3) | collective-permute-done | bytes 196640 | tf_op jit(solution)/shard_map/ppermute | solution.py:421
  33.7 1.3 %shard_map.90 = (f32[5,4,32,128]{3,2,1,0:T(8,128)S(1)}, f32[160,512]{1,0:T(8,128)S(1)}) custom-call(f32[6,16,32,128]{3,2,1,0:T(8,128)S(1)} %get-tuple-element.21.f, f32[3,32,128]{2,1,0:T(8,128)S(1)} %get-tuple-element.22.cols, f32[3,32,128]{2,1,0:T(8,128)S(1)} %collective-permute-done.cols_first, f32[3,32,128]{2,1,0:T(8,128)S(1)} %collective-permute-done.1.cols_second, ...), custom_call_target="tpu_custom_call" | custom-call | flops 268435456 | bytes 2097152 | tf_op jit(solution)/shard_map/pallas_call | solution.py:436
  35.0 2.6 %collective-permute-start.4 = (f32[160,512]{1,0:T(8,128)S(1)}, f32[160,512]{1,0:T(8,128)S(1)}, u32[]{:S(2)}, u32[]{:S(2)}) collective-permute-start(f32[160,512]{1,0:T(8,128)S(1)} %get-tuple-element.36), channel_id=1, source_target_pairs={{0,496},{16,480},{32,464},{48,448},{64,432},{80,416},{96,400},{112... | collective-permute-start | bytes 983048 | tf_op jit(solution)/shard_map/ppermute | solution.py:446
  37.6 1.1 %shard_map.91 = (bf16[512,2048]{1,0:T(8,128)(2,1)S(1)}, f32[8,2048]{1,0:T(8,128)S(1)}) custom-call(s32[1,512]{1,0:T(1,128)S(1)} %get-tuple-element.37.receivers), custom_call_target="tpu_custom_call" | custom-call | flops 4194304 | bytes 2097152 | tf_op jit(solution)/shard_map/pallas_call | solution.py:448
  38.7 16.9 %collective-permute-done.4.values = f32[160,512]{1,0:T(8,128)S(1)} collective-permute-done((f32[160,512]{1,0:T(8,128)S(1)}, f32[160,512]{1,0:T(8,128)S(1)}, u32[]{:S(2)}, u32[]{:S(2)}) %collective-permute-start.4) | collective-permute-done | bytes 327712 | tf_op jit(solution)/shard_map/ppermute | solution.py:446
  55.6 2.1 %shard_map.92 = (f32[4,1,32,16,128]{4,3,2,1,0:T(8,128)}, f32[1,32,16,128]{3,2,1,0:T(8,128)}) custom-call(f32[5,12,32,128]{3,2,1,0:T(8,128)S(1)} %get-tuple-element.27.mid, f32[5,4,32,128]{3,2,1,0:T(8,128)S(1)} %get-tuple-element.35.rim, f32[160,512]{1,0:T(8,128)S(1)} %collective-permute-done.4.values, bf16[512,2048]{1,0:T(8,128)(2,1)S(1)} %get-tuple-element.38.table, ...), custom_call_target="tpu_custom_call" | custom-call | flops 1073741824 | bytes 8388608 | tf_op jit(solution)/shard_map/pallas_call | solution.py:456
Async XLA Ops:
  3.1 9.7 %collective-permute-start = (f32[3,32,128]{2,1,0:T(8,128)S(1)}, f32[3,32,128]{2,1,0:T(8,128)S(1)}, u32[]{:S(2)}, u32[]{:S(2)}) collective-permute-start(f32[3,32,128]{2,1,0:T(8,128)S(1)} %get-tuple-element.22.cols), channel_id=1, source_target_pairs={{16,32},{32,16},{48,64},{64,48},{80,96},{96,80},{112,128},{128,112... | collective-permute-start | bytes 147464 | tf_op jit(solution)/shard_map/ppermute | solution.py:402
  8.6 6.0 %collective-permute-start.1 = (f32[3,32,128]{2,1,0:T(8,128)S(1)}, f32[3,32,128]{2,1,0:T(8,128)S(1)}, u32[]{:S(2)}, u32[]{:S(2)}) collective-permute-start(f32[3,32,128]{2,1,0:T(8,128)S(1)} %get-tuple-element.22.cols), channel_id=1, source_target_pairs={{0,16},{16,0},{32,48},{48,32},{64,80},{80,64},{96,112},{112,96},{1... | collective-permute-start | bytes 147464 | tf_op jit(solution)/shard_map/ppermute | solution.py:403
  14.7 18.3 %collective-permute-start.2 = (f32[12,32,128]{2,1,0:T(8,128)S(1)}, f32[12,32,128]{2,1,0:T(8,128)S(1)}, u32[]{:S(2)}, u32[]{:S(2)}) collective-permute-start(f32[12,32,128]{2,1,0:T(8,128)S(1)} %get-tuple-element.30), channel_id=1, source_target_pairs={{1,2},{2,1},{3,4},{4,3},{5,6},{6,5},{7,8},{8,7},{9,10},{10,9},{11,... | collective-permute-start | bytes 589832 | tf_op jit(solution)/shard_map/ppermute | solution.py:420
  26.1 7.6 %collective-permute-start.3 = (f32[12,32,128]{2,1,0:T(8,128)S(1)}, f32[12,32,128]{2,1,0:T(8,128)S(1)}, u32[]{:S(2)}, u32[]{:S(2)}) collective-permute-start(f32[12,32,128]{2,1,0:T(8,128)S(1)} %get-tuple-element.31), channel_id=1, source_target_pairs={{0,1},{1,0},{2,3},{3,2},{4,5},{5,4},{6,7},{7,6},{8,9},{9,8},{10,11... | collective-permute-start | bytes 589832 | tf_op jit(solution)/shard_map/ppermute | solution.py:421
  35.0 20.6 %collective-permute-start.4 = (f32[160,512]{1,0:T(8,128)S(1)}, f32[160,512]{1,0:T(8,128)S(1)}, u32[]{:S(2)}, u32[]{:S(2)}) collective-permute-start(f32[160,512]{1,0:T(8,128)S(1)} %get-tuple-element.36), channel_id=1, source_target_pairs={{0,496},{16,480},{32,464},{48,448},{64,432},{80,416},{96,400},{112... | collective-permute-start | bytes 983048 | tf_op jit(solution)/shard_map/ppermute | solution.py:446

commit v4 on v3

--- a/solution.py
+++ b/solution.py
@@ -35,8 +35,11 @@
 
 
 def lon_pair(x, edge, r):
+    return beside(x, roll(edge, 122 - 4 * r, 1))
+
+
+def beside(x, halo):
     lane = iota(1, x.shape)
-    halo = roll(edge, 122 - 4 * r, 1)
     lower = jnp.where(lane == 0, halo, roll(x, 1, 1))
     upper = jnp.where(lane == LON - 1, halo, roll(x, LON - 1, 1))
     return lower, upper
@@ -69,9 +72,18 @@
     return lax.rem(lax.axis_index(axis), 2) == 1
 
 
+def middle_of(lon):
+    return range(lon // 4, lon - lon // 4)
+
+
+def first_above():
+    b, middle = lax.axis_index("lon"), middle_of(lax.axis_size("lon"))
+    return odd("lat") == jnp.logical_and(b >= middle.start, b < middle.stop)
+
+
 def stage_kernel(
     motion, warmth, label, chart, receivers, donors, factors,
-    f, cols_out, first_out, second_out, receivers_out, donors_out, factors_out,
+    f, cols_out, side_first_out, side_second_out, first_out, second_out, receivers_out, donors_out, factors_out,
     lab, table, sems,
 ):
     small = [
@@ -119,31 +131,73 @@
             packed[1] = pack(1, r, packed[1])
     for q in range(3):
         cols_out[q] = packed[q]
-    is_odd = odd("lat")
-    for out, above in ((first_out, is_odd), (second_out, jnp.logical_not(is_odd))):
+    to_right, to_left = side_columns(packed, 0), side_columns(packed, 2)
+    for i in range(2):
+        rows = slice(0, DEP) if i == 0 else slice(DEP, DEP + DEP // 2)
+        side_first_out[rows] = jnp.where(odd("lon"), to_right[i], to_left[i])
+        side_second_out[rows] = jnp.where(odd("lon"), to_left[i], to_right[i])
+    is_above = first_above()
+    for out, above in ((first_out, is_above), (second_out, jnp.logical_not(is_above))):
         outer, inner = jnp.where(above, 14, 1), jnp.where(above, 15, 0)
         for k in range(5):
-            out[k] = f[k, outer]
+            out[block(k)] = f[k, outer]
         for k in range(6):
-            out[5 + k] = f[k, inner]
+            out[block(5 + k)] = f[k, inner]
     for c in small[1:]:
         c.wait()
 
 
+def block(i):
+    return slice(i * DEP, (i + 1) * DEP)
+
+
+def side_columns(packed, start):
+    low_lanes = (iota(1) & 3) < 2
+    low = [roll(p, (LON - start) % LON, 1) if start else p for p in packed]
+    high = [roll(p, (2 - start) % LON, 1) if start != 2 else p for p in packed]
+    half = DEP // 2
+    return jnp.where(low_lanes, low[0], high[1]), jnp.where(low_lanes[:half], low[2][:half], high[2][half:])
+
+
+def by_side(first, second):
+    is_odd = odd("lon")
+    return jnp.where(is_odd, second[...], first[...]), jnp.where(is_odd, first[...], second[...])
+
+
 def from_sides(first, second):
     left_lanes = (iota(1) & 3) < 2
-    return [jnp.where(left_lanes == odd("lon"), second[q], first[q]) for q in range(3)]
+    left, right = by_side(first, second)
+    l01, l2, r01, r2 = left[:DEP], left[DEP:], right[:DEP], right[DEP:]
+    lefts = (l01, roll(l01, LON - 2, 1), jnp.concatenate([l2, roll(l2, LON - 2, 1)], axis=0))
+    rights = (roll(r01, 2, 1), r01, jnp.concatenate([roll(r2, 2, 1), r2], axis=0))
+    return [jnp.where(left_lanes, a, b) for a, b in zip(lefts, rights)]
+
+
+CORNERS = slice(11 * DEP, 11 * DEP + 8)
 
 
 def corners_kernel(cols_first, cols_second, rows_first, rows_second, _, first_out, second_out, c1, c2, sems):
-    group = (iota(1) >> 2) & 15
-    pairs = from_sides(cols_first, cols_second)
-    up = jnp.where(group == 15, pairs[0], jnp.where(group == 14, roll(pairs[1], 124, 1), roll(pairs[2], 120, 1)))
-    down = jnp.where(group == 0, pairs[0], jnp.where(group == 1, roll(pairs[1], 4, 1), roll(pairs[2], 8, 1)))
-    c1[...] = jnp.where(odd("lat"), up, down)
-    c2[...] = jnp.where(odd("lat"), down, up)
-    a = pltpu.make_async_copy(c1, first_out.at[11], sems.at[0])
-    b = pltpu.make_async_copy(c2, second_out.at[11], sems.at[1])
+    lane = iota(1, (8, LON))
+    left_lanes, group = (lane & 3) < 2, (lane >> 2) & 15
+    left, right = by_side(cols_first, cols_second)
+    up = down = jnp.zeros((8, LON), F32)
+    for j in range(4):
+        for q in range(3):
+            if q < 2:
+                rows, from_left, from_right = slice(8 * j, 8 * j + 8), (0, -2)[q], (2, 0)[q]
+            else:
+                start = DEP + 8 * (j % 2)
+                rows, from_left, from_right = slice(start, start + 8), (0, -2)[j // 2], (2, 0)[j // 2]
+            move = 4 * q + 16 * j
+            put = lambda x, shift: roll(x[rows], shift % LON, 1) if shift % LON else x[rows]
+            to_up = jnp.where(left_lanes, put(left, from_left - move), put(right, from_right - move))
+            to_down = jnp.where(left_lanes, put(left, from_left + move), put(right, from_right + move))
+            up = jnp.where(group == 15 - q - 4 * j, to_up, up)
+            down = jnp.where(group == q + 4 * j, to_down, down)
+    c1[...] = jnp.where(first_above(), up, down)
+    c2[...] = jnp.where(first_above(), down, up)
+    a = pltpu.make_async_copy(c1, first_out.at[CORNERS], sems.at[0])
+    b = pltpu.make_async_copy(c2, second_out.at[CORNERS], sems.at[1])
     a.start()
     b.start()
     a.wait()
@@ -185,21 +239,23 @@
     lax.fori_loop(0, LAT, body, 0)
 
 
-def edge_columns(cols, first, second, corners):
-    lane = iota(1)
-    group = lane >> 2
+def edge_columns(cols, first, second):
     sides = from_sides(first, second)
     halo, own = [], []
     for k in range(6):
         q, h = k // 2, k % 2
-        c = roll(sides[q], 4 + 64 * h, 1)
-        low = high = 0.0
-        if corners is not None:
-            low = roll(corners[0], (68 + 64 * h + 4 * q) % 128, 1)
-            high = roll(corners[1], (68 + 64 * h - 4 * q) % 128, 1)
-        halo.append(jnp.where(group == 0, low, jnp.where(group == 17, high, c)))
+        halo.append(roll(sides[q], 4 + 64 * h, 1))
         own.append(roll(cols[q], 4 + 64 * h, 1))
     return halo, own
+
+
+def corner_columns(packed, k, up, lane):
+    q, h = k // 2, k % 2
+    parts = []
+    for j in range(4):
+        start = 64 * h + (60 - 4 * q - 16 * j if up else 4 * q + 16 * j)
+        parts.append(roll(packed, (lane - start) % LON, 1))
+    return jnp.concatenate(parts, axis=0)
 
 
 def relax_columns(halo, own):
@@ -247,10 +303,11 @@
     lhs[(5 + k) * DEP : (6 + k) * DEP, at] = (value - top.astype(F32)).astype(BF16)
 
 
-def inner_kernel(f, cols, cols_first, cols_second, whi, wlo, mid_out, values_out, s1_out, faces_out, s1, faces, edge, lhs):
-    halo, own = edge_columns(cols, cols_first, cols_second, None)
+def inner_kernel(f, cols, cols_first, cols_second, whi, wlo, mid_out, values_out, s1_out, faces_out, edges_out, s1, faces, edge, lhs):
+    halo, own = edge_columns(cols, cols_first, cols_second)
     for k in range(6):
         edge[k] = swap_middle(halo[k])
+        edges_out[k], edges_out[6 + k], edges_out[12 + k] = halo[k], own[k], edge[k]
     for k, v in enumerate(relax_columns(halo, own)):
         edge[6 + k] = swap_middle(v)
 
@@ -265,7 +322,7 @@
             s1[k, r] = v
         return 0
 
-    lax.fori_loop(1, LAT - 1, first, 0)
+    lax.fori_loop(1, LAT - 1, first, 0, unroll=2)
 
     def second(r, _):
         eta = f[4, r]
@@ -281,7 +338,7 @@
             put_split(lhs, k, at, new[k])
         return 0
 
-    lax.fori_loop(2, LAT - 2, second, 0)
+    lax.fori_loop(2, LAT - 2, second, 0, unroll=2)
     values_out[...] = blend(lhs[...], whi[2 * LON : 14 * LON], wlo[2 * LON : 14 * LON])
     for k in range(4):
         for j, r in enumerate((1, 2, 13, 14)):
@@ -291,33 +348,47 @@
             faces_out[k, j] = faces[k, r]
 
 
-def rim_kernel(f, cols, cols_first, cols_second, rows_first, rows_second, s1_in, faces_in, partial, whi, wlo, rim_out, values_out, lhs):
-    is_odd = odd("lat")
-    south = lambda i: jnp.where(is_odd, rows_second[i], rows_first[i])
-    north = lambda i: jnp.where(is_odd, rows_first[i], rows_second[i])
-    halo, own = edge_columns(cols, cols_first, cols_second, (south(11), north(11)))
-    edge = [swap_middle(h) for h in halo]
-    edge1 = [swap_middle(v) for v in relax_columns(halo, own)]
+def rim_kernel(f, edges, rows_first, rows_second, s1_in, faces_in, partial, whi, wlo, rim_out, values_out, lhs):
+    is_above = first_above()
+    south = lambda at: jnp.where(is_above, rows_second[at], rows_first[at])
+    north = lambda at: jnp.where(is_above, rows_first[at], rows_second[at])
+    low, high = south(CORNERS), north(CORNERS)
+    group = iota(1) >> 2
+    halo = []
+    for k in range(6):
+        c = edges[k]
+        if k < 5:
+            c = jnp.where(group == 0, corner_columns(low, k, True, 0), jnp.where(group == LAT + 1, corner_columns(high, k, False, 4 * LAT + 4), c))
+        halo.append(c)
+    edge1 = [swap_middle(v) for v in relax_columns(halo, [edges[6 + k] for k in range(6)])]
+    low_edge, high_edge = swap_middle(low), swap_middle(high)
+
+    def edge(k, r):
+        if r < 0:
+            return corner_columns(low_edge, k, True, LON - 2)
+        if r >= LAT:
+            return corner_columns(high_edge, k, False, LON - 2)
+        return roll(edges[12 + k], 122 - 4 * r, 1)
 
     def field(k, r):
         if r < 0:
-            return south(k if r == -2 else 5 + k)
+            return south(block(k if r == -2 else 5 + k))
         if r >= LAT:
-            return north(k if r == LAT + 1 else 5 + k)
+            return north(block(k if r == LAT + 1 else 5 + k))
         return f[k, r]
 
     s1, faces = {}, {}
     for j, r in enumerate((1, 2, 13, 14)):
         s1[r] = [s1_in[k, j] for k in range(4)]
     for j, r in enumerate((1, 14)):
-        low, high, left_face, right_face, scale = (faces_in[k, j] for k in range(5))
+        below, above, left_face, right_face, scale = (faces_in[k, j] for k in range(5))
         eta = f[4, r]
-        faces[r] = (((low, high), (eta + f[4, r - 1], eta + f[4, r + 1]), (left_face, right_face)), scale)
+        faces[r] = (((below, above), (eta + f[4, r - 1], eta + f[4, r + 1]), (left_face, right_face)), scale)
     for r in (-1, 0, LAT - 1, LAT):
         eta = field(4, r)
-        faces[r] = faces_of(eta, (depth_pair(eta), (field(4, r - 1), field(4, r + 1)), lon_pair(eta, edge[4], r)))
+        faces[r] = faces_of(eta, (depth_pair(eta), (field(4, r - 1), field(4, r + 1)), beside(eta, edge(4, r))))
         centre = [field(k, r) for k in range(4)]
-        pairs = [(depth_pair(centre[k]), (field(k, r - 1), field(k, r + 1)), lon_pair(centre[k], edge[k], r)) for k in range(4)]
+        pairs = [(depth_pair(centre[k]), (field(k, r - 1), field(k, r + 1)), beside(centre[k], edge(k, r))) for k in range(4)]
         s1[r] = relax(centre, pairs, *faces[r], eta, field(5, r))
         if r < 0 or r >= LAT:
             s1[r] = [jnp.where(eta > 0.0, v, 0.0) for v in s1[r]]
@@ -326,7 +397,7 @@
         pairs = [(depth_pair(centre[k]), (s1[r - 1][k], s1[r + 1][k]), lon_pair(centre[k], edge1[k], r)) for k in range(4)]
         t = f[5, r]
         new = relax(centre, pairs, *faces[r], f[4, r], t)
-        new.append(advance(t, (depth_pair(t), (field(5, r - 1), field(5, r + 1)), lon_pair(t, edge[5], r)), new))
+        new.append(advance(t, (depth_pair(t), (field(5, r - 1), field(5, r + 1)), beside(t, edge(5, r))), new))
         for k in range(5):
             rim_out[k, j] = new[k]
             put_split(lhs, k, slice(j * LON, (j + 1) * LON), new[k])
@@ -387,10 +458,11 @@
     lon, lat = lax.axis_size("lon"), lax.axis_size("lat")
     n, slab = 5 * DEP, (DEP, LON)
 
-    f, cols, rows_first, rows_second, receivers, donors, factors = call(
+    sides, rows = shape(DEP + DEP // 2, LON), shape(11 * DEP + 8, LON)
+    f, cols, side_first, side_second, rows_first, rows_second, receivers, donors, factors = call(
         stage_kernel,
         [
-            shape(6, LAT, *slab), shape(3, *slab), shape(12, *slab), shape(12, *slab),
+            shape(6, LAT, *slab), shape(3, *slab), sides, sides, rows, rows,
             shape(1, 512, dtype=jnp.int32), shape(4, 512, dtype=jnp.int32), shape(4, 512),
         ],
         [HBM] * 7,
@@ -399,8 +471,8 @@
     )(*map(in_hbm, (motion, warmth, label, chart, receivers.reshape(1, 512), donors.reshape(4, 512), factors.reshape(4, 512))))
 
     swap = lambda n, start: [(i + j, i + 1 - j) for i in range(start, n - 1, 2) for j in range(2)]
-    cols_first = lax.ppermute(cols, "lon", swap(lon, 1))
-    cols_second = lax.ppermute(cols, "lon", swap(lon, 0))
+    cols_first = lax.ppermute(side_first, "lon", swap(lon, 1))
+    cols_second = lax.ppermute(side_second, "lon", swap(lon, 0))
     whi, wlo = call(
         weights_kernel,
         [shape(LAT * LON, 512, dtype=BF16), shape(LAT * LON, 512, dtype=BF16)],
@@ -410,19 +482,23 @@
     )(donors, factors)
     rows_first, rows_second = call(
         corners_kernel,
-        [shape(12, *slab), shape(12, *slab)],
+        [rows, rows],
         [VMEM, VMEM, ANY, ANY, ANY],
-        [pltpu.VMEM(slab, F32), pltpu.VMEM(slab, F32), pltpu.SemaphoreType.DMA((2,))],
+        [pltpu.VMEM((8, LON), F32), pltpu.VMEM((8, LON), F32), pltpu.SemaphoreType.DMA((2,))],
         out_specs=[ANY, ANY],
         aliases={2: 0, 3: 1},
         size=1 << 16,
     )(cols_first, cols_second, rows_first, rows_second, whi)
-    rows_first = lax.ppermute(rows_first, "lat", swap(lat, 1))
-    rows_second = lax.ppermute(rows_second, "lat", swap(lat, 0))
-
-    mid, partial, s1, faces = call(
+    middle = middle_of(lon)
+    outer = [b for b in range(lon) if b not in middle]
+    among = lambda ones, start: [(b * lat + i, b * lat + j) for b in ones for i, j in swap(lat, start)]
+    axes = ("lon", "lat")
+    rows_in_first = lax.ppermute(rows_first, axes, among(middle, 1) + among(outer, 0))
+    rows_in_second = lax.ppermute(rows_second, axes, among(middle, 0) + among(outer, 1))
+
+    mid, partial, s1, faces, edges = call(
         inner_kernel,
-        [shape(5, 12, *slab), shape(n, 512), shape(4, 4, *slab), shape(5, 2, *slab)],
+        [shape(5, 12, *slab), shape(n, 512), shape(4, 4, *slab), shape(5, 2, *slab), shape(18, *slab)],
         [VMEM] * 6,
         [
             pltpu.VMEM((4, LAT) + slab, F32),
@@ -436,11 +512,11 @@
     rim, values = call(
         rim_kernel,
         [shape(5, 4, *slab), shape(n, 512)],
-        [VMEM] * 11,
+        [VMEM] * 9,
         [pltpu.VMEM((2 * n, 4 * LON), BF16)],
         size=2 << 20,
         flops=1 << 28,
-    )(f, cols, cols_first, cols_second, rows_first, rows_second, s1, faces, partial, whi, wlo)
+    )(f, edges, rows_in_first, rows_in_second, s1, faces, partial, whi, wlo)
 
     mirror = [(p * lon + b, (1 - p) * lon + lon - 1 - b) for p in range(2) for b in range(lon)]
     incoming = lax.ppermute(values, ("panel", "lon"), mirror)

time: 58.3 us -> 56.2 us (0.964)
  starting transfers between devices: 23.3 us -> 22.6 us
  Pallas kernels: 14.4 us -> 13.8 us
    ppermute x1, waiting for transfers between devices: 16.9 us -> 16 us  [shards(): incoming = lax.ppermute(values, ('panel', 'lon'), mirror)]
    pallas_call x1, Pallas kernels: 4.91 us -> 4.16 us  [shards(): call(inner_kernel, [shape(5, 12, *slab), shape(n, 512), shape(4, 4, *slab...]
    ppermute x1, starting transfers between devices: 2.59 us -> 1.92 us  [shards(): incoming = lax.ppermute(values, ('panel', 'lon'), mirror)]
  transfers between devices with their start and end apart: 5 -> 5, of which waited for: 4 -> 3; matrix products, arithmetic and copies ran while one was open for 0% -> 0% of each run, Pallas kernels for 14% -> 13%
where the time goes in v4:
time: 56.2 us; the launch traced here: 55.9 us
  starting transfers between devices  22.6 us (40%)
  waiting for transfers between devices  18.8 us (33%)
  Pallas kernels  13.8 us (25%)
  between operations  0.73 us (1%)
    ppermute x1, waiting for transfers between devices, shards(): incoming = lax.ppermute(values, ('panel', 'lon'), mirror)  16 us
    ppermute x1, starting transfers between devices, shards(): lax.ppermute(rows_first, axes, among(middle, 1) + among(outer, 0))  11.4 us
    ppermute x1, starting transfers between devices, shards(): cols_first = lax.ppermute(side_first, 'lon', swap(lon, 1))  5.45 us
    pallas_call x1, Pallas kernels, shards(): call(inner_kernel, [shape(5, 12, *slab), shape(n, 512), shape(4, 4, *slab...  4.16 us
    pallas_call x1, Pallas kernels, shards(): call(stage_kernel, [shape(6, LAT, *slab), shape(3, *slab), sides, sides,...  2.56 us
    pallas_call x1, Pallas kernels, shards(): call(weights_kernel, [shape(LAT * LON, 512, dtype=BF16), shape(LAT * LON,...  2.33 us
    pallas_call x1, Pallas kernels, shards(): call(place_kernel, [shape(4, 1, DEP, LAT, LON), shape(1, DEP, LAT, LON)],...  2.14 us
    ppermute x1, starting transfers between devices, shards(): cols_second = lax.ppermute(side_second, 'lon', swap(lon, 0))  1.92 us
  transfers between devices with their start and end apart: 5, of which 3 were waited for; matrix products, arithmetic and copies ran while one was open for 0% of the time, Pallas kernels for 13%

profile of v4, /device:TPU:48, one launch (start us, length us, event | category | flops | bytes accessed | tf_op | source)
XLA Modules:
  0.0 55.9 jit_solution(11480593252494079634)
XLA Ops:
  0.6 2.6 %shard_map.86 = (f32[6,16,32,128]{3,2,1,0:T(8,128)S(1)}, f32[3,32,128]{2,1,0:T(8,128)S(1)}, f32[48,128]{1,0:T(8,128)S(1)}, f32[48,128]{1,0:T(8,128)S(1)}, f32[36...) custom-call(f32[4,1,32,16,128]{4,3,2,1,0:T(8,128)} %motion.1, ...), custom_call_target="tpu_custom_call" | custom-call | bytes 2097152 | tf_op jit(solution)/shard_map/pallas_call | solution.py:462
  3.2 5.5 %collective-permute-start = (f32[48,128]{1,0:T(8,128)S(1)}, f32[48,128]{1,0:T(8,128)S(1)}, u32[]{:S(2)}, u32[]{:S(2)}) collective-permute-start(f32[48,128]{1,0:T(8,128)S(1)} %get-tuple-element.26), channel_id=1, source_target_pairs={{16,32},{32,16},{48,64},{64,48},{80,96},{96,80},{112,128},{128,112... | collective-permute-start | bytes 73736 | tf_op jit(solution)/shard_map/ppermute | solution.py:474
  8.7 1.9 %collective-permute-start.1 = (f32[48,128]{1,0:T(8,128)S(1)}, f32[48,128]{1,0:T(8,128)S(1)}, u32[]{:S(2)}, u32[]{:S(2)}) collective-permute-start(f32[48,128]{1,0:T(8,128)S(1)} %get-tuple-element.27), channel_id=1, source_target_pairs={{0,16},{16,0},{32,48},{48,32},{64,80},{80,64},{96,112},{112,96},{1... | collective-permute-start | bytes 73736 | tf_op jit(solution)/shard_map/ppermute | solution.py:475
  10.6 2.3 %shard_map.87 = (bf16[2048,512]{1,0:T(8,128)(2,1)S(1)}, bf16[2048,512]{1,0:T(8,128)(2,1)S(1)}) custom-call(s32[4,512]{1,0:T(4,128)S(1)} %get-tuple-element.28.donors, f32[4,512]{1,0:T(4,128)S(1)} %get-tuple-element.29.factors), custom_call_target="tpu_custom_call" | custom-call | flops 20971520 | bytes 4194304 | tf_op jit(solution)/shard_map/pallas_call | solution.py:476
  12.9 0.0 collective-permute-done.cols_first
  12.9 1.4 %collective-permute-done.1.cols_second = f32[48,128]{1,0:T(8,128)S(1)} collective-permute-done((f32[48,128]{1,0:T(8,128)S(1)}, f32[48,128]{1,0:T(8,128)S(1)}, u32[]{:S(2)}, u32[]{:S(2)}) %collective-permute-start.1) | collective-permute-done | bytes 24608 | tf_op jit(solution)/shard_map/ppermute | solution.py:475
  14.4 0.2 shard_map.89
  14.5 11.4 %collective-permute-start.2 = (f32[360,128]{1,0:T(8,128)S(1)}, f32[360,128]{1,0:T(8,128)S(1)}, u32[]{:S(2)}, u32[]{:S(2)}) collective-permute-start(f32[360,128]{1,0:T(8,128)S(1)} %get-tuple-element.36), channel_id=1, source_target_pairs={{65,66},{66,65},{67,68},{68,67},{69,70},{70,69},{71,72},{72,71},{7... | collective-permute-start | bytes 552968 | tf_op jit(solution)/shard_map/ppermute | solution.py:496
  25.9 1.9 %collective-permute-start.3 = (f32[360,128]{1,0:T(8,128)S(1)}, f32[360,128]{1,0:T(8,128)S(1)}, u32[]{:S(2)}, u32[]{:S(2)}) collective-permute-start(f32[360,128]{1,0:T(8,128)S(1)} %get-tuple-element.37), channel_id=1, source_target_pairs={{64,65},{65,64},{66,67},{67,66},{68,69},{69,68},{70,71},{71,70},{7... | collective-permute-start | bytes 552968 | tf_op jit(solution)/shard_map/ppermute | solution.py:497
  27.9 4.2 %shard_map.88 = (f32[5,12,32,128]{3,2,1,0:T(8,128)S(1)}, f32[160,512]{1,0:T(8,128)S(1)}, f32[4,4,32,128]{3,2,1,0:T(8,128)S(1)}, f32[5,2,32,128]{3,2,1,0:T(8,128)S(1)}, f32[18,32,128]{2,1,0:T(8,128)S(1)}) custom-call(f32[6,16,32,128]{3,2,1,0:T(8,128)S(1)} %get-tuple-element.24.f, f32[3,32,128]{2,1,0:T(8,128)S(1)} %get-tuple-element.25.cols, ...), custom_call_target="tpu_custom_call" | custom-call | flops 1073741824 | bytes 8388608 | tf_op jit(solution)/shard_map/pallas_call | solution.py:499
  32.0 1.4 %collective-permute-done.2.rows_first = f32[360,128]{1,0:T(8,128)S(1)} collective-permute-done((f32[360,128]{1,0:T(8,128)S(1)}, f32[360,128]{1,0:T(8,128)S(1)}, u32[]{:S(2)}, u32[]{:S(2)}) %collective-permute-start.2) | collective-permute-done | bytes 184352 | tf_op jit(solution)/shard_map/ppermute | solution.py:496
  33.4 0.0 collective-permute-done.3.rows_second
  33.4 1.4 %shard_map.90 = (f32[5,4,32,128]{3,2,1,0:T(8,128)S(1)}, f32[160,512]{1,0:T(8,128)S(1)}) custom-call(f32[6,16,32,128]{3,2,1,0:T(8,128)S(1)} %get-tuple-element.24.f, f32[18,32,128]{2,1,0:T(8,128)S(1)} %get-tuple-element.33.edges, f32[360,128]{1,0:T(8,128)S(1)} %collective-permute-done.2.rows_first, f32[360,128]{1,0:T(8,128)S(1)} %collective-permute-done.3.rows_second, ...), custom_call_target="tpu_custom_call" | custom-call | flops 268435456 | bytes 2097152 | tf_op jit(solution)/shard_map/pallas_call | solution.py:512
  34.8 1.9 %collective-permute-start.4 = (f32[160,512]{1,0:T(8,128)S(1)}, f32[160,512]{1,0:T(8,128)S(1)}, u32[]{:S(2)}, u32[]{:S(2)}) collective-permute-start(f32[160,512]{1,0:T(8,128)S(1)} %get-tuple-element.42), channel_id=1, source_target_pairs={{0,496},{16,480},{32,464},{48,448},{64,432},{80,416},{96,400},{112... | collective-permute-start | bytes 983048 | tf_op jit(solution)/shard_map/ppermute | solution.py:522
  36.7 1.1 %shard_map.91 = (bf16[512,2048]{1,0:T(8,128)(2,1)S(1)}, f32[8,2048]{1,0:T(8,128)S(1)}) custom-call(s32[1,512]{1,0:T(1,128)S(1)} %get-tuple-element.43.receivers), custom_call_target="tpu_custom_call" | custom-call | flops 4194304 | bytes 2097152 | tf_op jit(solution)/shard_map/pallas_call | solution.py:524
  37.8 16.0 %collective-permute-done.4.values = f32[160,512]{1,0:T(8,128)S(1)} collective-permute-done((f32[160,512]{1,0:T(8,128)S(1)}, f32[160,512]{1,0:T(8,128)S(1)}, u32[]{:S(2)}, u32[]{:S(2)}) %collective-permute-start.4) | collective-permute-done | bytes 327712 | tf_op jit(solution)/shard_map/ppermute | solution.py:522
  53.8 2.1 %shard_map.92 = (f32[4,1,32,16,128]{4,3,2,1,0:T(8,128)}, f32[1,32,16,128]{3,2,1,0:T(8,128)}) custom-call(f32[5,12,32,128]{3,2,1,0:T(8,128)S(1)} %get-tuple-element.32.mid, f32[5,4,32,128]{3,2,1,0:T(8,128)S(1)} %get-tuple-element.41.rim, f32[160,512]{1,0:T(8,128)S(1)} %collective-permute-done.4.values, bf16[512,2048]{1,0:T(8,128)(2,1)S(1)} %get-tuple-element.44.table, ...), custom_call_target="tpu_custom_call" | custom-call | flops 1073741824 | bytes 8388608 | tf_op jit(solution)/shard_map/pallas_call | solution.py:532
Async XLA Ops:
  3.2 9.7 %collective-permute-start = (f32[48,128]{1,0:T(8,128)S(1)}, f32[48,128]{1,0:T(8,128)S(1)}, u32[]{:S(2)}, u32[]{:S(2)}) collective-permute-start(f32[48,128]{1,0:T(8,128)S(1)} %get-tuple-element.26), channel_id=1, source_target_pairs={{16,32},{32,16},{48,64},{64,48},{80,96},{96,80},{112,128},{128,112... | collective-permute-start | bytes 73736 | tf_op jit(solution)/shard_map/ppermute | solution.py:474
  8.7 5.7 %collective-permute-start.1 = (f32[48,128]{1,0:T(8,128)S(1)}, f32[48,128]{1,0:T(8,128)S(1)}, u32[]{:S(2)}, u32[]{:S(2)}) collective-permute-start(f32[48,128]{1,0:T(8,128)S(1)} %get-tuple-element.27), channel_id=1, source_target_pairs={{0,16},{16,0},{32,48},{48,32},{64,80},{80,64},{96,112},{112,96},{1... | collective-permute-start | bytes 73736 | tf_op jit(solution)/shard_map/ppermute | solution.py:475
  14.5 18.9 %collective-permute-start.2 = (f32[360,128]{1,0:T(8,128)S(1)}, f32[360,128]{1,0:T(8,128)S(1)}, u32[]{:S(2)}, u32[]{:S(2)}) collective-permute-start(f32[360,128]{1,0:T(8,128)S(1)} %get-tuple-element.36), channel_id=1, source_target_pairs={{65,66},{66,65},{67,68},{68,67},{69,70},{70,69},{71,72},{72,71},{7... | collective-permute-start | bytes 552968 | tf_op jit(solution)/shard_map/ppermute | solution.py:496
  25.9 7.5 %collective-permute-start.3 = (f32[360,128]{1,0:T(8,128)S(1)}, f32[360,128]{1,0:T(8,128)S(1)}, u32[]{:S(2)}, u32[]{:S(2)}) collective-permute-start(f32[360,128]{1,0:T(8,128)S(1)} %get-tuple-element.37), channel_id=1, source_target_pairs={{64,65},{65,64},{66,67},{67,66},{68,69},{69,68},{70,71},{71,70},{7... | collective-permute-start | bytes 552968 | tf_op jit(solution)/shard_map/ppermute | solution.py:497
  34.8 19.0 %collective-permute-start.4 = (f32[160,512]{1,0:T(8,128)S(1)}, f32[160,512]{1,0:T(8,128)S(1)}, u32[]{:S(2)}, u32[]{:S(2)}) collective-permute-start(f32[160,512]{1,0:T(8,128)S(1)} %get-tuple-element.42), channel_id=1, source_target_pairs={{0,496},{16,480},{32,464},{48,448},{64,432},{80,416},{96,400},{112... | collective-permute-start | bytes 983048 | tf_op jit(solution)/shard_map/ppermute | solution.py:522

commit v5 on v4

--- a/solution.py
+++ b/solution.py
@@ -50,22 +50,36 @@
     return jnp.where(pos == 1, roll(c, LON - 1, 1), roll(c, 1, 1))
 
 
+def sums(pairs, faces, eta, warmth):
+    totals, change = [], 0.0
+    for c in range(3):
+        total = 4.0 * (warmth - 0.5) if c == 0 else 0.0
+        for e in range(3):
+            for face, value in zip(faces[e], pairs[c][e]):
+                if value is not None:
+                    total = total + face * value
+        for sign, p, u in zip((-1, 1), pairs[3][c], pairs[c][c]):
+            if p is not None:
+                total = total - p if sign > 0 else total + p
+                change = change - u if sign > 0 else change + u
+        totals.append(total)
+    return totals, (0.5 * BETA) * eta * change
+
+
+def add_lat(totals, change, face, eta, values, upper):
+    totals = [total + face * value for total, value in zip(totals, values)]
+    part = (0.5 * BETA) * eta * values[1]
+    if upper:
+        return [totals[0], totals[1] - values[3], totals[2]], change - part
+    return [totals[0], totals[1] + values[3], totals[2]], change + part
+
+
+def settle(centre, totals, change, scale):
+    return [(1.0 - OMEGA) * centre[c] + totals[c] * scale for c in range(3)] + [centre[3] + change]
+
+
 def relax(centre, pairs, faces, scale, eta, warmth):
-    out = []
-    for c in range(3):
-        total = 0.0
-        for e in range(3):
-            for s in range(2):
-                total = total + faces[e][s] * pairs[c][e][s]
-        total = total - (pairs[3][c][1] - pairs[3][c][0])
-        if c == 0:
-            total = total + 4.0 * (warmth - 0.5)
-        out.append((1.0 - OMEGA) * centre[c] + total * scale)
-    div = 0.0
-    for c in range(3):
-        div = div + (pairs[c][c][1] - pairs[c][c][0])
-    out.append(centre[3] - (0.5 * BETA) * eta * div)
-    return out
+    return settle(centre, *sums(pairs, faces, eta, warmth), scale)
 
 
 def odd(axis):
@@ -241,10 +255,12 @@
 
 def edge_columns(cols, first, second):
     sides = from_sides(first, second)
+    group = iota(1) >> 2
+    here = jnp.logical_and(group >= 1, group <= LAT)
     halo, own = [], []
     for k in range(6):
         q, h = k // 2, k % 2
-        halo.append(roll(sides[q], 4 + 64 * h, 1))
+        halo.append(jnp.where(here, roll(sides[q], 4 + 64 * h, 1), 0.0))
         own.append(roll(cols[q], 4 + 64 * h, 1))
     return halo, own
 
@@ -258,7 +274,7 @@
     return jnp.concatenate(parts, axis=0)
 
 
-def relax_columns(halo, own):
+def column_sums(halo, own):
     middle = (iota(1) & 3) == 1
 
     def pairs_of(k):
@@ -267,9 +283,15 @@
         upper = jnp.where(middle, roll(o, LON - 1, 1), roll(c, LON - 1, 1))
         return depth_pair(c), (roll(c, 4, 1), roll(c, LON - 4, 1)), (lower, upper)
 
-    faces, scale = faces_of(halo[4], pairs_of(4))
+    faces = [[halo[4] + n for n in pair] for pair in pairs_of(4)]
+    diagonal = faces[0][0] + faces[0][1] + faces[1][0] + faces[1][1] + faces[2][0] + faces[2][1]
+    totals, change = sums([pairs_of(k) for k in range(4)], faces, halo[4], halo[5])
+    return totals, change, diagonal
+
+
+def columns_done(halo, totals, change, diagonal):
     inside = halo[4] > 0.0
-    new = relax(halo[:4], [pairs_of(k) for k in range(4)], faces, scale, halo[4], halo[5])
+    new = settle(halo[:4], totals, change, OMEGA / jnp.where(inside, diagonal, 1.0))
     return [jnp.where(inside, v, 0.0) for v in new]
 
 
@@ -303,12 +325,15 @@
     lhs[(5 + k) * DEP : (6 + k) * DEP, at] = (value - top.astype(F32)).astype(BF16)
 
 
-def inner_kernel(f, cols, cols_first, cols_second, whi, wlo, mid_out, values_out, s1_out, faces_out, edges_out, s1, faces, edge, lhs):
+def inner_kernel(f, cols, cols_first, cols_second, whi, wlo, mid_out, values_out, s1_out, edges_out, parts_out, s1, faces, edge, lhs):
     halo, own = edge_columns(cols, cols_first, cols_second)
     for k in range(6):
         edge[k] = swap_middle(halo[k])
-        edges_out[k], edges_out[6 + k], edges_out[12 + k] = halo[k], own[k], edge[k]
-    for k, v in enumerate(relax_columns(halo, own)):
+        edges_out[k], edges_out[6 + k] = halo[k], edge[k]
+    totals, change, diagonal = column_sums(halo, own)
+    for k, v in enumerate((*totals, change, diagonal)):
+        edges_out[12 + k] = v
+    for k, v in enumerate(columns_done(halo, totals, change, diagonal)):
         edge[6 + k] = swap_middle(v)
 
     def first(r, _):
@@ -322,9 +347,9 @@
             s1[k, r] = v
         return 0
 
-    lax.fori_loop(1, LAT - 1, first, 0, unroll=2)
-
-    def second(r, _):
+    lax.fori_loop(1, LAT - 1, first, 0, unroll=7)
+
+    def second(r):
         eta = f[4, r]
         both = ((faces[0, r], faces[1, r]), (eta + f[4, r - 1], eta + f[4, r + 1]), (faces[2, r], faces[3, r]))
         centre = [s1[k, r] for k in range(4)]
@@ -332,35 +357,57 @@
         t = f[5, r]
         new = relax(centre, pairs, both, faces[4, r], eta, t)
         new.append(advance(t, (depth_pair(t), (f[5, r - 1], f[5, r + 1]), lon_pair(t, edge[5], r)), new))
-        at = pl.ds(pl.multiple_of((r - 2) * LON, LON), LON)
+        at = slice((r - 2) * LON, (r - 1) * LON)
         for k in range(5):
             mid_out[k, r - 2] = new[k]
             put_split(lhs, k, at, new[k])
-        return 0
-
-    lax.fori_loop(2, LAT - 2, second, 0, unroll=2)
-    values_out[...] = blend(lhs[...], whi[2 * LON : 14 * LON], wlo[2 * LON : 14 * LON])
-    for k in range(4):
-        for j, r in enumerate((1, 2, 13, 14)):
+
+    total = jnp.zeros((5 * DEP, 512), F32)
+    for start in range(2, LAT - 2, 2):
+        second(start)
+        second(start + 1)
+        at, cells = slice((start - 2) * LON, start * LON), slice(start * LON, (start + 2) * LON)
+        total = total + blend(lhs[:, at], whi[cells], wlo[cells])
+    values_out[...] = total
+    for j, r in enumerate((0, LAT - 1)):
+        eta = f[4, r]
+        lat = lambda k: (None if r == 0 else f[k, r - 1], None if r == LAT - 1 else f[k, r + 1])
+        depth, lon = depth_pair(eta), lon_pair(eta, edge[4], r)
+        inward = eta + f[4, 1 if r == 0 else r - 1]
+        both = ([eta + n for n in depth], (inward, inward), [eta + n for n in lon])
+        pairs = [(depth_pair(f[k, r]), lat(k), lon_pair(f[k, r], edge[k], r)) for k in range(4)]
+        totals, change = sums(pairs, both, eta, f[5, r])
+        diagonal = both[0][0] + both[0][1] + inward + both[2][0] + both[2][1]
+        for i, v in enumerate((*totals, change, diagonal, *both[0], *both[2])):
+            parts_out[j, i] = v
+    for j, r in enumerate((1, LAT - 2)):
+        eta = f[4, r]
+        inward = eta + f[4, 2 if r == 1 else r - 1]
+        lat = lambda k: (None, s1[k, 2]) if r == 1 else (s1[k, r - 1], None)
+        both = ((faces[0, r], faces[1, r]), (inward, inward), (faces[2, r], faces[3, r]))
+        pairs = [(depth_pair(s1[k, r]), lat(k), lon_pair(s1[k, r], edge[6 + k], r)) for k in range(4)]
+        totals, change = sums(pairs, both, eta, f[5, r])
+        for i, v in enumerate((*totals, change, faces[4, r])):
+            parts_out[2 + j, i] = v
+        for k in range(4):
             s1_out[k, j] = s1[k, r]
-    for k in range(5):
-        for j, r in enumerate((1, 14)):
-            faces_out[k, j] = faces[k, r]
-
-
-def rim_kernel(f, edges, rows_first, rows_second, s1_in, faces_in, partial, whi, wlo, rim_out, values_out, lhs):
+
+
+def rim_kernel(f, edges, rows_first, rows_second, s1_in, parts, partial, whi, wlo, rim_out, values_out, lhs):
     is_above = first_above()
     south = lambda at: jnp.where(is_above, rows_second[at], rows_first[at])
     north = lambda at: jnp.where(is_above, rows_first[at], rows_second[at])
     low, high = south(CORNERS), north(CORNERS)
+
     group = iota(1) >> 2
-    halo = []
-    for k in range(6):
-        c = edges[k]
-        if k < 5:
-            c = jnp.where(group == 0, corner_columns(low, k, True, 0), jnp.where(group == LAT + 1, corner_columns(high, k, False, 4 * LAT + 4), c))
-        halo.append(c)
-    edge1 = [swap_middle(v) for v in relax_columns(halo, [edges[6 + k] for k in range(6)])]
+    halo = [edges[k] for k in range(6)]
+    totals, change, diagonal = [edges[12 + c] for c in range(3)], edges[15], edges[16]
+    for upper, packed, row in ((False, low, 0), (True, high, LAT - 1)):
+        lanes = 4 * row + 4
+        corner = [jnp.where(group == row + 1, corner_columns(packed, k, not upper, lanes), 0.0) for k in range(5)]
+        diagonal = diagonal + corner[4]
+        totals, change = add_lat(totals, change, halo[4] + corner[4], halo[4], corner[:4], upper)
+    edge1 = [swap_middle(v) for v in columns_done(halo, totals, change, diagonal)]
     low_edge, high_edge = swap_middle(low), swap_middle(high)
 
     def edge(k, r):
@@ -368,7 +415,7 @@
             return corner_columns(low_edge, k, True, LON - 2)
         if r >= LAT:
             return corner_columns(high_edge, k, False, LON - 2)
-        return roll(edges[12 + k], 122 - 4 * r, 1)
+        return roll(edges[6 + k], 122 - 4 * r, 1)
 
     def field(k, r):
         if r < 0:
@@ -377,30 +424,35 @@
             return north(block(k if r == LAT + 1 else 5 + k))
         return f[k, r]
 
-    s1, faces = {}, {}
-    for j, r in enumerate((1, 2, 13, 14)):
+    s1, new = {}, {}
+    for j, r in enumerate((1, LAT - 2)):
         s1[r] = [s1_in[k, j] for k in range(4)]
-    for j, r in enumerate((1, 14)):
-        below, above, left_face, right_face, scale = (faces_in[k, j] for k in range(5))
+    for j, (out, r, inward) in enumerate(((-1, 0, 1), (LAT, LAT - 1, LAT - 2))):
+        upper = out > r
+        order = (lambda a, b: (b, a)) if upper else (lambda a, b: (a, b))
+        eta = field(4, out)
+        far = 2 * out - r
+        both, scale = faces_of(eta, (depth_pair(eta), order(field(4, far), field(4, r)), beside(eta, edge(4, out))))
+        centre = [field(k, out) for k in range(4)]
+        pairs = [(depth_pair(centre[k]), order(field(k, far), field(k, r)), beside(centre[k], edge(k, out))) for k in range(4)]
+        s1[out] = [jnp.where(eta > 0.0, v, 0.0) for v in relax(centre, pairs, both, scale, eta, field(5, out))]
         eta = f[4, r]
-        faces[r] = (((below, above), (eta + f[4, r - 1], eta + f[4, r + 1]), (left_face, right_face)), scale)
-    for r in (-1, 0, LAT - 1, LAT):
-        eta = field(4, r)
-        faces[r] = faces_of(eta, (depth_pair(eta), (field(4, r - 1), field(4, r + 1)), beside(eta, edge(4, r))))
-        centre = [field(k, r) for k in range(4)]
-        pairs = [(depth_pair(centre[k]), (field(k, r - 1), field(k, r + 1)), beside(centre[k], edge(k, r))) for k in range(4)]
-        s1[r] = relax(centre, pairs, *faces[r], eta, field(5, r))
-        if r < 0 or r >= LAT:
-            s1[r] = [jnp.where(eta > 0.0, v, 0.0) for v in s1[r]]
-    for j, r in enumerate((0, 1, 14, 15)):
-        centre = s1[r]
-        pairs = [(depth_pair(centre[k]), (s1[r - 1][k], s1[r + 1][k]), lon_pair(centre[k], edge1[k], r)) for k in range(4)]
+        outward = eta + field(4, out)
+        scale = OMEGA / (parts[j, 4] + outward)
+        totals, change = add_lat([parts[j, c] for c in range(3)], parts[j, 3], outward, eta, [field(k, out) for k in range(4)], upper)
+        s1[r] = settle([f[k, r] for k in range(4)], totals, change, scale)
+        inner_face = eta + f[4, inward]
+        both = ((parts[j, 5], parts[j, 6]), order(outward, inner_face), (parts[j, 7], parts[j, 8]))
+        pairs = [(depth_pair(s1[r][k]), order(s1[out][k], s1[inward][k]), lon_pair(s1[r][k], edge1[k], r)) for k in range(4)]
+        new[r] = relax(s1[r], pairs, both, scale, eta, f[5, r])
+        totals, change = add_lat([parts[2 + j, c] for c in range(3)], parts[2 + j, 3], inner_face, f[4, inward], s1[r], upper)
+        new[inward] = settle(s1[inward], totals, change, parts[2 + j, 4])
+    for j, r in enumerate((0, 1, LAT - 2, LAT - 1)):
         t = f[5, r]
-        new = relax(centre, pairs, *faces[r], f[4, r], t)
-        new.append(advance(t, (depth_pair(t), (field(5, r - 1), field(5, r + 1)), beside(t, edge(5, r))), new))
+        new[r].append(advance(t, (depth_pair(t), (field(5, r - 1), field(5, r + 1)), beside(t, edge(5, r))), new[r]))
         for k in range(5):
-            rim_out[k, j] = new[k]
-            put_split(lhs, k, slice(j * LON, (j + 1) * LON), new[k])
+            rim_out[k, j] = new[r][k]
+            put_split(lhs, k, slice(j * LON, (j + 1) * LON), new[r][k])
     low, high = slice(0, 2 * LON), slice(14 * LON, 16 * LON)
     values_out[...] = (
         partial[...] + blend(lhs[:, : 2 * LON], whi[low], wlo[low]) + blend(lhs[:, 2 * LON :], whi[high], wlo[high])
@@ -496,9 +548,9 @@
     rows_in_first = lax.ppermute(rows_first, axes, among(middle, 1) + among(outer, 0))
     rows_in_second = lax.ppermute(rows_second, axes, among(middle, 0) + among(outer, 1))
 
-    mid, partial, s1, faces, edges = call(
+    mid, partial, s1, edges, parts = call(
         inner_kernel,
-        [shape(5, 12, *slab), shape(n, 512), shape(4, 4, *slab), shape(5, 2, *slab), shape(18, *slab)],
+        [shape(5, 12, *slab), shape(n, 512), shape(4, 2, *slab), shape(17, *slab), shape(4, 9, *slab)],
         [VMEM] * 6,
         [
             pltpu.VMEM((4, LAT) + slab, F32),
@@ -516,7 +568,7 @@
         [pltpu.VMEM((2 * n, 4 * LON), BF16)],
         size=2 << 20,
         flops=1 << 28,
-    )(f, edges, rows_in_first, rows_in_second, s1, faces, partial, whi, wlo)
+    )(f, edges, rows_in_first, rows_in_second, s1, parts, partial, whi, wlo)
 
     mirror = [(p * lon + b, (1 - p) * lon + lon - 1 - b) for p in range(2) for b in range(lon)]
     incoming = lax.ppermute(values, ("panel", "lon"), mirror)

time: 56.2 us -> 55.7 us (level)
  Pallas kernels: 13.8 us -> 12.4 us
  waiting for transfers between devices: 18.8 us -> 19.7 us
    ppermute x1, waiting for transfers between devices: 1.35 us -> 2.26 us  [shards(): lax.ppermute(rows_first, axes, among(middle, 1) + among(outer, 0))]
    pallas_call x1, Pallas kernels: 4.16 us -> 3.27 us  [shards(): call(inner_kernel, [shape(5, 12, *slab), shape(n, 512), shape(4, 2, *slab...]
  transfers between devices with their start and end apart: 5 -> 5, of which waited for: 3 -> 3; matrix products, arithmetic and copies ran while one was open for 0% -> 0% of each run, Pallas kernels for 13% -> 12%
where the time goes in v5:
time: 55.7 us; the launch traced here: 55.5 us
  starting transfers between devices  22.6 us (41%)
  waiting for transfers between devices  19.7 us (35%)
  Pallas kernels  12.4 us (22%)
  between operations  0.72 us (1%)
    ppermute x1, waiting for transfers between devices, shards(): incoming = lax.ppermute(values, ('panel', 'lon'), mirror)  16 us
    ppermute x1, starting transfers between devices, shards(): lax.ppermute(rows_first, axes, among(middle, 1) + among(outer, 0))  11.4 us
    ppermute x1, starting transfers between devices, shards(): cols_first = lax.ppermute(side_first, 'lon', swap(lon, 1))  5.45 us
    pallas_call x1, Pallas kernels, shards(): call(inner_kernel, [shape(5, 12, *slab), shape(n, 512), shape(4, 2, *slab...  3.27 us
    pallas_call x1, Pallas kernels, shards(): call(stage_kernel, [shape(6, LAT, *slab), shape(3, *slab), sides, sides,...  2.56 us
    pallas_call x1, Pallas kernels, shards(): call(weights_kernel, [shape(LAT * LON, 512, dtype=BF16), shape(LAT * LON,...  2.33 us
    ppermute x1, waiting for transfers between devices, shards(): lax.ppermute(rows_first, axes, among(middle, 1) + among(outer, 0))  2.26 us
    pallas_call x1, Pallas kernels, shards(): call(place_kernel, [shape(4, 1, DEP, LAT, LON), shape(1, DEP, LAT, LON)],...  2.15 us
  transfers between devices with their start and end apart: 5, of which 3 were waited for; matrix products, arithmetic and copies ran while one was open for 0% of the time, Pallas kernels for 12%

profile of v5, /device:TPU:48, one launch (start us, length us, event | category | flops | bytes accessed | tf_op | source)
XLA Modules:
  0.0 55.5 jit_solution(14524387632227422878)
XLA Ops:
  0.6 2.6 %shard_map.86 = (f32[6,16,32,128]{3,2,1,0:T(8,128)S(1)}, f32[3,32,128]{2,1,0:T(8,128)S(1)}, f32[48,128]{1,0:T(8,128)S(1)}, f32[48,128]{1,0:T(8,128)S(1)}, f32[36...) custom-call(f32[4,1,32,16,128]{4,3,2,1,0:T(8,128)} %motion.1, ...), custom_call_target="tpu_custom_call" | custom-call | bytes 2097152 | tf_op jit(solution)/shard_map/pallas_call | solution.py:514
  3.2 5.5 %collective-permute-start = (f32[48,128]{1,0:T(8,128)S(1)}, f32[48,128]{1,0:T(8,128)S(1)}, u32[]{:S(2)}, u32[]{:S(2)}) collective-permute-start(f32[48,128]{1,0:T(8,128)S(1)} %get-tuple-element.26), channel_id=1, source_target_pairs={{16,32},{32,16},{48,64},{64,48},{80,96},{96,80},{112,128},{128,112... | collective-permute-start | bytes 73736 | tf_op jit(solution)/shard_map/ppermute | solution.py:526
  8.7 1.9 %collective-permute-start.1 = (f32[48,128]{1,0:T(8,128)S(1)}, f32[48,128]{1,0:T(8,128)S(1)}, u32[]{:S(2)}, u32[]{:S(2)}) collective-permute-start(f32[48,128]{1,0:T(8,128)S(1)} %get-tuple-element.27), channel_id=1, source_target_pairs={{0,16},{16,0},{32,48},{48,32},{64,80},{80,64},{96,112},{112,96},{1... | collective-permute-start | bytes 73736 | tf_op jit(solution)/shard_map/ppermute | solution.py:527
  10.6 2.3 %shard_map.87 = (bf16[2048,512]{1,0:T(8,128)(2,1)S(1)}, bf16[2048,512]{1,0:T(8,128)(2,1)S(1)}) custom-call(s32[4,512]{1,0:T(4,128)S(1)} %get-tuple-element.28.donors, f32[4,512]{1,0:T(4,128)S(1)} %get-tuple-element.29.factors), custom_call_target="tpu_custom_call" | custom-call | flops 20971520 | bytes 4194304 | tf_op jit(solution)/shard_map/pallas_call | solution.py:528
  12.9 0.0 collective-permute-done.cols_first
  12.9 1.4 %collective-permute-done.1.cols_second = f32[48,128]{1,0:T(8,128)S(1)} collective-permute-done((f32[48,128]{1,0:T(8,128)S(1)}, f32[48,128]{1,0:T(8,128)S(1)}, u32[]{:S(2)}, u32[]{:S(2)}) %collective-permute-start.1) | collective-permute-done | bytes 24608 | tf_op jit(solution)/shard_map/ppermute | solution.py:527
  14.4 0.2 shard_map.89
  14.5 11.4 %collective-permute-start.2 = (f32[360,128]{1,0:T(8,128)S(1)}, f32[360,128]{1,0:T(8,128)S(1)}, u32[]{:S(2)}, u32[]{:S(2)}) collective-permute-start(f32[360,128]{1,0:T(8,128)S(1)} %get-tuple-element.36), channel_id=1, source_target_pairs={{65,66},{66,65},{67,68},{68,67},{69,70},{70,69},{71,72},{72,71},{7... | collective-permute-start | bytes 552968 | tf_op jit(solution)/shard_map/ppermute | solution.py:548
  25.9 1.9 %collective-permute-start.3 = (f32[360,128]{1,0:T(8,128)S(1)}, f32[360,128]{1,0:T(8,128)S(1)}, u32[]{:S(2)}, u32[]{:S(2)}) collective-permute-start(f32[360,128]{1,0:T(8,128)S(1)} %get-tuple-element.37), channel_id=1, source_target_pairs={{64,65},{65,64},{66,67},{67,66},{68,69},{69,68},{70,71},{71,70},{7... | collective-permute-start | bytes 552968 | tf_op jit(solution)/shard_map/ppermute | solution.py:549
  27.9 3.3 %shard_map.88 = (f32[5,12,32,128]{3,2,1,0:T(8,128)S(1)}, f32[160,512]{1,0:T(8,128)S(1)}, f32[4,2,32,128]{3,2,1,0:T(8,128)S(1)}, f32[17,32,128]{2,1,0:T(8,128)S(1)}, f32[4,9,32,128]{3,2,1,0:T(8,128)S(1)}) custom-call(f32[6,16,32,128]{3,2,1,0:T(8,128)S(1)} %get-tuple-element.24.f, f32[3,32,128]{2,1,0:T(8,128)S(1)} %get-tuple-element.25.cols, ...), custom_call_target="tpu_custom_call" | custom-call | flops 1073741824 | bytes 8388608 | tf_op jit(solution)/shard_map/pallas_call | solution.py:551
  31.1 2.3 %collective-permute-done.2.rows_first = f32[360,128]{1,0:T(8,128)S(1)} collective-permute-done((f32[360,128]{1,0:T(8,128)S(1)}, f32[360,128]{1,0:T(8,128)S(1)}, u32[]{:S(2)}, u32[]{:S(2)}) %collective-permute-start.2) | collective-permute-done | bytes 184352 | tf_op jit(solution)/shard_map/ppermute | solution.py:548
  33.4 0.0 collective-permute-done.3.rows_second
  33.4 0.9 %shard_map.90 = (f32[5,4,32,128]{3,2,1,0:T(8,128)S(1)}, f32[160,512]{1,0:T(8,128)S(1)}) custom-call(f32[6,16,32,128]{3,2,1,0:T(8,128)S(1)} %get-tuple-element.24.f, f32[17,32,128]{2,1,0:T(8,128)S(1)} %get-tuple-element.33.edges, f32[360,128]{1,0:T(8,128)S(1)} %collective-permute-done.2.rows_first, f32[360,128]{1,0:T(8,128)S(1)} %collective-permute-done.3.rows_second, ...), custom_call_target="tpu_custom_call" | custom-call | flops 268435456 | bytes 2097152 | tf_op jit(solution)/shard_map/pallas_call | solution.py:564
  34.3 1.9 %collective-permute-start.4 = (f32[160,512]{1,0:T(8,128)S(1)}, f32[160,512]{1,0:T(8,128)S(1)}, u32[]{:S(2)}, u32[]{:S(2)}) collective-permute-start(f32[160,512]{1,0:T(8,128)S(1)} %get-tuple-element.42), channel_id=1, source_target_pairs={{0,496},{16,480},{32,464},{48,448},{64,432},{80,416},{96,400},{112... | collective-permute-start | bytes 983048 | tf_op jit(solution)/shard_map/ppermute | solution.py:574
  36.3 1.1 %shard_map.91 = (bf16[512,2048]{1,0:T(8,128)(2,1)S(1)}, f32[8,2048]{1,0:T(8,128)S(1)}) custom-call(s32[1,512]{1,0:T(1,128)S(1)} %get-tuple-element.43.receivers), custom_call_target="tpu_custom_call" | custom-call | flops 4194304 | bytes 2097152 | tf_op jit(solution)/shard_map/pallas_call | solution.py:576
  37.3 16.0 %collective-permute-done.4.values = f32[160,512]{1,0:T(8,128)S(1)} collective-permute-done((f32[160,512]{1,0:T(8,128)S(1)}, f32[160,512]{1,0:T(8,128)S(1)}, u32[]{:S(2)}, u32[]{:S(2)}) %collective-permute-start.4) | collective-permute-done | bytes 327712 | tf_op jit(solution)/shard_map/ppermute | solution.py:574
  53.3 2.1 %shard_map.92 = (f32[4,1,32,16,128]{4,3,2,1,0:T(8,128)}, f32[1,32,16,128]{3,2,1,0:T(8,128)}) custom-call(f32[5,12,32,128]{3,2,1,0:T(8,128)S(1)} %get-tuple-element.32.mid, f32[5,4,32,128]{3,2,1,0:T(8,128)S(1)} %get-tuple-element.41.rim, f32[160,512]{1,0:T(8,128)S(1)} %collective-permute-done.4.values, bf16[512,2048]{1,0:T(8,128)(2,1)S(1)} %get-tuple-element.44.table, ...), custom_call_target="tpu_custom_call" | custom-call | flops 1073741824 | bytes 8388608 | tf_op jit(solution)/shard_map/pallas_call | solution.py:584
Async XLA Ops:
  3.2 9.7 %collective-permute-start = (f32[48,128]{1,0:T(8,128)S(1)}, f32[48,128]{1,0:T(8,128)S(1)}, u32[]{:S(2)}, u32[]{:S(2)}) collective-permute-start(f32[48,128]{1,0:T(8,128)S(1)} %get-tuple-element.26), channel_id=1, source_target_pairs={{16,32},{32,16},{48,64},{64,48},{80,96},{96,80},{112,128},{128,112... | collective-permute-start | bytes 73736 | tf_op jit(solution)/shard_map/ppermute | solution.py:526
  8.7 5.7 %collective-permute-start.1 = (f32[48,128]{1,0:T(8,128)S(1)}, f32[48,128]{1,0:T(8,128)S(1)}, u32[]{:S(2)}, u32[]{:S(2)}) collective-permute-start(f32[48,128]{1,0:T(8,128)S(1)} %get-tuple-element.27), channel_id=1, source_target_pairs={{0,16},{16,0},{32,48},{48,32},{64,80},{80,64},{96,112},{112,96},{1... | collective-permute-start | bytes 73736 | tf_op jit(solution)/shard_map/ppermute | solution.py:527
  14.5 18.9 %collective-permute-start.2 = (f32[360,128]{1,0:T(8,128)S(1)}, f32[360,128]{1,0:T(8,128)S(1)}, u32[]{:S(2)}, u32[]{:S(2)}) collective-permute-start(f32[360,128]{1,0:T(8,128)S(1)} %get-tuple-element.36), channel_id=1, source_target_pairs={{65,66},{66,65},{67,68},{68,67},{69,70},{70,69},{71,72},{72,71},{7... | collective-permute-start | bytes 552968 | tf_op jit(solution)/shard_map/ppermute | solution.py:548
  25.9 7.5 %collective-permute-start.3 = (f32[360,128]{1,0:T(8,128)S(1)}, f32[360,128]{1,0:T(8,128)S(1)}, u32[]{:S(2)}, u32[]{:S(2)}) collective-permute-start(f32[360,128]{1,0:T(8,128)S(1)} %get-tuple-element.37), channel_id=1, source_target_pairs={{64,65},{65,64},{66,67},{67,66},{68,69},{69,68},{70,71},{71,70},{7... | collective-permute-start | bytes 552968 | tf_op jit(solution)/shard_map/ppermute | solution.py:549
  34.3 19.0 %collective-permute-start.4 = (f32[160,512]{1,0:T(8,128)S(1)}, f32[160,512]{1,0:T(8,128)S(1)}, u32[]{:S(2)}, u32[]{:S(2)}) collective-permute-start(f32[160,512]{1,0:T(8,128)S(1)} %get-tuple-element.42), channel_id=1, source_target_pairs={{0,496},{16,480},{32,464},{48,448},{64,432},{80,416},{96,400},{112... | collective-permute-start | bytes 983048 | tf_op jit(solution)/shard_map/ppermute | solution.py:574

commit v6 on v5

--- a/solution.py
+++ b/solution.py
@@ -97,7 +97,7 @@
 
 def stage_kernel(
     motion, warmth, label, chart, receivers, donors, factors,
-    f, cols_out, side_first_out, side_second_out, first_out, second_out, receivers_out, donors_out, factors_out,
+    f, cols_out, side_first_out, side_second_out, receivers_out, donors_out, factors_out,
     lab, table, sems,
 ):
     small = [
@@ -150,13 +150,6 @@
         rows = slice(0, DEP) if i == 0 else slice(DEP, DEP + DEP // 2)
         side_first_out[rows] = jnp.where(odd("lon"), to_right[i], to_left[i])
         side_second_out[rows] = jnp.where(odd("lon"), to_left[i], to_right[i])
-    is_above = first_above()
-    for out, above in ((first_out, is_above), (second_out, jnp.logical_not(is_above))):
-        outer, inner = jnp.where(above, 14, 1), jnp.where(above, 15, 0)
-        for k in range(5):
-            out[block(k)] = f[k, outer]
-        for k in range(6):
-            out[block(5 + k)] = f[k, inner]
     for c in small[1:]:
         c.wait()
 
@@ -190,7 +183,7 @@
 CORNERS = slice(11 * DEP, 11 * DEP + 8)
 
 
-def corners_kernel(cols_first, cols_second, rows_first, rows_second, _, first_out, second_out, c1, c2, sems):
+def corners_kernel(cols_first, cols_second, rows_first, rows_second, first_out, second_out, c1, c2, sems):
     lane = iota(1, (8, LON))
     left_lanes, group = (lane & 3) < 2, (lane >> 2) & 15
     left, right = by_side(cols_first, cols_second)
@@ -218,7 +211,15 @@
     b.wait()
 
 
-def weights_kernel(donors, factors, hi, lo):
+def weights_kernel(donors, factors, f, hi, lo, first_out, second_out):
+    is_above = first_above()
+    for out, above in ((first_out, is_above), (second_out, jnp.logical_not(is_above))):
+        outer, inner = jnp.where(above, 14, 1), jnp.where(above, 15, 0)
+        for k in range(5):
+            out[block(k)] = f[k, outer]
+        for k in range(6):
+            out[block(5 + k)] = f[k, inner]
+
     def body(i, _):
         cell = iota(0, (32, 512)) + i * 32
         w = jnp.zeros((32, 512), F32)
@@ -511,10 +512,10 @@
     n, slab = 5 * DEP, (DEP, LON)
 
     sides, rows = shape(DEP + DEP // 2, LON), shape(11 * DEP + 8, LON)
-    f, cols, side_first, side_second, rows_first, rows_second, receivers, donors, factors = call(
+    f, cols, side_first, side_second, receivers, donors, factors = call(
         stage_kernel,
         [
-            shape(6, LAT, *slab), shape(3, *slab), sides, sides, rows, rows,
+            shape(6, LAT, *slab), shape(3, *slab), sides, sides,
             shape(1, 512, dtype=jnp.int32), shape(4, 512, dtype=jnp.int32), shape(4, 512),
         ],
         [HBM] * 7,
@@ -525,22 +526,22 @@
     swap = lambda n, start: [(i + j, i + 1 - j) for i in range(start, n - 1, 2) for j in range(2)]
     cols_first = lax.ppermute(side_first, "lon", swap(lon, 1))
     cols_second = lax.ppermute(side_second, "lon", swap(lon, 0))
-    whi, wlo = call(
+    whi, wlo, rows_first, rows_second = call(
         weights_kernel,
-        [shape(LAT * LON, 512, dtype=BF16), shape(LAT * LON, 512, dtype=BF16)],
-        [VMEM, VMEM],
+        [shape(LAT * LON, 512, dtype=BF16), shape(LAT * LON, 512, dtype=BF16), rows, rows],
+        [VMEM, VMEM, VMEM],
         size=4 << 20,
         flops=20 << 20,
-    )(donors, factors)
+    )(donors, factors, f)
     rows_first, rows_second = call(
         corners_kernel,
         [rows, rows],
-        [VMEM, VMEM, ANY, ANY, ANY],
+        [VMEM, VMEM, ANY, ANY],
         [pltpu.VMEM((8, LON), F32), pltpu.VMEM((8, LON), F32), pltpu.SemaphoreType.DMA((2,))],
         out_specs=[ANY, ANY],
         aliases={2: 0, 3: 1},
         size=1 << 16,
-    )(cols_first, cols_second, rows_first, rows_second, whi)
+    )(cols_first, cols_second, rows_first, rows_second)
     middle = middle_of(lon)
     outer = [b for b in range(lon) if b not in middle]
     among = lambda ones, start: [(b * lat + i, b * lat + j) for b in ones for i, j in swap(lat, start)]

time: 55.7 us -> 55.7 us (level)
  no operation moved by 1% of the time
where the time goes in v6:
time: 55.7 us; the launch traced here: 55.4 us
  starting transfers between devices  22.6 us (41%)
  waiting for transfers between devices  19.8 us (36%)
  Pallas kernels  12.3 us (22%)
  between operations  0.72 us (1%)
    ppermute x1, waiting for transfers between devices, shards(): incoming = lax.ppermute(values, ('panel', 'lon'), mirror)  16 us
    ppermute x1, starting transfers between devices, shards(): lax.ppermute(rows_first, axes, among(middle, 1) + among(outer, 0))  11.4 us
    ppermute x1, starting transfers between devices, shards(): cols_first = lax.ppermute(side_first, 'lon', swap(lon, 1))  5.45 us
    pallas_call x1, Pallas kernels, shards(): call(inner_kernel, [shape(5, 12, *slab), shape(n, 512), shape(4, 2, *slab...  3.15 us
    pallas_call x1, Pallas kernels, shards(): call(stage_kernel, [shape(6, LAT, *slab), shape(3, *slab), sides, sides,...  2.55 us
    ppermute x1, waiting for transfers between devices, shards(): lax.ppermute(rows_first, axes, among(middle, 1) + among(outer, 0))  2.38 us
    pallas_call x1, Pallas kernels, shards(): call(weights_kernel, [shape(LAT * LON, 512, dtype=BF16), shape(LAT * LON,...  2.37 us
    pallas_call x1, Pallas kernels, shards(): call(place_kernel, [shape(4, 1, DEP, LAT, LON), shape(1, DEP, LAT, LON)],...  2.14 us
  transfers between devices with their start and end apart: 5, of which 3 were waited for; matrix products, arithmetic and copies ran while one was open for 0% of the time, Pallas kernels for 12%

profile of v6, /device:TPU:48, one launch (start us, length us, event | category | flops | bytes accessed | tf_op | source)
XLA Modules:
  0.0 55.4 jit_solution(15446986272737902972)
XLA Ops:
  0.6 2.6 %shard_map.86 = (f32[6,16,32,128]{3,2,1,0:T(8,128)S(1)}, f32[3,32,128]{2,1,0:T(8,128)S(1)}, f32[48,128]{1,0:T(8,128)S(1)}, f32[48,128]{1,0:T(8,128)S(1)}, s32[1,...) custom-call(f32[4,1,32,16,128]{4,3,2,1,0:T(8,128)} %motion.1, f32[1,32,16,128]{3,2,1,0:T(8,128)} %warmth.1, ...), custom_call_target="tpu_custom_call" | custom-call | bytes 2097152 | tf_op jit(solution)/shard_map/pallas_call | solution.py:515
  3.2 5.5 %collective-permute-start = (f32[48,128]{1,0:T(8,128)S(1)}, f32[48,128]{1,0:T(8,128)S(1)}, u32[]{:S(2)}, u32[]{:S(2)}) collective-permute-start(f32[48,128]{1,0:T(8,128)S(1)} %get-tuple-element.26), channel_id=1, source_target_pairs={{16,32},{32,16},{48,64},{64,48},{80,96},{96,80},{112,128},{128,112... | collective-permute-start | bytes 73736 | tf_op jit(solution)/shard_map/ppermute | solution.py:527
  8.7 1.9 %collective-permute-start.1 = (f32[48,128]{1,0:T(8,128)S(1)}, f32[48,128]{1,0:T(8,128)S(1)}, u32[]{:S(2)}, u32[]{:S(2)}) collective-permute-start(f32[48,128]{1,0:T(8,128)S(1)} %get-tuple-element.27), channel_id=1, source_target_pairs={{0,16},{16,0},{32,48},{48,32},{64,80},{80,64},{96,112},{112,96},{1... | collective-permute-start | bytes 73736 | tf_op jit(solution)/shard_map/ppermute | solution.py:528
  10.6 2.4 %shard_map.87 = (bf16[2048,512]{1,0:T(8,128)(2,1)S(1)}, bf16[2048,512]{1,0:T(8,128)(2,1)S(1)}, f32[360,128]{1,0:T(8,128)S(1)}, f32[360,128]{1,0:T(8,128)S(1)}) custom-call(s32[4,512]{1,0:T(4,128)S(1)} %get-tuple-element.28.donors, f32[4,512]{1,0:T(4,128)S(1)} %get-tuple-element.29.factors, f32[6,16,32,128]{3,2,1,0:T(8,128)S(1)} %get-tuple-element.24.f), custom_call_target="tpu_custom_call" | custom-call | flops 20971520 | bytes 4194304 | tf_op jit(solution)/shard_map/pallas_call | solution.py:529
  13.0 0.0 collective-permute-done.cols_first
  13.0 1.4 %collective-permute-done.1.cols_second = f32[48,128]{1,0:T(8,128)S(1)} collective-permute-done((f32[48,128]{1,0:T(8,128)S(1)}, f32[48,128]{1,0:T(8,128)S(1)}, u32[]{:S(2)}, u32[]{:S(2)}) %collective-permute-start.1) | collective-permute-done | bytes 24608 | tf_op jit(solution)/shard_map/ppermute | solution.py:528
  14.4 0.2 shard_map.89
  14.5 11.4 %collective-permute-start.2 = (f32[360,128]{1,0:T(8,128)S(1)}, f32[360,128]{1,0:T(8,128)S(1)}, u32[]{:S(2)}, u32[]{:S(2)}) collective-permute-start(f32[360,128]{1,0:T(8,128)S(1)} %get-tuple-element.36), channel_id=1, source_target_pairs={{65,66},{66,65},{67,68},{68,67},{69,70},{70,69},{71,72},{72,71},{7... | collective-permute-start | bytes 552968 | tf_op jit(solution)/shard_map/ppermute | solution.py:549
  25.9 1.9 %collective-permute-start.3 = (f32[360,128]{1,0:T(8,128)S(1)}, f32[360,128]{1,0:T(8,128)S(1)}, u32[]{:S(2)}, u32[]{:S(2)}) collective-permute-start(f32[360,128]{1,0:T(8,128)S(1)} %get-tuple-element.37), channel_id=1, source_target_pairs={{64,65},{65,64},{66,67},{67,66},{68,69},{69,68},{70,71},{71,70},{7... | collective-permute-start | bytes 552968 | tf_op jit(solution)/shard_map/ppermute | solution.py:550
  27.9 3.1 %shard_map.88 = (f32[5,12,32,128]{3,2,1,0:T(8,128)S(1)}, f32[160,512]{1,0:T(8,128)S(1)}, f32[4,2,32,128]{3,2,1,0:T(8,128)S(1)}, f32[17,32,128]{2,1,0:T(8,128)S(1)}, f32[4,9,32,128]{3,2,1,0:T(8,128)S(1)}) custom-call(f32[6,16,32,128]{3,2,1,0:T(8,128)S(1)} %get-tuple-element.24.f, f32[3,32,128]{2,1,0:T(8,128)S(1)} %get-tuple-element.25.cols, ...), custom_call_target="tpu_custom_call" | custom-call | flops 1073741824 | bytes 8388608 | tf_op jit(solution)/shard_map/pallas_call | solution.py:552
  31.0 2.4 %collective-permute-done.2.rows_first = f32[360,128]{1,0:T(8,128)S(1)} collective-permute-done((f32[360,128]{1,0:T(8,128)S(1)}, f32[360,128]{1,0:T(8,128)S(1)}, u32[]{:S(2)}, u32[]{:S(2)}) %collective-permute-start.2) | collective-permute-done | bytes 184352 | tf_op jit(solution)/shard_map/ppermute | solution.py:549
  33.4 0.0 collective-permute-done.3.rows_second
  33.4 0.9 %shard_map.90 = (f32[5,4,32,128]{3,2,1,0:T(8,128)S(1)}, f32[160,512]{1,0:T(8,128)S(1)}) custom-call(f32[6,16,32,128]{3,2,1,0:T(8,128)S(1)} %get-tuple-element.24.f, f32[17,32,128]{2,1,0:T(8,128)S(1)} %get-tuple-element.33.edges, f32[360,128]{1,0:T(8,128)S(1)} %collective-permute-done.2.rows_first, f32[360,128]{1,0:T(8,128)S(1)} %collective-permute-done.3.rows_second, ...), custom_call_target="tpu_custom_call" | custom-call | flops 268435456 | bytes 2097152 | tf_op jit(solution)/shard_map/pallas_call | solution.py:565
  34.3 1.9 %collective-permute-start.4 = (f32[160,512]{1,0:T(8,128)S(1)}, f32[160,512]{1,0:T(8,128)S(1)}, u32[]{:S(2)}, u32[]{:S(2)}) collective-permute-start(f32[160,512]{1,0:T(8,128)S(1)} %get-tuple-element.42), channel_id=1, source_target_pairs={{0,496},{16,480},{32,464},{48,448},{64,432},{80,416},{96,400},{112... | collective-permute-start | bytes 983048 | tf_op jit(solution)/shard_map/ppermute | solution.py:575
  36.2 1.1 %shard_map.91 = (bf16[512,2048]{1,0:T(8,128)(2,1)S(1)}, f32[8,2048]{1,0:T(8,128)S(1)}) custom-call(s32[1,512]{1,0:T(1,128)S(1)} %get-tuple-element.43.receivers), custom_call_target="tpu_custom_call" | custom-call | flops 4194304 | bytes 2097152 | tf_op jit(solution)/shard_map/pallas_call | solution.py:577
  37.3 16.0 %collective-permute-done.4.values = f32[160,512]{1,0:T(8,128)S(1)} collective-permute-done((f32[160,512]{1,0:T(8,128)S(1)}, f32[160,512]{1,0:T(8,128)S(1)}, u32[]{:S(2)}, u32[]{:S(2)}) %collective-permute-start.4) | collective-permute-done | bytes 327712 | tf_op jit(solution)/shard_map/ppermute | solution.py:575
  53.3 2.1 %shard_map.92 = (f32[4,1,32,16,128]{4,3,2,1,0:T(8,128)}, f32[1,32,16,128]{3,2,1,0:T(8,128)}) custom-call(f32[5,12,32,128]{3,2,1,0:T(8,128)S(1)} %get-tuple-element.32.mid, f32[5,4,32,128]{3,2,1,0:T(8,128)S(1)} %get-tuple-element.41.rim, f32[160,512]{1,0:T(8,128)S(1)} %collective-permute-done.4.values, bf16[512,2048]{1,0:T(8,128)(2,1)S(1)} %get-tuple-element.44.table, ...), custom_call_target="tpu_custom_call" | custom-call | flops 1073741824 | bytes 8388608 | tf_op jit(solution)/shard_map/pallas_call | solution.py:585
Async XLA Ops:
  3.2 9.8 %collective-permute-start = (f32[48,128]{1,0:T(8,128)S(1)}, f32[48,128]{1,0:T(8,128)S(1)}, u32[]{:S(2)}, u32[]{:S(2)}) collective-permute-start(f32[48,128]{1,0:T(8,128)S(1)} %get-tuple-element.26), channel_id=1, source_target_pairs={{16,32},{32,16},{48,64},{64,48},{80,96},{96,80},{112,128},{128,112... | collective-permute-start | bytes 73736 | tf_op jit(solution)/shard_map/ppermute | solution.py:527
  8.7 5.7 %collective-permute-start.1 = (f32[48,128]{1,0:T(8,128)S(1)}, f32[48,128]{1,0:T(8,128)S(1)}, u32[]{:S(2)}, u32[]{:S(2)}) collective-permute-start(f32[48,128]{1,0:T(8,128)S(1)} %get-tuple-element.27), channel_id=1, source_target_pairs={{0,16},{16,0},{32,48},{48,32},{64,80},{80,64},{96,112},{112,96},{1... | collective-permute-start | bytes 73736 | tf_op jit(solution)/shard_map/ppermute | solution.py:528
  14.5 18.9 %collective-permute-start.2 = (f32[360,128]{1,0:T(8,128)S(1)}, f32[360,128]{1,0:T(8,128)S(1)}, u32[]{:S(2)}, u32[]{:S(2)}) collective-permute-start(f32[360,128]{1,0:T(8,128)S(1)} %get-tuple-element.36), channel_id=1, source_target_pairs={{65,66},{66,65},{67,68},{68,67},{69,70},{70,69},{71,72},{72,71},{7... | collective-permute-start | bytes 552968 | tf_op jit(solution)/shard_map/ppermute | solution.py:549
  25.9 7.5 %collective-permute-start.3 = (f32[360,128]{1,0:T(8,128)S(1)}, f32[360,128]{1,0:T(8,128)S(1)}, u32[]{:S(2)}, u32[]{:S(2)}) collective-permute-start(f32[360,128]{1,0:T(8,128)S(1)} %get-tuple-element.37), channel_id=1, source_target_pairs={{64,65},{65,64},{66,67},{67,66},{68,69},{69,68},{70,71},{71,70},{7... | collective-permute-start | bytes 552968 | tf_op jit(solution)/shard_map/ppermute | solution.py:550
  34.3 19.0 %collective-permute-start.4 = (f32[160,512]{1,0:T(8,128)S(1)}, f32[160,512]{1,0:T(8,128)S(1)}, u32[]{:S(2)}, u32[]{:S(2)}) collective-permute-start(f32[160,512]{1,0:T(8,128)S(1)} %get-tuple-element.42), channel_id=1, source_target_pairs={{0,496},{16,480},{32,464},{48,448},{64,432},{80,416},{96,400},{112... | collective-permute-start | bytes 983048 | tf_op jit(solution)/shard_map/ppermute | solution.py:575

commit v7 on v5

--- a/solution.py
+++ b/solution.py
@@ -115,7 +115,7 @@
         c.start()
     small[0].wait()
 
-    step = 4
+    step = 2
     for start in range(0, LAT, step):
         for c in scalars[2 * start : 2 * (start + step)]:
             c.wait()

time: 55.7 us -> 56 us (level)
  no operation moved by 1% of the time
where the time goes in v7:
time: 56 us; the launch traced here: 55.7 us
  starting transfers between devices  22.6 us (40%)
  waiting for transfers between devices  19.7 us (35%)
  Pallas kernels  12.7 us (23%)
  between operations  0.72 us (1%)
    ppermute x1, waiting for transfers between devices, shards(): incoming = lax.ppermute(values, ('panel', 'lon'), mirror)  16 us
    ppermute x1, starting transfers between devices, shards(): lax.ppermute(rows_first, axes, among(middle, 1) + among(outer, 0))  11.4 us
    ppermute x1, starting transfers between devices, shards(): cols_first = lax.ppermute(side_first, 'lon', swap(lon, 1))  5.45 us
    pallas_call x1, Pallas kernels, shards(): call(inner_kernel, [shape(5, 12, *slab), shape(n, 512), shape(4, 2, *slab...  3.27 us
    pallas_call x1, Pallas kernels, shards(): call(stage_kernel, [shape(6, LAT, *slab), shape(3, *slab), sides, sides,...  2.78 us
    pallas_call x1, Pallas kernels, shards(): call(weights_kernel, [shape(LAT * LON, 512, dtype=BF16), shape(LAT * LON,...  2.33 us
    ppermute x1, waiting for transfers between devices, shards(): lax.ppermute(rows_first, axes, among(middle, 1) + among(outer, 0))  2.26 us
    pallas_call x1, Pallas kernels, shards(): call(place_kernel, [shape(4, 1, DEP, LAT, LON), shape(1, DEP, LAT, LON)],...  2.15 us
  transfers between devices with their start and end apart: 5, of which 3 were waited for; matrix products, arithmetic and copies ran while one was open for 0% of the time, Pallas kernels for 12%

profile of v7, /device:TPU:48, one launch (start us, length us, event | category | flops | bytes accessed | tf_op | source)
XLA Modules:
  0.0 55.7 jit_solution(9834032615241284150)
XLA Ops:
  0.6 2.8 %shard_map.86 = (f32[6,16,32,128]{3,2,1,0:T(8,128)S(1)}, f32[3,32,128]{2,1,0:T(8,128)S(1)}, f32[48,128]{1,0:T(8,128)S(1)}, f32[48,128]{1,0:T(8,128)S(1)}, f32[36...) custom-call(f32[4,1,32,16,128]{4,3,2,1,0:T(8,128)} %motion.1, ...), custom_call_target="tpu_custom_call" | custom-call | bytes 2097152 | tf_op jit(solution)/shard_map/pallas_call | solution.py:514
  3.4 5.5 %collective-permute-start = (f32[48,128]{1,0:T(8,128)S(1)}, f32[48,128]{1,0:T(8,128)S(1)}, u32[]{:S(2)}, u32[]{:S(2)}) collective-permute-start(f32[48,128]{1,0:T(8,128)S(1)} %get-tuple-element.26), channel_id=1, source_target_pairs={{16,32},{32,16},{48,64},{64,48},{80,96},{96,80},{112,128},{128,112... | collective-permute-start | bytes 73736 | tf_op jit(solution)/shard_map/ppermute | solution.py:526
  8.9 1.9 %collective-permute-start.1 = (f32[48,128]{1,0:T(8,128)S(1)}, f32[48,128]{1,0:T(8,128)S(1)}, u32[]{:S(2)}, u32[]{:S(2)}) collective-permute-start(f32[48,128]{1,0:T(8,128)S(1)} %get-tuple-element.27), channel_id=1, source_target_pairs={{0,16},{16,0},{32,48},{48,32},{64,80},{80,64},{96,112},{112,96},{1... | collective-permute-start | bytes 73736 | tf_op jit(solution)/shard_map/ppermute | solution.py:527
  10.8 2.3 %shard_map.87 = (bf16[2048,512]{1,0:T(8,128)(2,1)S(1)}, bf16[2048,512]{1,0:T(8,128)(2,1)S(1)}) custom-call(s32[4,512]{1,0:T(4,128)S(1)} %get-tuple-element.28.donors, f32[4,512]{1,0:T(4,128)S(1)} %get-tuple-element.29.factors), custom_call_target="tpu_custom_call" | custom-call | flops 20971520 | bytes 4194304 | tf_op jit(solution)/shard_map/pallas_call | solution.py:528
  13.1 0.0 collective-permute-done.cols_first
  13.2 1.4 %collective-permute-done.1.cols_second = f32[48,128]{1,0:T(8,128)S(1)} collective-permute-done((f32[48,128]{1,0:T(8,128)S(1)}, f32[48,128]{1,0:T(8,128)S(1)}, u32[]{:S(2)}, u32[]{:S(2)}) %collective-permute-start.1) | collective-permute-done | bytes 24608 | tf_op jit(solution)/shard_map/ppermute | solution.py:527
  14.6 0.2 shard_map.89
  14.8 11.4 %collective-permute-start.2 = (f32[360,128]{1,0:T(8,128)S(1)}, f32[360,128]{1,0:T(8,128)S(1)}, u32[]{:S(2)}, u32[]{:S(2)}) collective-permute-start(f32[360,128]{1,0:T(8,128)S(1)} %get-tuple-element.36), channel_id=1, source_target_pairs={{65,66},{66,65},{67,68},{68,67},{69,70},{70,69},{71,72},{72,71},{7... | collective-permute-start | bytes 552968 | tf_op jit(solution)/shard_map/ppermute | solution.py:548
  26.2 1.9 %collective-permute-start.3 = (f32[360,128]{1,0:T(8,128)S(1)}, f32[360,128]{1,0:T(8,128)S(1)}, u32[]{:S(2)}, u32[]{:S(2)}) collective-permute-start(f32[360,128]{1,0:T(8,128)S(1)} %get-tuple-element.37), channel_id=1, source_target_pairs={{64,65},{65,64},{66,67},{67,66},{68,69},{69,68},{70,71},{71,70},{7... | collective-permute-start | bytes 552968 | tf_op jit(solution)/shard_map/ppermute | solution.py:549
  28.1 3.3 %shard_map.88 = (f32[5,12,32,128]{3,2,1,0:T(8,128)S(1)}, f32[160,512]{1,0:T(8,128)S(1)}, f32[4,2,32,128]{3,2,1,0:T(8,128)S(1)}, f32[17,32,128]{2,1,0:T(8,128)S(1)}, f32[4,9,32,128]{3,2,1,0:T(8,128)S(1)}) custom-call(f32[6,16,32,128]{3,2,1,0:T(8,128)S(1)} %get-tuple-element.24.f, f32[3,32,128]{2,1,0:T(8,128)S(1)} %get-tuple-element.25.cols, ...), custom_call_target="tpu_custom_call" | custom-call | flops 1073741824 | bytes 8388608 | tf_op jit(solution)/shard_map/pallas_call | solution.py:551
  31.4 2.3 %collective-permute-done.2.rows_first = f32[360,128]{1,0:T(8,128)S(1)} collective-permute-done((f32[360,128]{1,0:T(8,128)S(1)}, f32[360,128]{1,0:T(8,128)S(1)}, u32[]{:S(2)}, u32[]{:S(2)}) %collective-permute-start.2) | collective-permute-done | bytes 184352 | tf_op jit(solution)/shard_map/ppermute | solution.py:548
  33.6 0.0 collective-permute-done.3.rows_second
  33.6 0.9 %shard_map.90 = (f32[5,4,32,128]{3,2,1,0:T(8,128)S(1)}, f32[160,512]{1,0:T(8,128)S(1)}) custom-call(f32[6,16,32,128]{3,2,1,0:T(8,128)S(1)} %get-tuple-element.24.f, f32[17,32,128]{2,1,0:T(8,128)S(1)} %get-tuple-element.33.edges, f32[360,128]{1,0:T(8,128)S(1)} %collective-permute-done.2.rows_first, f32[360,128]{1,0:T(8,128)S(1)} %collective-permute-done.3.rows_second, ...), custom_call_target="tpu_custom_call" | custom-call | flops 268435456 | bytes 2097152 | tf_op jit(solution)/shard_map/pallas_call | solution.py:564
  34.6 1.9 %collective-permute-start.4 = (f32[160,512]{1,0:T(8,128)S(1)}, f32[160,512]{1,0:T(8,128)S(1)}, u32[]{:S(2)}, u32[]{:S(2)}) collective-permute-start(f32[160,512]{1,0:T(8,128)S(1)} %get-tuple-element.42), channel_id=1, source_target_pairs={{0,496},{16,480},{32,464},{48,448},{64,432},{80,416},{96,400},{112... | collective-permute-start | bytes 983048 | tf_op jit(solution)/shard_map/ppermute | solution.py:574
  36.5 1.1 %shard_map.91 = (bf16[512,2048]{1,0:T(8,128)(2,1)S(1)}, f32[8,2048]{1,0:T(8,128)S(1)}) custom-call(s32[1,512]{1,0:T(1,128)S(1)} %get-tuple-element.43.receivers), custom_call_target="tpu_custom_call" | custom-call | flops 4194304 | bytes 2097152 | tf_op jit(solution)/shard_map/pallas_call | solution.py:576
  37.6 16.0 %collective-permute-done.4.values = f32[160,512]{1,0:T(8,128)S(1)} collective-permute-done((f32[160,512]{1,0:T(8,128)S(1)}, f32[160,512]{1,0:T(8,128)S(1)}, u32[]{:S(2)}, u32[]{:S(2)}) %collective-permute-start.4) | collective-permute-done | bytes 327712 | tf_op jit(solution)/shard_map/ppermute | solution.py:574
  53.5 2.1 %shard_map.92 = (f32[4,1,32,16,128]{4,3,2,1,0:T(8,128)}, f32[1,32,16,128]{3,2,1,0:T(8,128)}) custom-call(f32[5,12,32,128]{3,2,1,0:T(8,128)S(1)} %get-tuple-element.32.mid, f32[5,4,32,128]{3,2,1,0:T(8,128)S(1)} %get-tuple-element.41.rim, f32[160,512]{1,0:T(8,128)S(1)} %collective-permute-done.4.values, bf16[512,2048]{1,0:T(8,128)(2,1)S(1)} %get-tuple-element.44.table, ...), custom_call_target="tpu_custom_call" | custom-call | flops 1073741824 | bytes 8388608 | tf_op jit(solution)/shard_map/pallas_call | solution.py:584
Async XLA Ops:
  3.4 9.7 %collective-permute-start = (f32[48,128]{1,0:T(8,128)S(1)}, f32[48,128]{1,0:T(8,128)S(1)}, u32[]{:S(2)}, u32[]{:S(2)}) collective-permute-start(f32[48,128]{1,0:T(8,128)S(1)} %get-tuple-element.26), channel_id=1, source_target_pairs={{16,32},{32,16},{48,64},{64,48},{80,96},{96,80},{112,128},{128,112... | collective-permute-start | bytes 73736 | tf_op jit(solution)/shard_map/ppermute | solution.py:526
  8.9 5.7 %collective-permute-start.1 = (f32[48,128]{1,0:T(8,128)S(1)}, f32[48,128]{1,0:T(8,128)S(1)}, u32[]{:S(2)}, u32[]{:S(2)}) collective-permute-start(f32[48,128]{1,0:T(8,128)S(1)} %get-tuple-element.27), channel_id=1, source_target_pairs={{0,16},{16,0},{32,48},{48,32},{64,80},{80,64},{96,112},{112,96},{1... | collective-permute-start | bytes 73736 | tf_op jit(solution)/shard_map/ppermute | solution.py:527
  14.8 18.9 %collective-permute-start.2 = (f32[360,128]{1,0:T(8,128)S(1)}, f32[360,128]{1,0:T(8,128)S(1)}, u32[]{:S(2)}, u32[]{:S(2)}) collective-permute-start(f32[360,128]{1,0:T(8,128)S(1)} %get-tuple-element.36), channel_id=1, source_target_pairs={{65,66},{66,65},{67,68},{68,67},{69,70},{70,69},{71,72},{72,71},{7... | collective-permute-start | bytes 552968 | tf_op jit(solution)/shard_map/ppermute | solution.py:548
  26.2 7.5 %collective-permute-start.3 = (f32[360,128]{1,0:T(8,128)S(1)}, f32[360,128]{1,0:T(8,128)S(1)}, u32[]{:S(2)}, u32[]{:S(2)}) collective-permute-start(f32[360,128]{1,0:T(8,128)S(1)} %get-tuple-element.37), channel_id=1, source_target_pairs={{64,65},{65,64},{66,67},{67,66},{68,69},{69,68},{70,71},{71,70},{7... | collective-permute-start | bytes 552968 | tf_op jit(solution)/shard_map/ppermute | solution.py:549
  34.6 19.0 %collective-permute-start.4 = (f32[160,512]{1,0:T(8,128)S(1)}, f32[160,512]{1,0:T(8,128)S(1)}, u32[]{:S(2)}, u32[]{:S(2)}) collective-permute-start(f32[160,512]{1,0:T(8,128)S(1)} %get-tuple-element.42), channel_id=1, source_target_pairs={{0,496},{16,480},{32,464},{48,448},{64,432},{80,416},{96,400},{112... | collective-permute-start | bytes 983048 | tf_op jit(solution)/shard_map/ppermute | solution.py:574
